TPU v7x, 128 devices: a whole 4x4x4 slice. The times are simulated.
128 devices in a mesh: frames: 32 (over z, y, core), obj: 4 (over x).
Axes of the slice: x: 4, y: 4, z: 4, core: 2. Of those that a mesh axis runs over, the one named last changes fastest.
Arguments:
- object_tiles: float32 [2, 4096, 32, 128], P(None, ('frames', 'obj')), may hold values from -6 to 6
- amplitudes: bfloat16 [2048, 256, 256], P(('frames', 'obj')), may hold values from 0.5 to 3
- probe: float32 [2, 256, 256], replicated, may hold values from -6 to 6
- frame_pos: int32 [2048, 2], P(('frames', 'obj')), may hold values from 0 to 126, as said below
Outputs:
- object_out: float32 [2, 4096, 32, 128], P(None, ('frames', 'obj'))
Inputs may be any that keep to these rules, and one draw needn't show every extreme that they name: `frame_pos`: each row is (r, c) with 0 <= r <= 24 and 0 <= c <= 126, and c + 2 r is a multiple of 16. `frame_pos`: A frame's group is ((c + 2 r) mod 128) // 16. Within each aligned block of 16 frames (the frames of one device) no group holds more than 3 frames, and in every draw one group holds exactly 3 frames in every block.
All inputs are finite; a program needn't handle non-finite values.
Results may differ from a plain program's by a relative error of at most 0.0085.
The roundings to bfloat16 on the way count: a program that leaves them out, or rounds other values in their place, can miss the bound.
Values may be sent and summed in bfloat16 or wider, within the bound.
No kernel may reach another device: no remote copies, remote signals or barrier semaphores. Data moves between devices by JAX's collectives and lax.ppermute only.
A program may use at most 128 MiB of HBM per device.

v0:
```python
import jax
import jax.numpy as jnp
from jax import lax
from jax.sharding import PartitionSpec as P

ITERS = 2


magnitude_floor = 0.3
delta_reg = 1.0
tv_step = 0.1
smooth_eps = 0.1


def shifted(array, axis, by):
    count = lax.axis_size(axis)
    return lax.ppermute(array, axis, [(i, (i + by) % count) for i in range(count)])


def dft_tables(frame_size):
    indices = jnp.arange(frame_size, dtype=jnp.int32)
    phase_step = indices[:, None] * indices[None, :] % frame_size
    angles = phase_step.astype(jnp.float32) * (2.0 * jnp.pi / frame_size)
    norm_scale = 1.0 / jnp.sqrt(jnp.float32(frame_size))
    cosine = jnp.cos(angles) * norm_scale
    minus_sine = -jnp.sin(angles) * norm_scale
    forward = jnp.stack([jnp.stack([cosine, -minus_sine]), jnp.stack([minus_sine, cosine])])
    inverse = jnp.stack([jnp.stack([cosine, minus_sine]), jnp.stack([-minus_sine, cosine])])
    return (forward.astype(jnp.bfloat16), inverse.astype(jnp.bfloat16))


def project_frames(patches, amplitudes, probe, forward, inverse):
    real_part = patches[:, 0].astype(jnp.float32)
    imag_part = patches[:, 1].astype(jnp.float32)
    object_wave = jnp.stack(
        [probe[0] * real_part - probe[1] * imag_part, probe[0] * imag_part + probe[1] * real_part],
        axis=1,
    ).astype(jnp.bfloat16)
    midway = jnp.einsum(
        "pqab,fqbc->fpac", forward, object_wave, preferred_element_type=jnp.float32
    ).astype(jnp.bfloat16)
    far_field = jnp.einsum("fqab,qpbc->fpac", midway, inverse, preferred_element_type=jnp.float32)
    modulus = jnp.sqrt(far_field[:, 0] * far_field[:, 0] + far_field[:, 1] * far_field[:, 1])
    rescale = amplitudes.astype(jnp.float32) / jnp.maximum(modulus, magnitude_floor) - 1.0
    change = (far_field * rescale[:, None]).astype(jnp.bfloat16)
    halfway = jnp.einsum(
        "pqab,fqbc->fpac", inverse, change, preferred_element_type=jnp.float32
    ).astype(jnp.bfloat16)
    returned_wave = jnp.einsum(
        "fqab,qpbc->fpac", halfway, forward, preferred_element_type=jnp.float32
    )
    return jnp.stack(
        [
            probe[0] * returned_wave[:, 0] + probe[1] * returned_wave[:, 1],
            probe[0] * returned_wave[:, 1] - probe[1] * returned_wave[:, 0],
        ],
        axis=1,
    )


def neighbour(edge_piece, offset):
    return shifted(edge_piece, ("frames", "obj"), offset)


def tv_gradient(field, own_index, devices):
    tile_rows = field.shape[1]
    tile_height = field.shape[2]
    tile_width = field.shape[3]
    left_edge = neighbour(field[:, :, :, -1], 1)
    right_edge = neighbour(field[:, :, :, 0], -1)
    above_edge = jnp.roll(neighbour(field[:, :, -1, :], 2), 1, axis=1)
    below_edge = jnp.roll(neighbour(field[:, :, 0, :], -2), -1, axis=1)
    tile_row = jnp.arange(tile_rows, dtype=jnp.int32)
    column = (own_index - 2 * tile_row) % devices
    widened = jnp.concatenate([left_edge[..., None], field, right_edge[..., None]], axis=3)
    across = widened[..., 1:] - widened[..., :-1]
    weight_across = (
        across / jnp.sqrt(across[0] * across[0] + across[1] * across[1] + smooth_eps)[None]
    )
    edge_across = jnp.arange(tile_width + 1, dtype=jnp.int32)[None, :]
    mask_across = jnp.where(
        edge_across == 0,
        (column != 0)[:, None],
        jnp.where(edge_across == tile_width, (column != devices - 1)[:, None], True),
    )
    weight_across = weight_across * mask_across[None, :, None, :].astype(jnp.float32)
    pull_across = weight_across[..., :-1] - weight_across[..., 1:]
    tall = jnp.concatenate([above_edge[:, :, None, :], field, below_edge[:, :, None, :]], axis=2)
    down = tall[:, :, 1:] - tall[:, :, :-1]
    weight_down = down / jnp.sqrt(down[0] * down[0] + down[1] * down[1] + smooth_eps)[None]
    edge_down = jnp.arange(tile_height + 1, dtype=jnp.int32)[None, :]
    mask_down = jnp.where(
        edge_down == 0,
        (tile_row != 0)[:, None],
        jnp.where(edge_down == tile_height, (tile_row != tile_rows - 1)[:, None], True),
    )
    weight_down = weight_down * mask_down[None, :, :, None].astype(jnp.float32)
    pull_down = weight_down[:, :, :-1] - weight_down[:, :, 1:]
    return pull_across + pull_down


def shards(object_tiles, amplitudes, probe, frame_pos):
    devices = lax.axis_size(("frames", "obj"))
    own_index = lax.axis_index(("frames", "obj"))
    frame_count = amplitudes.shape[0]
    tile_rows = object_tiles.shape[1]
    tile_height = object_tiles.shape[2]
    tile_width = object_tiles.shape[3]
    frame_size = probe.shape[1]
    groups = devices // 16
    slot_depth = max(2, 24 * frame_count // devices)
    start_rows = frame_pos[:, 0]
    start_cols = frame_pos[:, 1]
    owner_group = (start_cols + 2 * start_rows) % devices // 16
    frame_order = jnp.arange(frame_count, dtype=jnp.int32)
    before = (owner_group[:, None] == owner_group[None, :]) & (
        frame_order[None, :] < frame_order[:, None]
    )
    slot_rank = jnp.sum(before.astype(jnp.int32), axis=1)
    slot_index = owner_group * slot_depth + slot_rank
    chosen = slot_index[:, None] == jnp.arange(groups * slot_depth, dtype=jnp.int32)[None, :]
    filled = jnp.any(chosen, axis=0).reshape(groups, slot_depth)
    first_row = jnp.sum(jnp.where(chosen, start_rows[:, None], 0), axis=0).reshape(
        groups, slot_depth
    )
    offsets = jnp.arange(16, dtype=jnp.int32) // 2
    wanted = first_row[:, None, :] + offsets[None, :, None]
    wanted = jnp.where(filled[:, None, :], wanted, -1).reshape(devices, slot_depth)
    requested = lax.all_to_all(wanted, ("frames", "obj"), split_axis=0, concat_axis=0, tiled=True)
    flat_requests = requested.reshape(-1)
    members = (flat_requests[None, :] == jnp.arange(tile_rows, dtype=jnp.int32)[:, None]).astype(
        jnp.float32
    )
    counts = jnp.sum(members, axis=1)
    gather_rows = jnp.maximum(flat_requests, 0)
    probe_part = own_index % 16
    probe_block = lax.dynamic_slice(
        probe,
        (jnp.zeros((), jnp.int32), probe_part // 2 * tile_height, probe_part % 2 * tile_width),
        (2, tile_height, tile_width),
    )
    intensity = probe_block[0] * probe_block[0] + probe_block[1] * probe_block[1]
    illumination = counts[:, None, None] * intensity[None]
    forward, inverse = dft_tables(frame_size)
    current = object_tiles
    for sweep in range(ITERS):
        outbound = jnp.take(current.astype(jnp.bfloat16), gather_rows, axis=1).reshape(
            2, devices, slot_depth, tile_height, tile_width
        )
        arrived = lax.all_to_all(
            outbound, ("frames", "obj"), split_axis=1, concat_axis=1, tiled=True
        )
        pieces = arrived.reshape(2, groups, 16, slot_depth, tile_height, tile_width)[
            :, owner_group, :, slot_rank
        ]
        patches = (
            pieces.reshape(frame_count, 2, 8, 2, tile_height, tile_width)
            .transpose(0, 1, 2, 4, 3, 5)
            .reshape(frame_count, 2, frame_size, frame_size)
        )
        update = project_frames(patches, amplitudes, probe, forward, inverse)
        tiles_out = (
            update.reshape(frame_count, 2, 8, tile_height, 2, tile_width)
            .transpose(0, 1, 2, 4, 3, 5)
            .reshape(frame_count, 2, 16, tile_height, tile_width)
        )
        outgoing = (
            jnp.zeros((2, groups, 16, slot_depth, tile_height, tile_width), jnp.float32)
            .at[:, owner_group, :, slot_rank]
            .set(tiles_out)
        )
        outgoing = outgoing.reshape(2, devices, slot_depth, tile_height, tile_width)
        returned = lax.all_to_all(
            outgoing, ("frames", "obj"), split_axis=1, concat_axis=1, tiled=True
        )
        numerator = jnp.einsum(
            "ms,psab->pmab",
            members,
            returned.reshape(2, devices * slot_depth, tile_height, tile_width),
            precision=lax.Precision.HIGHEST,
        )
        relaxed = current + numerator / (illumination[None] + delta_reg)
        current = relaxed - tv_step * tv_gradient(relaxed, own_index, devices)
    return current


def solution(mesh):
    return jax.shard_map(
        shards,
        mesh=mesh,
        in_specs=(
            P(None, ("frames", "obj"), None, None),
            P(("frames", "obj"), None, None),
            P(),
            P(("frames", "obj"), None),
        ),
        out_specs=P(None, ("frames", "obj"), None, None),
        check_vma=False,
    )
```

profile of v0, /device:TPU:0, one launch (start us, length us, event | category | flops | bytes accessed | tf_op | source)
XLA Modules:
  0.0 942.1 jit_solution(3453264968261051532)
XLA Ops:
  3.5 11.1 %all-to-all-start = ((s32[128,1,3]{2,1,0:T(1,128)}), s32[128,1,3]{2,1,0:T(1,128)S(1)}, u32[]{:S(2)}, u32[]{:S(2)}) async-start(s32[128,1,3]{2,1,0:T(1,128)} %copy.271), calls=%async_computation | async-start | bytes 131072 | tf_op jit(solution)/shard_map/all_to_all | solution.py:129
  25.4 13.3 %gather_fusion.2 = bf16[384,2,32,128]{3,2,1,0:T(8,128)(2,1)} fusion(bf16[2,32,32,128]{3,2,1,0:T(8,128)(2,1)S(1)} %convert_element_type.124, s32[1024]{0:T(1024)S(1)} %pad_clamp_fusion), kind=kCustom, calls=%fused_computation.clone | custom fusion | bytes 12584448 | tf_op jit(solution)/shard_map/jit(_take)/gather | solution.py:147
  59.6 70.3 %all-to-all-done.1 = bf16[2,128,3,32,128]{4,3,2,0,1:T(8,128)(2,1)} async-done(((bf16[2,128,3,32,128]{4,3,2,0,1:T(8,128)(2,1)}), bf16[2,128,3,32,128]{4,3,2,0,1:T(8,128)(2,1)}, u32[]{:S(2)}, u32[]{:S(2)}) %all-to-all-start.1) | async-done | bytes 6291488 | tf_op jit(solution)/shard_map/all_to_all | solution.py:150
  177.0 10.3 %fusion.55 = f32[16,2,256,256]{2,3,0,1:T(8,128)} fusion(bf16[16,1,256,256]{2,3,1,0:T(8,128)(2,1)} %get-tuple-element.17, bf16[16,1,256,256]{2,3,1,0:T(8,128)(2,1)} %get-tuple-element.16, bf16[1,2,256,256]{3,2,1,0:T(8,128)(2,1)} %get-tuple-element.37, bf16[1,2,256,256]{3,2,1,0:T(8,128)(2,1)S(1)} %copy-done.9, ...), kind=kOutput, calls=%fused_computation.81 | convolution fusion | flops 4306763776 | bytes 13631488 | tf_op jit(solution)/shard_map/fqab,qpbc->fpac/dot_general | solution.py:42
  194.7 12.7 %fusion.52 = f32[16,2,256,256]{2,3,1,0:T(8,128)} fusion(bf16[1,2,256,256]{3,2,1,0:T(8,128)(2,1)} %get-tuple-element.37, bf16[1,2,256,256]{3,2,1,0:T(8,128)(2,1)S(1)} %copy-done.9, bf16[1,2,256,256]{3,2,1,0:T(8,128)(2,1)} %get-tuple-element.33, bf16[1,2,256,256]{3,2,1,0:T(8,128)(2,1)} %get-tuple-element.36, f32[16,2,256,256]{2,3,0,1:T(8,128)} %fusion.55, ...), kind=kOutput, calls=%fused_computation.80 | convolution fusion | flops 4303355904 | bytes 22020096 | tf_op jit(solution)/shard_map/fqab,qpbc->fpac/dot_general | solution.py:49
  215.5 10.9 %copy.286 = f32[16,1,256,256]{3,1,2,0:T(1,128)} copy(f32[16,1,256,256]{2,3,1,0:T(8,128)} %get-tuple-element.12) | data formatting | bytes 8388608 | tf_op jit(solution)/shard_map/add | solution.py:54
  226.4 10.9 %copy.287 = f32[16,1,256,256]{3,1,2,0:T(1,128)} copy(f32[16,1,256,256]{2,3,1,0:T(8,128)} %get-tuple-element.13) | data formatting | bytes 8388608 | tf_op jit(solution)/shard_map/sub | solution.py:55
  253.9 15.6 %scatter_fusion = f32[2,8,16,3,32,128]{5,4,3,2,1,0:T(8,128)} fusion(f32[2,8,16,3,32,128]{5,4,3,2,1,0:T(8,128)} %broadcast.589.clone, s32[16]{0:T(128)S(1)} %get-tuple-element.8, f32[16,2,16,32,128]{4,3,2,1,0:T(8,128)} %bitcast.285), kind=kCustom, calls=%fused_computation.4 | custom fusion | bytes 25165952 | tf_op jit(solution)/shard_map/scatter | solution.py:170
  269.5 11.4 %copy.289 = f32[2,128,3,32,128]{4,3,2,0,1:T(8,128)} copy(f32[2,128,3,32,128]{4,3,2,1,0:T(8,128)} %bitcast.281) | data formatting | bytes 25165824 | tf_op jit(solution)/shard_map/reshape | solution.py:172
  288.2 153.1 %all-to-all-done.2 = f32[2,128,3,32,128]{4,3,2,0,1:T(8,128)} async-done(((f32[2,128,3,32,128]{4,3,2,0,1:T(8,128)}), f32[2,128,3,32,128]{4,3,2,0,1:T(8,128)}, u32[]{:S(2)}, u32[]{:S(2)}) %all-to-all-start.2) | async-done | bytes 12582944 | tf_op jit(solution)/shard_map/all_to_all | solution.py:173
  441.4 11.1 %copy.290 = f32[2,128,3,32,128]{4,3,2,1,0:T(8,128)} copy(f32[2,128,3,32,128]{4,3,2,0,1:T(8,128)} %all-to-all-done.2) | data formatting | bytes 25165824 | tf_op jit(solution)/shard_map/all_to_all | solution.py:173
  452.5 16.0 %fusion.81 = f32[2,32,32,128]{3,1,2,0:T(8,128)S(1)} fusion(f32[2,384,32,128]{3,2,1,0:T(8,128)} %bitcast.283, f32[2,32,32,128]{3,2,1,0:T(8,128)S(1)} %copy-done.6, f32[32,32,128]{2,0,1:T(8,128)S(1)} %copy-done, s32[384]{0:T(512)S(1)} %reshape.449), kind=kOutput, calls=%fused_computation.91 | convolution fusion | flops 1208496128 | bytes 15205888 | tf_op jit(solution)/shard_map/ms,psab->pmab/dot_general | solution.py:176
  498.2 13.3 %gather_fusion.3 = bf16[384,2,32,128]{3,2,1,0:T(8,128)(2,1)} fusion(bf16[2,32,32,128]{3,2,1,0:T(8,128)(2,1)S(1)} %copy.299, s32[1024]{0:T(1024)S(1)} %pad_clamp_fusion), kind=kCustom, calls=%fused_computation.1.clone | custom fusion | bytes 12584448 | tf_op jit(solution)/shard_map/jit(_take)/gather | solution.py:147
  517.1 83.0 %all_to_all.26 = bf16[2,128,3,32,128]{4,3,2,0,1:T(8,128)(2,1)S(1)} all-to-all(bf16[2,128,3,32,128]{4,3,2,0,1:T(8,128)(2,1)S(1)} %copy.301), channel_id=1, replica_groups=mesh['frames'=32,'obj'=4] {'frames','obj'}, dimensions={1} | all-to-all | bytes 12582912 | tf_op jit(solution)/shard_map/all_to_all | solution.py:150
  609.9 8.7 copy.303
  644.8 10.1 %fusion.49 = f32[16,2,256,256]{2,3,0,1:T(8,128)} fusion(bf16[16,1,256,256]{2,3,1,0:T(8,128)(2,1)} %get-tuple-element.15, bf16[16,1,256,256]{2,3,1,0:T(8,128)(2,1)} %get-tuple-element.14, bf16[1,2,256,256]{3,2,1,0:T(8,128)(2,1)} %get-tuple-element.37, bf16[1,2,256,256]{3,2,1,0:T(8,128)(2,1)S(1)} %copy-done.10, bf16[1,2,256,256]{3,2,1,0:T(8,128)(2,1)S(1)} %copy-done.11, ...), kind=kOutput, calls=%fused_computation.79 | convolution fusion | flops 4306763776 | bytes 13631488 | tf_op jit(solution)/shard_map/fqab,qpbc->fpac/dot_general | solution.py:42
  662.3 12.6 %fusion.46 = f32[16,2,256,256]{2,3,1,0:T(8,128)} fusion(bf16[1,2,256,256]{3,2,1,0:T(8,128)(2,1)} %get-tuple-element.37, bf16[1,2,256,256]{3,2,1,0:T(8,128)(2,1)S(1)} %copy-done.10, bf16[1,2,256,256]{3,2,1,0:T(8,128)(2,1)S(1)} %copy-done.11, bf16[1,2,256,256]{3,2,1,0:T(8,128)(2,1)S(1)} %copy-done.12, f32[16,2,256,256]{2,3,0,1:T(8,128)} %fusion.49, ...), kind=kOutput, calls=%fused_computation.78 | convolution fusion | flops 4303355904 | bytes 22020096 | tf_op jit(solution)/shard_map/fqab,qpbc->fpac/dot_general | solution.py:49
  683.1 10.9 %copy.312 = f32[16,1,256,256]{3,1,2,0:T(1,128)} copy(f32[16,1,256,256]{2,3,1,0:T(8,128)} %get-tuple-element.10) | data formatting | bytes 8388608 | tf_op jit(solution)/shard_map/add | solution.py:54
  694.0 10.9 %copy.313 = f32[16,1,256,256]{3,1,2,0:T(1,128)} copy(f32[16,1,256,256]{2,3,1,0:T(8,128)} %get-tuple-element.11) | data formatting | bytes 8388608 | tf_op jit(solution)/shard_map/sub | solution.py:55
  721.4 15.6 %scatter_fusion.1 = f32[2,8,16,3,32,128]{5,4,3,2,1,0:T(8,128)} fusion(f32[2,8,16,3,32,128]{5,4,3,2,1,0:T(8,128)} %broadcast.589, s32[16]{0:T(128)S(1)} %get-tuple-element.8, f32[16,2,16,32,128]{4,3,2,1,0:T(8,128)} %bitcast.284), kind=kCustom, calls=%fused_computation.5 | custom fusion | bytes 25165952 | tf_op jit(solution)/shard_map/scatter | solution.py:170
  737.0 11.4 %copy.315 = f32[2,128,3,32,128]{4,3,2,0,1:T(8,128)} copy(f32[2,128,3,32,128]{4,3,2,1,0:T(8,128)} %bitcast.280) | data formatting | bytes 25165824 | tf_op jit(solution)/shard_map/reshape | solution.py:172
  748.4 149.0 %all_to_all.27 = f32[2,128,3,32,128]{4,3,2,0,1:T(8,128)} all-to-all(f32[2,128,3,32,128]{4,3,2,0,1:T(8,128)} %copy.315), channel_id=1, replica_groups=mesh['frames'=32,'obj'=4] {'frames','obj'}, dimensions={1} | all-to-all | bytes 25165824 | tf_op jit(solution)/shard_map/all_to_all | solution.py:173
  897.4 11.1 %copy.316 = f32[2,128,3,32,128]{4,3,2,1,0:T(8,128)} copy(f32[2,128,3,32,128]{4,3,2,0,1:T(8,128)} %all_to_all.27) | data formatting | bytes 25165824 | tf_op jit(solution)/shard_map/all_to_all | solution.py:173
  908.5 15.5 %fusion.75 = f32[2,32,32,128]{3,1,2,0:T(8,128)S(1)} fusion(f32[2,32,32,128]{3,1,2,0:T(8,128)S(1)} %copy-done.7, f32[2,384,32,128]{3,2,1,0:T(8,128)} %bitcast.282, f32[32,32,128]{2,0,1:T(8,128)S(1)} %copy-done.1, s32[384]{0:T(512)S(1)} %reshape.449), kind=kOutput, calls=%fused_computation.89 | convolution fusion | flops 1208496128 | bytes 15205888 | tf_op jit(solution)/shard_map/ms,psab->pmab/dot_general | solution.py:176
  (154 shorter events, 242.3 us)
Async XLA Ops:
  3.5 20.4 %all-to-all-start = ((s32[128,1,3]{2,1,0:T(1,128)}), s32[128,1,3]{2,1,0:T(1,128)S(1)}, u32[]{:S(2)}, u32[]{:S(2)}) async-start(s32[128,1,3]{2,1,0:T(1,128)} %copy.271), calls=%async_computation | async-start | bytes 131072 | tf_op jit(solution)/shard_map/all_to_all | solution.py:129
  47.0 6.1 copy-start.8
  47.0 82.8 %all-to-all-start.1 = ((bf16[2,128,3,32,128]{4,3,2,0,1:T(8,128)(2,1)}), bf16[2,128,3,32,128]{4,3,2,0,1:T(8,128)(2,1)}, u32[]{:S(2)}, u32[]{:S(2)}) async-start(bf16[2,128,3,32,128]{4,3,2,0,1:T(8,128)(2,1)} %copy.273), calls=%async_computation.1 | async-start | bytes 12582912 | tf_op jit(solution)/shard_map/all_to_all | solution.py:150
  53.5 154.0 %copy-start.4 = (f32[256,256]{0,1:T(8,128)}, f32[256,256]{0,1:T(8,128)S(1)}, u32[]{:S(2)}) copy-start(f32[256,256]{0,1:T(8,128)S(1)} %copy.277) | copy-start | bytes 786436
  171.4 5.6 copy-start.9
  280.9 160.5 %all-to-all-start.2 = ((f32[2,128,3,32,128]{4,3,2,0,1:T(8,128)}), f32[2,128,3,32,128]{4,3,2,0,1:T(8,128)}, u32[]{:S(2)}, u32[]{:S(2)}) async-start(f32[2,128,3,32,128]{4,3,2,0,1:T(8,128)} %copy.289), calls=%async_computation.2 | async-start | bytes 25165824 | tf_op jit(solution)/shard_map/all_to_all | solution.py:173
  441.4 11.1 %copy-start = (f32[32,32,128]{2,0,1:T(8,128)S(1)}, f32[32,32,128]{2,0,1:T(8,128)}, u32[]{:S(2)}) copy-start(f32[32,32,128]{2,0,1:T(8,128)} %multiply_add_fusion.2) | copy-start | bytes 1572868
  441.4 11.1 %copy-start.6 = (f32[2,32,32,128]{3,2,1,0:T(8,128)S(1)}, f32[2,32,32,128]{3,2,1,0:T(8,128)}, u32[]{:S(2)}) copy-start(f32[2,32,32,128]{3,2,1,0:T(8,128)} %param.6) | copy-start | bytes 3145732
  472.5 14.7 %collective-permute-start = (f32[2,32,32]{2,1,0:T(8,128)}, f32[2,32,32]{2,1,0:T(8,128)}, u32[]{:S(2)}, u32[]{:S(2)}) collective-permute-start(f32[2,32,32]{2,1,0:T(8,128)} %bitcast.51), channel_id=1, source_target_pairs={{0,127},{1,0},{2,1},{3,2},{4,3},{5,4},{6,5},{7,6},{8,7},{9,8},{10,... | collective-permute-start | bytes 24584 | tf_op jit(solution)/shard_map/ppermute | solution.py:17
  478.5 11.2 %collective-permute-start.1 = (f32[2,32,32]{2,1,0:T(8,128)}, f32[2,32,32]{2,1,0:T(8,128)}, u32[]{:S(2)}, u32[]{:S(2)}) collective-permute-start(f32[2,32,32]{2,1,0:T(8,128)} %bitcast.53), channel_id=1, source_target_pairs={{0,1},{1,2},{2,3},{3,4},{4,5},{5,6},{6,7},{7,8},{8,9},{9,10},{10,1... | collective-permute-start | bytes 24584 | tf_op jit(solution)/shard_map/ppermute | solution.py:17
  479.3 16.5 %collective-permute-start.3 = (f32[2,32,128]{2,1,0:T(8,128)}, f32[2,32,128]{2,1,0:T(8,128)S(1)}, u32[]{:S(2)}, u32[]{:S(2)}) collective-permute-start(f32[2,32,128]{2,1,0:T(8,128)} %get-tuple-element.28), channel_id=1, source_target_pairs={{0,2},{1,3},{2,4},{3,5},{4,6},{5,7},{6,8},{7,9},{8,10},{9,11},{10,... | collective-permute-start | bytes 98312 | tf_op jit(solution)/shard_map/ppermute | solution.py:17
  486.8 9.1 collective-permute-start.2
  492.4 2.7 copy-start.2
  492.4 2.7 copy-start.3
  630.9 8.3 copy-start.5
  639.2 5.6 copy-start.10
  639.2 5.6 copy-start.11
  639.2 5.6 copy-start.12
  897.4 11.1 %copy-start.1 = (f32[32,32,128]{2,0,1:T(8,128)S(1)}, f32[32,32,128]{2,0,1:T(8,128)}, u32[]{:S(2)}) copy-start(f32[32,32,128]{2,0,1:T(8,128)} %multiply_add_fusion.2) | copy-start | bytes 1572868
  897.4 11.1 %copy-start.7 = (f32[2,32,32,128]{3,1,2,0:T(8,128)S(1)}, f32[2,32,32,128]{3,1,2,0:T(8,128)}, u32[]{:S(2)}) copy-start(f32[2,32,32,128]{3,1,2,0:T(8,128)} %get-tuple-element.7) | copy-start | bytes 3145732
  925.0 10.4 %collective-permute-start.4 = (f32[2,32,32]{2,1,0:T(8,128)S(1)}, f32[2,32,32]{2,1,0:T(8,128)S(1)}, u32[]{:S(2)}, u32[]{:S(2)}) collective-permute-start(f32[2,32,32]{2,1,0:T(8,128)S(1)} %bitcast.300), channel_id=1, source_target_pairs={{0,127},{1,0},{2,1},{3,2},{4,3},{5,4},{6,5},{7,6},{8,7},{9,8},{10,... | collective-permute-start | bytes 24584 | tf_op jit(solution)/shard_map/ppermute | solution.py:17
  925.7 10.7 %collective-permute-start.5 = (f32[2,32,32]{2,1,0:T(8,128)S(1)}, f32[2,32,32]{2,1,0:T(8,128)S(1)}, u32[]{:S(2)}, u32[]{:S(2)}) collective-permute-start(f32[2,32,32]{2,1,0:T(8,128)S(1)} %bitcast.302), channel_id=1, source_target_pairs={{0,1},{1,2},{2,3},{3,4},{4,5},{5,6},{6,7},{7,8},{8,9},{9,10},{10,1... | collective-permute-start | bytes 24584 | tf_op jit(solution)/shard_map/ppermute | solution.py:17
  927.8 11.3 %collective-permute-start.7 = (f32[2,32,128]{2,1,0:T(8,128)S(1)}, f32[2,32,128]{2,1,0:T(8,128)S(1)}, u32[]{:S(2)}, u32[]{:S(2)}) collective-permute-start(f32[2,32,128]{2,1,0:T(8,128)S(1)} %get-tuple-element.24), channel_id=1, source_target_pairs={{0,2},{1,3},{2,4},{3,5},{4,6},{5,7},{6,8},{7,9},{8,10},{9,11},{10,... | collective-permute-start | bytes 98312 | tf_op jit(solution)/shard_map/ppermute | solution.py:17
  928.3 10.8 %collective-permute-start.6 = (f32[2,32,128]{2,1,0:T(8,128)S(1)}, f32[2,32,128]{2,1,0:T(8,128)S(1)}, u32[]{:S(2)}, u32[]{:S(2)}) collective-permute-start(f32[2,32,128]{2,1,0:T(8,128)S(1)} %get-tuple-element.25), channel_id=1, source_target_pairs={{0,126},{1,127},{2,0},{3,1},{4,2},{5,3},{6,4},{7,5},{8,6},{9,7},{1... | collective-permute-start | bytes 98312 | tf_op jit(solution)/shard_map/ppermute | solution.py:17
where the time goes:
time: 951 us; the launch traced here: 942 us
  local copies, waits for them, and re-layouts  277 us (29%)
  blocking collectives  232 us (24%)
  waiting for transfers between devices  231 us (24%)
  other arithmetic  79.1 us (8%)
  matrix products  77.2 us (8%)
  starting transfers between devices  44.7 us (5%)
    all_to_all x1, waiting for transfers between devices, shards(): lax.all_to_all(outgoing, ('frames', 'obj'), split_axis=1, concat_axis=1,...  153 us
    all_to_all x1, blocking collectives, shards(): lax.all_to_all(outgoing, ('frames', 'obj'), split_axis=1, concat_axis=1,...  149 us
    all_to_all x1, blocking collectives, shards(): lax.all_to_all(outbound, ('frames', 'obj'), split_axis=1, concat_axis=1,...  83 us
    all_to_all x1, waiting for transfers between devices, shards(): lax.all_to_all(outbound, ('frames', 'obj'), split_axis=1, concat_axis=1,...  70.3 us
    dot_general x2, matrix products, shards(): jnp.einsum('ms,psab->pmab', members, returned.reshape(2, devices * slot_d...  31.5 us
    scatter x2, local copies, waits for them, and re-layouts, shards(): outgoing = jnp.zeros((2, groups, 16, slot_depth, tile_height, tile_width)...  31.2 us
    gather x2, local copies, waits for them, and re-layouts, shards(): jnp.take(current.astype(jnp.bfloat16), gather_rows, axis=1)  26.7 us
    dot_general x2, matrix products, project_frames(): jnp.einsum('fqab,qpbc->fpac', halfway, forward, preferred_element_type=jn...  25.4 us
  transfers between devices with their start and end apart: 11, of which 3 were waited for; matrix products, arithmetic and copies ran while one was open for 3% of the time, Pallas kernels for 0%

commit v1 on v0

v1 whole, which is shorter than its diff:
```python
import jax
import jax.numpy as jnp
import numpy as np
from jax import lax
from jax.experimental import pallas as pl
from jax.experimental.pallas import tpu as pltpu
from jax.sharding import PartitionSpec as P

FLOOR = 0.3
DELTA = 1.0
STEP = 0.1
EPS = 0.1
CENTRE = 1.75
F32 = jnp.float32
BF16 = jnp.bfloat16
SIDE = 256
ALL = ("frames", "obj")
GROUPS = [list(range(16 * g, 16 * g + 16)) for g in range(8)]


def params(limit_mb=40):
    return pltpu.CompilerParams(vmem_limit_bytes=limit_mb << 20)


def dft_blocks():
    index = np.arange(SIDE)
    angle = (index[:, None] * index[None, :] % SIDE) * (2.0 * np.pi / SIDE)
    cosine, sine = np.cos(angle) / 16.0, np.sin(angle) / 16.0
    forward = np.block([[cosine, sine], [-sine, cosine]])
    return jnp.asarray(forward, F32).astype(BF16), jnp.asarray(forward.T, F32).astype(BF16)


def iota(shape, axis):
    return lax.broadcasted_iota(jnp.int32, shape, axis)


def dot(a, b):
    return jnp.dot(a, b, preferred_element_type=F32)


def picker(source_of):
    return (iota((256, 256), 1) == source_of(iota((256, 256), 0))).astype(F32).astype(BF16)


def window_rows(dev):
    group, member = dev // 16, dev % 16
    return group, [(2 * member + 8 * group + w) % 32 for w in range(2)]


def pieces_kernel(pos_ref, amp_ref, out_ref):
    swap = picker(lambda o: (o % 16) * 16 + o // 16)
    lane = iota((8, 128), 1)
    code = jnp.zeros((8, 128), jnp.int32)
    for f in range(16):
        row, column = pos_ref[f, 0], pos_ref[f, 1]
        group = ((column + 2 * row) & 127) >> 4
        local = (row - 8 * group) & 31
        owner = (local & 1) * 128 + 16 * group + (local >> 1)
        code = jnp.where((lane & 15) == f, owner, code)
    code = code.astype(F32).astype(BF16)
    for block in range(4):
        rows = amp_ref[:, 16 * block:16 * block + 16, :].reshape(256, 256)
        turned = dot(swap, rows).astype(BF16)
        for part in range(8):
            quad, half = part // 2, part % 2
            out_ref[8 * block + part, 0:64, :] = turned[64 * quad:64 * quad + 64, 128 * half:128 * half + 128]
            out_ref[8 * block + part, 64:72, :] = code


def amplitude_pieces(frame_pos, amplitudes):
    return pl.pallas_call(
        pieces_kernel,
        grid=(4,),
        in_specs=[
            pl.BlockSpec(memory_space=pltpu.SMEM),
            pl.BlockSpec((16, 64, 256), lambda s: (0, s, 0)),
        ],
        out_specs=pl.BlockSpec((32, 72, 128), lambda s: (s, 0, 0)),
        out_shape=jax.ShapeDtypeStruct((128, 72, 128), BF16),
        compiler_params=params(),
        name="amplitude_pieces",
    )(frame_pos, amplitudes)


def sums_kernel(dev_ref, in_ref, out_ref, count_ref, total_ref, number_ref):
    step = pl.program_id(0)

    @pl.when(step == 0)
    def _():
        total_ref[...] = jnp.zeros_like(total_ref)

    lane = iota((8, 128), 1)
    owner = iota((256, 128), 0).astype(F32)
    members, values = [], []
    for t in range(4):
        code = jnp.zeros((8, 128), F32)
        for s in range(8):
            code = jnp.where((lane >> 4) == s, in_ref[8 * t + s, 64:72, :].astype(F32), code)
        members.append((owner == jnp.tile(code, (32, 1))).astype(F32).astype(BF16))
        values.append(
            jnp.concatenate(
                [in_ref[8 * t:8 * t + 8, 16 * c:16 * c + 16, :].reshape(128, 128) for c in range(4)]
                + [jnp.ones((128, 128), BF16)],
                axis=1,
            )
        )
    total_ref[...] += dot(jnp.concatenate(members, axis=1), jnp.concatenate(values, axis=0))

    @pl.when(step == pl.num_programs(0) - 1)
    def _():
        turn = picker(lambda o: (o % 8) * 32 + o // 8)
        for block in range(4):
            parts = []
            for w in range(2):
                rows = slice(128 * w + 32 * block, 128 * w + 32 * block + 32)
                mean = CENTRE * total_ref[rows, 512:640]
                for c in range(4):
                    parts.append(total_ref[rows, 128 * c:128 * c + 128] - mean)
            stacked = jnp.concatenate(parts, axis=0).astype(BF16)
            out_ref[32 * block:32 * block + 32] = dot(turn, stacked).reshape(32, 8, 128).astype(BF16)
        number_ref[...] = total_ref[:, 512:640]
        for w in range(2):
            own = number_ref[pl.ds(dev_ref[0] + 128 * w, 1), :]
            count_ref[8 * w:8 * w + 8, :] = jnp.broadcast_to(own, (8, 128))


def window_sums(dev, arrived):
    return pl.pallas_call(
        sums_kernel,
        grid=(4,),
        in_specs=[
            pl.BlockSpec(memory_space=pltpu.SMEM),
            pl.BlockSpec((32, 72, 128), lambda s: (s, 0, 0)),
        ],
        out_specs=[
            pl.BlockSpec((128, 8, 128), lambda s: (0, 0, 0)),
            pl.BlockSpec((16, 128), lambda s: (0, 0)),
        ],
        out_shape=[
            jax.ShapeDtypeStruct((128, 8, 128), BF16),
            jax.ShapeDtypeStruct((16, 128), F32),
        ],
        scratch_shapes=[pltpu.VMEM((256, 640), F32), pltpu.VMEM((256, 128), F32)],
        compiler_params=params(),
        name="window_sums",
    )(dev, arrived)


def outbound_kernel(dev_ref, in_ref, out_ref):
    dev = dev_ref[0]
    shift = 8 * (dev // 16) + (dev % 16) // 2
    for member in range(16):
        for w in range(2):
            row = (shift + 2 * member + w) % 32
            for part in range(2):
                out_ref[member, w, part] = in_ref[part, row].astype(BF16)


def outbound_tiles(dev, tiles):
    return pl.pallas_call(
        outbound_kernel,
        in_specs=[pl.BlockSpec(memory_space=pltpu.SMEM), pl.BlockSpec(memory_space=pltpu.VMEM)],
        out_specs=pl.BlockSpec(memory_space=pltpu.VMEM),
        out_shape=jax.ShapeDtypeStruct((16, 2, 2, 32, 128), BF16),
        compiler_params=params(),
        name="outbound_tiles",
    )(dev, tiles)


def inbound_kernel(dev_ref, in_ref, out_ref):
    dev = dev_ref[0]
    shift = 8 * (dev // 16) + (dev % 16) // 2
    for member in range(16):
        for w in range(2):
            row = (shift + 2 * member + w) % 32
            for part in range(2):
                out_ref[part, row] = in_ref[member, w, part].astype(F32)


def inbound_tiles(dev, arrived):
    return pl.pallas_call(
        inbound_kernel,
        in_specs=[pl.BlockSpec(memory_space=pltpu.SMEM), pl.BlockSpec(memory_space=pltpu.VMEM)],
        out_specs=pl.BlockSpec(memory_space=pltpu.VMEM),
        out_shape=jax.ShapeDtypeStruct((2, 32, 32, 128), F32),
        compiler_params=params(),
        name="inbound_tiles",
    )(dev, arrived)


def to_far_field(image, probe_ref, forward_ref, inverse_ref):
    waves = []
    for w in range(2):
        real, imag = [image[w][part].astype(BF16).astype(F32) for part in range(2)]
        waves.append(
            [
                (probe_ref[0] * real - probe_ref[1] * imag).astype(BF16),
                (probe_ref[0] * imag + probe_ref[1] * real).astype(BF16),
            ]
        )
    wave = jnp.concatenate(
        [jnp.concatenate([waves[0][part], waves[1][part]], axis=1) for part in range(2)], axis=0
    )
    midway = dot(forward_ref[...], wave).astype(BF16)
    midway = jnp.concatenate(
        [
            jnp.concatenate([midway[:256, 256 * w:256 * w + 256], midway[256:, 256 * w:256 * w + 256]], axis=1)
            for w in range(2)
        ],
        axis=0,
    )
    return dot(midway, inverse_ref[...])


def from_far_field(far, totals, counts, image, probe_ref, forward_ref, inverse_ref):
    changes = []
    for w in range(2):
        real, imag = far[256 * w:256 * w + 256, :256], far[256 * w:256 * w + 256, 256:]
        power = jnp.maximum(real * real + imag * imag, FLOOR * FLOOR)
        scale = totals[w] * lax.rsqrt(power) - counts[w]
        changes.append([(real * scale).astype(BF16), (imag * scale).astype(BF16)])
    change = jnp.concatenate(
        [jnp.concatenate([changes[0][part], changes[1][part]], axis=1) for part in range(2)], axis=0
    )
    halfway = dot(inverse_ref[...], change).astype(BF16)
    halfway = jnp.concatenate(
        [
            jnp.concatenate([halfway[:256, 256 * w:256 * w + 256], halfway[256:, 256 * w:256 * w + 256]], axis=1)
            for w in range(2)
        ],
        axis=0,
    )
    returned = dot(halfway, forward_ref[...])
    intensity = probe_ref[0] * probe_ref[0] + probe_ref[1] * probe_ref[1]
    relaxed = []
    for w in range(2):
        real, imag = returned[256 * w:256 * w + 256, :256], returned[256 * w:256 * w + 256, 256:]
        weight = 1.0 / (counts[w] * intensity + DELTA)
        relaxed.append(
            [
                image[w][0] + (probe_ref[0] * real + probe_ref[1] * imag) * weight,
                image[w][1] + (probe_ref[0] * imag - probe_ref[1] * real) * weight,
            ]
        )
    return relaxed


def own_counts(count_ref):
    return [jnp.tile(count_ref[8 * w:8 * w + 8, :], (32, 2)) for w in range(2)]


def write_relaxed(relaxed, relaxed_ref, edge_refs):
    ahead_ref, behind_ref, up_ref, down_ref = edge_refs
    for w in range(2):
        for part in range(2):
            relaxed_ref[w, part] = relaxed[w][part]
    lane = iota((256, 128), 1)
    sources = []
    for w, side in ((0, 1), (1, 0), (1, 1), (0, 0)):
        for part in range(2):
            sources.append((relaxed[w][part][:, 128 * side:128 * side + 128], 127 * side))
    columns = jnp.zeros((256, 128), F32)
    for place, (block, at) in enumerate(sources):
        turned = pltpu.roll(block, (place - at) % 128, 1) if place != at else block
        columns = jnp.where(lane == place, turned, columns)
    rows = columns.T[:8]
    place = iota((8, 256), 0)
    zero = jnp.zeros((8, 256), F32)
    ahead_ref[...] = jnp.where(place >= 6, pltpu.roll(rows, 6, 0), zero)
    behind_ref[...] = jnp.where(place >= 6, pltpu.roll(rows, 4, 0), zero)
    up = jnp.where(place >= 4, rows, zero)
    down = jnp.where(place >= 4, pltpu.roll(rows, 6, 0), zero)
    for w in range(2):
        for part in range(2):
            at = 2 * w + part
            up = jnp.where(place == at, pltpu.roll(relaxed[w][part][248:], (at - 7) % 8, 0), up)
            first = relaxed[w][part][:8]
            down = jnp.where(place == at, pltpu.roll(first, at, 0) if at else first, down)
    up_ref[...] = jnp.where(place >= 6, zero, up)
    down_ref[...] = jnp.where(place >= 6, zero, down)


def smooth(dev, relaxed_ref, halo_refs):
    up_own, up_in, down_own, down_in = [ref[...] for ref in halo_refs]
    group, starts = window_rows(dev)
    lane8 = iota((8, 256), 1)
    left = jnp.where(lane8 < 32, pltpu.roll(up_in, 32, 1), pltpu.roll(up_own, 32, 1))
    right = jnp.where(lane8 >= 224, pltpu.roll(down_in, 224, 1), pltpu.roll(down_own, 224, 1))
    sides = jnp.concatenate([left, right, jnp.zeros((112, 256), F32)], axis=0).T
    lane = iota((256, 256), 1)
    row = iota((256, 256), 0)
    row8 = iota((8, 256), 0)
    image = []
    for w in range(2):
        start = starts[w]
        x = [relaxed_ref[w, part] for part in range(2)]
        wrapped = (row // 32 + start) >= 32
        column = (16 * group - 2 * start + jnp.where(wrapped, 64, 0)) & 127
        keep_left = (column[:, :128] != 0).astype(F32)
        keep_right = jnp.logical_not((lane == 255) & (column == 126)).astype(F32)
        keep_down = (((32 * start + row) & 1023) != 1023).astype(F32)
        keep_up = (start != 0).astype(F32)

        def halo(at, to):
            shift = (to - at) % 128
            return pltpu.roll(sides, shift, 1) if shift else sides

        across, edge, down, top = [], [], [], []
        for part in range(2):
            beyond = halo(8 + 4 + 2 * (1 - w) + part, 127)
            beyond = jnp.concatenate([beyond, beyond], axis=1)
            across.append(jnp.where(lane == 255, beyond, pltpu.roll(x[part], 255, 1)) - x[part])
            edge.append(x[part][:, :128] - halo(4 + 2 * w + part, 0))
            at = 2 * w + part
            below = jnp.broadcast_to(down_in[at:at + 1], (256, 256))
            down.append(jnp.where(row == 255, below, pltpu.roll(x[part], 255, 0)) - x[part])
            top.append(x[part][:8] - jnp.broadcast_to(up_in[at:at + 1], (8, 256)))
        across_weight = lax.rsqrt(across[0] * across[0] + across[1] * across[1] + EPS) * keep_right
        edge_weight = lax.rsqrt(edge[0] * edge[0] + edge[1] * edge[1] + EPS) * keep_left
        down_weight = lax.rsqrt(down[0] * down[0] + down[1] * down[1] + EPS) * keep_down
        top_weight = lax.rsqrt(top[0] * top[0] + top[1] * top[1] + EPS) * keep_up
        parts = []
        for part in range(2):
            to_right = across[part] * across_weight
            first = edge[part] * edge_weight
            to_left = jnp.where(lane == 0, jnp.concatenate([first, first], axis=1), pltpu.roll(to_right, 1, 1))
            to_below = down[part] * down_weight
            moved = pltpu.roll(to_below, 1, 0)
            to_above = jnp.concatenate(
                [jnp.where(row8 == 0, top[part] * top_weight, moved[:8]), moved[8:]], axis=0
            )
            parts.append(x[part] - STEP * ((to_left - to_right) + (to_above - to_below)))
        image.append(parts)
    return image


def first_far_kernel(in_ref, probe_ref, forward_ref, inverse_ref, far_ref, image_ref):
    image = []
    for w in range(2):
        image.append([])
        for part in range(2):
            whole = jnp.concatenate(
                [
                    jnp.concatenate([in_ref[2 * i, w, part], in_ref[2 * i + 1, w, part]], axis=1)
                    for i in range(8)
                ],
                axis=0,
            )
            image_ref[w, part] = whole
            image[w].append(whole)
    far_ref[...] = to_far_field(image, probe_ref, forward_ref, inverse_ref)


def first_back_kernel(
    far_ref, image_ref, sums_ref, count_ref, probe_ref, forward_ref, inverse_ref, relaxed_ref, total_ref, *edge_refs
):
    counts = own_counts(count_ref)

    def source(o):
        w, half, row = o // 128, (o // 64) % 2, o % 64
        return ((row // 4) * 2 + half) * 8 + w * 4 + row % 4

    place = picker(source)
    blocks = []
    for block in range(4):
        rows = sums_ref[32 * block:32 * block + 32].astype(F32).reshape(256, 128).astype(BF16)
        blocks.append(dot(place, rows))
    totals = []
    for w in range(2):
        total = jnp.concatenate(
            [
                jnp.concatenate([b[128 * w:128 * w + 64], b[128 * w + 64:128 * w + 128]], axis=1)
                for b in blocks
            ],
            axis=0,
        ) + CENTRE * counts[w]
        total_ref[w] = total
        totals.append(total)
    image = [[image_ref[w, part].astype(F32) for part in range(2)] for w in range(2)]
    relaxed = from_far_field(far_ref[...], totals, counts, image, probe_ref, forward_ref, inverse_ref)
    write_relaxed(relaxed, relaxed_ref, edge_refs)


def second_kernel(
    dev_ref, in_ref, up_own, up_in, down_own, down_in, total_ref, count_ref, probe_ref, forward_ref, inverse_ref,
    relaxed_ref, *edge_refs
):
    image = smooth(dev_ref[0], in_ref, (up_own, up_in, down_own, down_in))
    far = to_far_field(image, probe_ref, forward_ref, inverse_ref)
    totals = [total_ref[w] for w in range(2)]
    relaxed = from_far_field(far, totals, own_counts(count_ref), image, probe_ref, forward_ref, inverse_ref)
    write_relaxed(relaxed, relaxed_ref, edge_refs)


def last_kernel(dev_ref, in_ref, up_own, up_in, down_own, down_in, out_ref):
    image = smooth(dev_ref[0], in_ref, (up_own, up_in, down_own, down_in))
    for w in range(2):
        for part in range(2):
            low = image[w][part].astype(BF16)
            for k in range(16):
                i, j = k // 2, k % 2
                out_ref[k, w, part] = low[32 * i:32 * i + 32, 128 * j:128 * j + 128]


SCALAR = pl.BlockSpec(memory_space=pltpu.SMEM)
BLOCK = pl.BlockSpec(memory_space=pltpu.VMEM)
PAIR = jax.ShapeDtypeStruct((2, 2, SIDE, SIDE), F32)
EDGE = jax.ShapeDtypeStruct((8, SIDE), F32)


def exchange_edges(ahead, behind, up, down):
    devices = range(128)
    from_next = lax.ppermute(ahead, ALL, [(s, s // 16 * 16 + (s - 1) % 16) for s in devices])
    from_previous = lax.ppermute(behind, ALL, [(s, s // 16 * 16 + (s + 1) % 16) for s in devices])
    up, down = up + from_next, down + from_previous
    up_in = lax.ppermute(up, ALL, [(s, (s + 16) % 128) for s in devices])
    down_in = lax.ppermute(down, ALL, [(s, (s - 16) % 128) for s in devices])
    return up, up_in, down, down_in


def shards(object_tiles, amplitudes, probe, frame_pos):
    dev = lax.axis_index(ALL).astype(jnp.int32).reshape(1)
    forward, inverse = dft_blocks()

    pieces = lax.all_to_all(amplitude_pieces(frame_pos, amplitudes), ALL, 0, 0, tiled=True)
    tiles = lax.all_to_all(
        outbound_tiles(dev, object_tiles), ALL, 0, 0, axis_index_groups=GROUPS, tiled=True
    )
    sums, counts = window_sums(dev, pieces)
    far, image = pl.pallas_call(
        first_far_kernel,
        in_specs=[BLOCK] * 4,
        out_specs=[BLOCK] * 2,
        out_shape=[jax.ShapeDtypeStruct((512, 512), F32), jax.ShapeDtypeStruct((2, 2, SIDE, SIDE), BF16)],
        compiler_params=params(),
        name="first_far",
    )(tiles, probe, forward, inverse)
    sums = lax.all_to_all(sums, ALL, 0, 0, tiled=True)
    relaxed, totals, *edges = pl.pallas_call(
        first_back_kernel,
        in_specs=[BLOCK] * 7,
        out_specs=[BLOCK] * 6,
        out_shape=[PAIR, jax.ShapeDtypeStruct((2, SIDE, SIDE), F32)] + [EDGE] * 4,
        compiler_params=params(),
        name="first_back",
    )(far, image, sums, counts, probe, forward, inverse)
    relaxed, *edges = pl.pallas_call(
        second_kernel,
        in_specs=[SCALAR] + [BLOCK] * 10,
        out_specs=[BLOCK] * 5,
        out_shape=[PAIR] + [EDGE] * 4,
        compiler_params=params(),
        name="second_sweep",
    )(dev, relaxed, *exchange_edges(*edges), totals, counts, probe, forward, inverse)
    tiles = pl.pallas_call(
        last_kernel,
        in_specs=[SCALAR] + [BLOCK] * 5,
        out_specs=BLOCK,
        out_shape=jax.ShapeDtypeStruct((16, 2, 2, 32, 128), BF16),
        compiler_params=params(),
        name="last_smoothing",
    )(dev, relaxed, *exchange_edges(*edges))
    tiles = lax.all_to_all(tiles, ALL, 0, 0, axis_index_groups=GROUPS, tiled=True)
    return inbound_tiles(dev, tiles)


def solution(mesh):
    return jax.shard_map(
        shards,
        mesh=mesh,
        in_specs=(P(None, ALL, None, None), P(ALL, None, None), P(), P(ALL, None)),
        out_specs=P(None, ALL, None, None),
        check_vma=False,
    )
```

time: 951 us -> 130 us (0.14)
  local copies, waits for them, and re-layouts: 277 us -> 6.31 us
  blocking collectives: 232 us -> 14.5 us
  waiting for transfers between devices: 231 us -> 59.8 us
  other arithmetic: 79.1 us -> 0.01 us
  matrix products: 77.2 us -> 0 us
  Pallas kernels: 0 us -> 13.2 us
  starting transfers between devices: 44.7 us -> 34.8 us
    all_to_all x2 -> x1, blocking collectives: 232 us -> 14.5 us  [shards(): lax.all_to_all(tiles, ALL, 0, 0, axis_index_groups=GROUPS, tiled=True)]
    all_to_all x3, waiting for transfers between devices: 231 us -> 47.8 us  [the longest x1 32 us: shards(): lax.all_to_all(amplitude_pieces(frame_pos, amplitudes), ALL, 0, 0, tiled=...]
    dot_general x6 -> x0, matrix products: 77.2 us -> none  [the longest x2 31.5 us: shards(): jnp.einsum('ms,psab->pmab', members, returned.reshape(2, devices * slot_d...]
    reshape x7 -> x0, local copies, waits for them, and re-layouts: 43.7 us -> none  [the longest x2 22.7 us: shards(): outgoing = outgoing.reshape(2, devices, slot_depth, tile_height, tile_width)]
    gather x4 -> x0, local copies, waits for them, and re-layouts: 38.4 us -> none  [the longest x2 26.7 us: shards(): jnp.take(current.astype(jnp.bfloat16), gather_rows, axis=1)]
    all_to_all x5 -> x0, local copies, waits for them, and re-layouts: 33.1 us -> none  [the longest x2 22.2 us: shards(): lax.all_to_all(outgoing, ('frames', 'obj'), split_axis=1, concat_axis=1,...]
    scatter x2 -> x0, local copies, waits for them, and re-layouts: 31.2 us -> none  [shards(): outgoing = jnp.zeros((2, groups, 16, slot_depth, tile_height, tile_width)...]
    transpose x4 -> x0, local copies, waits for them, and re-layouts: 26.4 us -> none  [the longest x2 17.4 us: shards(): patches = pieces.reshape(frame_count, 2, 8, 2, tile_height, tile_width).t...]
  transfers between devices with their start and end apart: 11 -> 11, of which waited for: 3 -> 9; matrix products, arithmetic and copies ran while one was open for 3% -> 0% of each run, Pallas kernels for 0% -> 3%
where the time goes in v1:
time: 130 us; the launch traced here: 129 us
  waiting for transfers between devices  59.8 us (46%)
  starting transfers between devices  34.8 us (27%)
  blocking collectives  14.5 us (11%)
  Pallas kernels  13.2 us (10%)
  local copies, waits for them, and re-layouts  6.31 us (5%)
    all_to_all x1, waiting for transfers between devices, shards(): lax.all_to_all(amplitude_pieces(frame_pos, amplitudes), ALL, 0, 0, tiled=...  32 us
    all_to_all x1, blocking collectives, shards(): lax.all_to_all(tiles, ALL, 0, 0, axis_index_groups=GROUPS, tiled=True)  14.5 us
    all_to_all x1, starting transfers between devices, shards(): lax.all_to_all(amplitude_pieces(frame_pos, amplitudes), ALL, 0, 0, tiled=...  11.1 us
    all_to_all x1, waiting for transfers between devices, shards(): lax.all_to_all(outbound_tiles(dev, object_tiles), ALL, 0, 0, axis_index_g...  8.06 us
    all_to_all x1, waiting for transfers between devices, shards(): sums = lax.all_to_all(sums, ALL, 0, 0, tiled=True)  7.74 us
    ppermute x2, starting transfers between devices, exchange_edges(): lax.ppermute(ahead, ALL, [(s, s // 16 * 16 + (s - 1) % 16) for s in devic...  7.14 us
    unnamed x19, local copies, waits for them, and re-layouts  6.31 us
    ppermute x2, waiting for transfers between devices, exchange_edges(): up_in = lax.ppermute(up, ALL, [(s, (s + 16) % 128) for s in devices])  6.03 us
  transfers between devices with their start and end apart: 11, of which 9 were waited for; matrix products, arithmetic and copies ran while one was open for 0% of the time, Pallas kernels for 3%

profile of v1, /device:TPU:0, one launch (start us, length us, event | category | flops | bytes accessed | tf_op | source)
XLA Modules:
  0.0 128.9 jit_solution(16750856155176487419)
XLA Ops:
  0.8 1.6 %copy-done.5 = bf16[16,256,256]{2,1,0:T(8,128)(2,1)S(1)} copy-done((bf16[16,256,256]{2,1,0:T(8,128)(2,1)S(1)}, bf16[16,256,256]{2,1,0:T(8,128)(2,1)}, u32[]{:S(2)}) %copy-start.5) | copy-done | bytes 2097176
  2.3 2.1 %amplitude_pieces.1 = bf16[128,72,128]{2,1,0:T(8,128)(2,1)S(1)} custom-call(s32[16,2]{1,0:T(8,128)S(1)} %copy.7.pos_ref, bf16[16,256,256]{2,1,0:T(8,128)(2,1)S(1)} %copy-done.5), custom_call_target="tpu_custom_call" | custom-call | tf_op jit(solution)/shard_map/amplitude_pieces/pallas_call | solution.py:71
  4.5 1.4 %copy-done = bf16[128,72,128]{2,1,0:T(8,128)(2,1)} copy-done((bf16[128,72,128]{2,1,0:T(8,128)(2,1)}, bf16[128,72,128]{2,1,0:T(8,128)(2,1)S(1)}, u32[]{:S(2)}) %copy-start) | copy-done | bytes 2359320
  5.9 11.1 %all-to-all-start.1 = ((bf16[128,72,128]{2,1,0:T(8,128)(2,1)}), bf16[128,72,128]{2,1,0:T(8,128)(2,1)S(1)}, u32[]{:S(2)}, u32[]{:S(2)}) async-start(bf16[128,72,128]{2,1,0:T(8,128)(2,1)} %copy-done), calls=%async_computation.1 | async-start | bytes 4718592 | tf_op jit(solution)/shard_map/all_to_all | solution.py:425
  18.0 32.0 %all-to-all-done.1.in_ref = bf16[128,72,128]{2,1,0:T(8,128)(2,1)S(1)} async-done(((bf16[128,72,128]{2,1,0:T(8,128)(2,1)}), bf16[128,72,128]{2,1,0:T(8,128)(2,1)S(1)}, u32[]{:S(2)}, u32[]{:S(2)}) %all-to-all-start.1) | async-done | bytes 2359328 | tf_op jit(solution)/shard_map/all_to_all | solution.py:425
  50.0 4.2 %all-to-all-start = ((bf16[16,2,2,32,128]{4,3,2,1,0:T(8,128)(2,1)}), bf16[16,2,2,32,128]{4,3,2,1,0:T(8,128)(2,1)}, u32[]{:S(2)}, u32[]{:S(2)}) async-start(bf16[16,2,2,32,128]{4,3,2,1,0:T(8,128)(2,1)} %copy-done.6), calls=%async_computation | async-start | bytes 1048576 | tf_op jit(solution)/shard_map/all_to_all | solution.py:426
  54.3 1.9 %window_sums.1 = (bf16[128,8,128]{2,1,0:T(8,128)(2,1)S(1)}, f32[16,128]{1,0:T(8,128)S(1)}) custom-call(s32[1]{0:T(128)} %bitcast.dev_ref, bf16[128,72,128]{2,1,0:T(8,128)(2,1)S(1)} %all-to-all-done.1.in_ref), custom_call_target="tpu_custom_call" | custom-call | tf_op jit(solution)/shard_map/window_sums/pallas_call | solution.py:128
  56.9 8.1 %all-to-all-done.in_ref = bf16[16,2,2,32,128]{4,3,2,1,0:T(8,128)(2,1)} async-done(((bf16[16,2,2,32,128]{4,3,2,1,0:T(8,128)(2,1)}), bf16[16,2,2,32,128]{4,3,2,1,0:T(8,128)(2,1)}, u32[]{:S(2)}, u32[]{:S(2)}) %all-to-all-start) | async-done | bytes 524320 | tf_op jit(solution)/shard_map/all_to_all | solution.py:426
  65.0 4.6 %all-to-all-start.2 = ((bf16[128,8,128]{2,1,0:T(8,128)(2,1)}), bf16[128,8,128]{2,1,0:T(8,128)(2,1)S(1)}, u32[]{:S(2)}, u32[]{:S(2)}) async-start(bf16[128,8,128]{2,1,0:T(8,128)(2,1)} %copy-done.8), calls=%async_computation.2 | async-start | bytes 524288 | tf_op jit(solution)/shard_map/all_to_all | solution.py:438
  70.6 1.9 %first_far.1 = (f32[512,512]{1,0:T(8,128)S(1)}, bf16[2,2,256,256]{3,2,1,0:T(8,128)(2,1)S(1)}) custom-call(bf16[16,2,2,32,128]{4,3,2,1,0:T(8,128)(2,1)} %all-to-all-done.in_ref, f32[2,256,256]{2,1,0:T(8,128)S(1)} %copy-done.1, bf16[512,512]{1,0:T(8,128)(2,1)S(1)} %copy-done.2, bf16[512,512]{1,0:T(8,128)(2,1)S(1)} %copy-done.3), custom_call_target="tpu_custom_call" | custom-call | tf_op jit(solution)/shard_map/first_far/pallas_call | solution.py:430
  72.5 7.7 %all-to-all-done.2.sums_ref = bf16[128,8,128]{2,1,0:T(8,128)(2,1)S(1)} async-done(((bf16[128,8,128]{2,1,0:T(8,128)(2,1)}), bf16[128,8,128]{2,1,0:T(8,128)(2,1)S(1)}, u32[]{:S(2)}, u32[]{:S(2)}) %all-to-all-start.2) | async-done | bytes 262176 | tf_op jit(solution)/shard_map/all_to_all | solution.py:438
  80.3 1.4 %first_back.1 = (f32[2,2,256,256]{3,2,1,0:T(8,128)S(1)}, f32[2,256,256]{2,1,0:T(8,128)S(1)}, f32[8,256]{1,0:T(8,128)S(1)}, f32[8,256]{1,0:T(8,128)S(1)}, f32[8,256]{1,0:T(8,128)S(1)}, /*index=5*/f32[8,256]{1,0:T(8,128)S(1)}) custom-call(f32[512,512]{1,0:T(8,128)S(1)} %get-tuple-element.20.far_ref, bf16[2,2,256,256]{3,2,1,0:T(8,128)(2,1)S(1)} %get-tuple-element.21.image_ref, ...), custom_call_target="tpu_custom_call" | custom-call | tf_op jit(solution)/shard_map/first_back/pallas_call | solution.py:439
  82.3 3.3 %collective-permute-start = (f32[8,256]{1,0:T(8,128)S(1)}, f32[8,256]{1,0:T(8,128)S(1)}, u32[]{:S(2)}, u32[]{:S(2)}) collective-permute-start(f32[8,256]{1,0:T(8,128)S(1)} %get-tuple-element.26), channel_id=1, source_target_pairs={{0,15},{1,0},{2,1},{3,2},{4,3},{5,4},{6,5},{7,6},{8,7},{9,8},{10,9... | collective-permute-start | bytes 24584 | tf_op jit(solution)/shard_map/ppermute | solution.py:413
  87.0 1.8 %collective-permute-start.3 = (f32[8,256]{1,0:T(8,128)S(1)}, f32[8,256]{1,0:T(8,128)S(1)}, u32[]{:S(2)}, u32[]{:S(2)}) collective-permute-start(f32[8,256]{1,0:T(8,128)S(1)} %add.17.down_own), channel_id=1, source_target_pairs={{0,112},{1,113},{2,114},{3,115},{4,116},{5,117},{6,118},{7,119},{8... | collective-permute-start | bytes 24584 | tf_op jit(solution)/shard_map/ppermute | solution.py:417
  88.7 1.8 %collective-permute-start.1 = (f32[8,256]{1,0:T(8,128)S(1)}, f32[8,256]{1,0:T(8,128)S(1)}, u32[]{:S(2)}, u32[]{:S(2)}) collective-permute-start(f32[8,256]{1,0:T(8,128)S(1)} %add.16.up_own), channel_id=1, source_target_pairs={{0,16},{1,17},{2,18},{3,19},{4,20},{5,21},{6,22},{7,23},{8,24},{9,... | collective-permute-start | bytes 24584 | tf_op jit(solution)/shard_map/ppermute | solution.py:416
  90.5 1.7 %collective-permute-done.3.down_in = f32[8,256]{1,0:T(8,128)S(1)} collective-permute-done((f32[8,256]{1,0:T(8,128)S(1)}, f32[8,256]{1,0:T(8,128)S(1)}, u32[]{:S(2)}, u32[]{:S(2)}) %collective-permute-start.3) | collective-permute-done | bytes 8224 | tf_op jit(solution)/shard_map/ppermute | solution.py:417
  92.2 3.8 %collective-permute-done.1.up_in = f32[8,256]{1,0:T(8,128)S(1)} collective-permute-done((f32[8,256]{1,0:T(8,128)S(1)}, f32[8,256]{1,0:T(8,128)S(1)}, u32[]{:S(2)}, u32[]{:S(2)}) %collective-permute-start.1) | collective-permute-done | bytes 8224 | tf_op jit(solution)/shard_map/ppermute | solution.py:416
  96.0 3.2 %second_sweep.1 = (f32[2,2,256,256]{3,2,1,0:T(8,128)S(1)}, f32[8,256]{1,0:T(8,128)S(1)}, f32[8,256]{1,0:T(8,128)S(1)}, f32[8,256]{1,0:T(8,128)S(1)}, f32[8,256]{1,0:T(8,128)S(1)}) custom-call(s32[1]{0:T(128)} %bitcast.dev_ref, f32[2,2,256,256]{3,2,1,0:T(8,128)S(1)} %get-tuple-element.24.in_ref, f32[8,256]{1,0:T(8,128)S(1)} %add.16.up_own, ...), custom_call_target="tpu_custom_call" | custom-call | tf_op jit(solution)/shard_map/second_sweep/pallas_call | solution.py:447
  99.2 3.8 %collective-permute-start.4 = (f32[8,256]{1,0:T(8,128)S(1)}, f32[8,256]{1,0:T(8,128)S(1)}, u32[]{:S(2)}, u32[]{:S(2)}) collective-permute-start(f32[8,256]{1,0:T(8,128)S(1)} %get-tuple-element.32), channel_id=1, source_target_pairs={{0,15},{1,0},{2,1},{3,2},{4,3},{5,4},{6,5},{7,6},{8,7},{9,8},{10,9... | collective-permute-start | bytes 24584 | tf_op jit(solution)/shard_map/ppermute | solution.py:413
  104.5 3.5 %collective-permute-start.5 = (f32[8,256]{1,0:T(8,128)S(1)}, f32[8,256]{1,0:T(8,128)S(1)}, u32[]{:S(2)}, u32[]{:S(2)}) collective-permute-start(f32[8,256]{1,0:T(8,128)S(1)} %add.18.up_own), channel_id=1, source_target_pairs={{0,16},{1,17},{2,18},{3,19},{4,20},{5,21},{6,22},{7,23},{8,24},{9,... | collective-permute-start | bytes 24584 | tf_op jit(solution)/shard_map/ppermute | solution.py:416
  108.0 1.6 %collective-permute-done.7.down_in = f32[8,256]{1,0:T(8,128)S(1)} collective-permute-done((f32[8,256]{1,0:T(8,128)S(1)}, f32[8,256]{1,0:T(8,128)S(1)}, u32[]{:S(2)}, u32[]{:S(2)}) %collective-permute-start.7) | collective-permute-done | bytes 8224 | tf_op jit(solution)/shard_map/ppermute | solution.py:417
  109.6 2.2 %collective-permute-done.5.up_in = f32[8,256]{1,0:T(8,128)S(1)} collective-permute-done((f32[8,256]{1,0:T(8,128)S(1)}, f32[8,256]{1,0:T(8,128)S(1)}, u32[]{:S(2)}, u32[]{:S(2)}) %collective-permute-start.5) | collective-permute-done | bytes 8224 | tf_op jit(solution)/shard_map/ppermute | solution.py:416
  111.8 1.5 %last_smoothing.1 = bf16[16,2,2,32,128]{4,3,2,1,0:T(8,128)(2,1)S(1)} custom-call(s32[1]{0:T(128)} %bitcast.dev_ref, f32[2,2,256,256]{3,2,1,0:T(8,128)S(1)} %get-tuple-element.30.in_ref, f32[8,256]{1,0:T(8,128)S(1)} %add.18.up_own, f32[8,256]{1,0:T(8,128)S(1)} %collective-permute-done.5.up_in, f32[8,256]{1,0:T(8,128)S(1)} %add.19.down_own, ...), custom_call_target="tpu_custom_call" | custom-call | tf_op jit(solution)/shard_map/last_smoothing/pallas_call | solution.py:455
  113.3 14.5 %all_to_all.20.in_ref = bf16[16,2,2,32,128]{4,3,2,1,0:T(8,128)(2,1)S(1)} all-to-all(bf16[16,2,2,32,128]{4,3,2,1,0:T(8,128)(2,1)S(1)} %last_smoothing.1), channel_id=1, replica_groups={{0,1,2,3,4,5,6,7,8,9,10,11,12,13,14,15},{16,17,18,19,20,21,22,23,24,25,..., dimensions={0} | all-to-all | bytes 1048576 | tf_op jit(solution)/shard_map/all_to_all | solution.py:463
  (30 shorter events, 7.9 us)
Async XLA Ops:
  0.8 1.6 %copy-start.5 = (bf16[16,256,256]{2,1,0:T(8,128)(2,1)S(1)}, bf16[16,256,256]{2,1,0:T(8,128)(2,1)}, u32[]{:S(2)}) copy-start(bf16[16,256,256]{2,1,0:T(8,128)(2,1)} %amp_ref.1) | copy-start | bytes 6291460
  4.4 1.4 %copy-start = (bf16[128,72,128]{2,1,0:T(8,128)(2,1)}, bf16[128,72,128]{2,1,0:T(8,128)(2,1)S(1)}, u32[]{:S(2)}) copy-start(bf16[128,72,128]{2,1,0:T(8,128)(2,1)S(1)} %amplitude_pieces.1) | copy-start | bytes 7077892
  5.9 11.2 %copy-start.7 = (f32[2,32,32,128]{3,2,1,0:T(8,128)S(1)}, f32[2,32,32,128]{3,2,1,0:T(8,128)}, u32[]{:S(2)}) copy-start(f32[2,32,32,128]{3,2,1,0:T(8,128)} %in_ref.1) | copy-start | bytes 3145732
  5.9 44.1 %all-to-all-start.1 = ((bf16[128,72,128]{2,1,0:T(8,128)(2,1)}), bf16[128,72,128]{2,1,0:T(8,128)(2,1)S(1)}, u32[]{:S(2)}, u32[]{:S(2)}) async-start(bf16[128,72,128]{2,1,0:T(8,128)(2,1)} %copy-done), calls=%async_computation.1 | async-start | bytes 4718592 | tf_op jit(solution)/shard_map/all_to_all | solution.py:425
  17.2 0.8 copy-start.6
  18.0 51.6 %copy-start.1 = (f32[2,256,256]{2,1,0:T(8,128)S(1)}, f32[2,256,256]{2,1,0:T(8,128)}, u32[]{:S(2)}) copy-start(f32[2,256,256]{2,1,0:T(8,128)} %probe_ref.5) | copy-start | bytes 1572868
  18.0 51.6 %copy-start.2 = (bf16[512,512]{1,0:T(8,128)(2,1)S(1)}, bf16[512,512]{1,0:T(8,128)(2,1)}, u32[]{:S(2)}) copy-start(bf16[512,512]{1,0:T(8,128)(2,1)} %constant.20.forward_ref) | copy-start | bytes 1572868
  50.0 15.0 %all-to-all-start = ((bf16[16,2,2,32,128]{4,3,2,1,0:T(8,128)(2,1)}), bf16[16,2,2,32,128]{4,3,2,1,0:T(8,128)(2,1)}, u32[]{:S(2)}, u32[]{:S(2)}) async-start(bf16[16,2,2,32,128]{4,3,2,1,0:T(8,128)(2,1)} %copy-done.6), calls=%async_computation | async-start | bytes 1048576 | tf_op jit(solution)/shard_map/all_to_all | solution.py:426
  56.2 0.7 copy-start.8
  56.9 23.3 %copy-start.4 = (bf16[512,512]{1,0:T(8,128)(2,1)S(1)}, bf16[512,512]{1,0:T(8,128)(2,1)}, u32[]{:S(2)}) copy-start(bf16[512,512]{1,0:T(8,128)(2,1)} %constant.21.inverse_ref) | copy-start | bytes 1572868
  65.0 15.3 %all-to-all-start.2 = ((bf16[128,8,128]{2,1,0:T(8,128)(2,1)}), bf16[128,8,128]{2,1,0:T(8,128)(2,1)S(1)}, u32[]{:S(2)}, u32[]{:S(2)}) async-start(bf16[128,8,128]{2,1,0:T(8,128)(2,1)} %copy-done.8), calls=%async_computation.2 | async-start | bytes 524288 | tf_op jit(solution)/shard_map/all_to_all | solution.py:438
  69.6 1.0 copy-start.3
  81.7 5.3 %collective-permute-start.2 = (f32[8,256]{1,0:T(8,128)S(1)}, f32[8,256]{1,0:T(8,128)S(1)}, u32[]{:S(2)}, u32[]{:S(2)}) collective-permute-start(f32[8,256]{1,0:T(8,128)S(1)} %get-tuple-element.28), channel_id=1, source_target_pairs={{0,1},{1,2},{2,3},{3,4},{4,5},{5,6},{6,7},{7,8},{8,9},{9,10},{10,1... | collective-permute-start | bytes 24584 | tf_op jit(solution)/shard_map/ppermute | solution.py:414
  82.3 6.4 %collective-permute-start = (f32[8,256]{1,0:T(8,128)S(1)}, f32[8,256]{1,0:T(8,128)S(1)}, u32[]{:S(2)}, u32[]{:S(2)}) collective-permute-start(f32[8,256]{1,0:T(8,128)S(1)} %get-tuple-element.26), channel_id=1, source_target_pairs={{0,15},{1,0},{2,1},{3,2},{4,3},{5,4},{6,5},{7,6},{8,7},{9,8},{10,9... | collective-permute-start | bytes 24584 | tf_op jit(solution)/shard_map/ppermute | solution.py:413
  87.0 5.2 %collective-permute-start.3 = (f32[8,256]{1,0:T(8,128)S(1)}, f32[8,256]{1,0:T(8,128)S(1)}, u32[]{:S(2)}, u32[]{:S(2)}) collective-permute-start(f32[8,256]{1,0:T(8,128)S(1)} %add.17.down_own), channel_id=1, source_target_pairs={{0,112},{1,113},{2,114},{3,115},{4,116},{5,117},{6,118},{7,119},{8... | collective-permute-start | bytes 24584 | tf_op jit(solution)/shard_map/ppermute | solution.py:417
  88.7 7.3 %collective-permute-start.1 = (f32[8,256]{1,0:T(8,128)S(1)}, f32[8,256]{1,0:T(8,128)S(1)}, u32[]{:S(2)}, u32[]{:S(2)}) collective-permute-start(f32[8,256]{1,0:T(8,128)S(1)} %add.16.up_own), channel_id=1, source_target_pairs={{0,16},{1,17},{2,18},{3,19},{4,20},{5,21},{6,22},{7,23},{8,24},{9,... | collective-permute-start | bytes 24584 | tf_op jit(solution)/shard_map/ppermute | solution.py:416
  99.2 5.3 %collective-permute-start.6 = (f32[8,256]{1,0:T(8,128)S(1)}, f32[8,256]{1,0:T(8,128)S(1)}, u32[]{:S(2)}, u32[]{:S(2)}) collective-permute-start(f32[8,256]{1,0:T(8,128)S(1)} %get-tuple-element.34), channel_id=1, source_target_pairs={{0,1},{1,2},{2,3},{3,4},{4,5},{5,6},{6,7},{7,8},{8,9},{9,10},{10,1... | collective-permute-start | bytes 24584 | tf_op jit(solution)/shard_map/ppermute | solution.py:414
  99.2 5.2 %collective-permute-start.4 = (f32[8,256]{1,0:T(8,128)S(1)}, f32[8,256]{1,0:T(8,128)S(1)}, u32[]{:S(2)}, u32[]{:S(2)}) collective-permute-start(f32[8,256]{1,0:T(8,128)S(1)} %get-tuple-element.32), channel_id=1, source_target_pairs={{0,15},{1,0},{2,1},{3,2},{4,3},{5,4},{6,5},{7,6},{8,7},{9,8},{10,9... | collective-permute-start | bytes 24584 | tf_op jit(solution)/shard_map/ppermute | solution.py:413
  104.4 5.2 %collective-permute-start.7 = (f32[8,256]{1,0:T(8,128)S(1)}, f32[8,256]{1,0:T(8,128)S(1)}, u32[]{:S(2)}, u32[]{:S(2)}) collective-permute-start(f32[8,256]{1,0:T(8,128)S(1)} %add.19.down_own), channel_id=1, source_target_pairs={{0,112},{1,113},{2,114},{3,115},{4,116},{5,117},{6,118},{7,119},{8... | collective-permute-start | bytes 24584 | tf_op jit(solution)/shard_map/ppermute | solution.py:417
  104.5 7.3 %collective-permute-start.5 = (f32[8,256]{1,0:T(8,128)S(1)}, f32[8,256]{1,0:T(8,128)S(1)}, u32[]{:S(2)}, u32[]{:S(2)}) collective-permute-start(f32[8,256]{1,0:T(8,128)S(1)} %add.18.up_own), channel_id=1, source_target_pairs={{0,16},{1,17},{2,18},{3,19},{4,20},{5,21},{6,22},{7,23},{8,24},{9,... | collective-permute-start | bytes 24584 | tf_op jit(solution)/shard_map/ppermute | solution.py:416

commit v2 on v1

v2 whole, which is shorter than its diff:
```python
import jax
import jax.numpy as jnp
import numpy as np
from jax import lax
from jax.experimental import pallas as pl
from jax.experimental.pallas import tpu as pltpu
from jax.sharding import PartitionSpec as P

FLOOR = 0.3
DELTA = 1.0
STEP = 0.1
EPS = 0.1
CENTRE = 1.75
F32 = jnp.float32
BF16 = jnp.bfloat16
SIDE = 256
ALL = ("frames", "obj")
GROUPS = [list(range(16 * g, 16 * g + 16)) for g in range(8)]
SCALAR = pl.BlockSpec(memory_space=pltpu.SMEM)
BLOCK = pl.BlockSpec(memory_space=pltpu.VMEM)
ANYWHERE = pl.BlockSpec(memory_space=pl.ANY)
PAIR = jax.ShapeDtypeStruct((2, 2, SIDE, SIDE), F32)
EDGE = jax.ShapeDtypeStruct((8, SIDE), F32)


def place_of(group, member):
    far = (member // 8) ^ (group & 1)
    along = member % 4
    chip = along + far * (7 - 2 * along)
    return 2 * chip + (((member // 4) & 1) ^ (chip & 1))


def member_of(group, place):
    chip = place // 2
    far = chip // 4
    along = chip + far * (7 - 2 * chip)
    return 8 * (far ^ (group & 1)) + 4 * ((place & 1) ^ (chip & 1)) + along


def partners(move):
    pairs = []
    for dev in range(128):
        group, place = move(dev // 16, place_of(dev // 16, dev % 16))
        group, place = group % 8, place % 16
        pairs.append((dev, 16 * group + member_of(group, place)))
    return pairs


def params(limit_mb=40):
    return pltpu.CompilerParams(vmem_limit_bytes=limit_mb << 20)


def dft_blocks():
    index = np.arange(SIDE)
    angle = (index[:, None] * index[None, :] % SIDE) * (2.0 * np.pi / SIDE)
    cosine, sine = np.cos(angle) / 16.0, np.sin(angle) / 16.0
    forward = np.block([[cosine, sine], [-sine, cosine]])
    return jnp.asarray(forward, F32).astype(BF16), jnp.asarray(forward.T, F32).astype(BF16)


def iota(shape, axis):
    return lax.broadcasted_iota(jnp.int32, shape, axis)


def dot(a, b):
    return jnp.dot(a, b, preferred_element_type=F32)


def picker(source_of):
    return (iota((256, 256), 1) == source_of(iota((256, 256), 0))).astype(F32).astype(BF16)


def window_rows(dev):
    group = dev // 16
    place = place_of(group, dev % 16)
    return group, place, [(2 * place + 8 * group + w) % 32 for w in range(2)]


def pieces_kernel(pos_ref, amp_ref, out_ref, amp, out, in_sem, out_sem):
    fetch = [
        pltpu.make_async_copy(amp_ref.at[:, pl.ds(64 * b, 64), :], amp.at[:, pl.ds(64 * b, 64), :], in_sem.at[b])
        for b in range(4)
    ]
    store = [
        pltpu.make_async_copy(out.at[pl.ds(32 * b, 32)], out_ref.at[pl.ds(32 * b, 32)], out_sem.at[b])
        for b in range(4)
    ]
    for copy in fetch:
        copy.start()
    swap = picker(lambda o: (o % 16) * 16 + o // 16)
    row, column = pos_ref[0:1, :], pos_ref[1:2, :]
    group = ((column + 2 * row) & 127) >> 4
    local = (row - 8 * group) & 31
    owner = ((local & 1) * 128 + 16 * group + member_of(group, local >> 1)).astype(F32)
    code = jnp.where(iota((16, 16), 0) == iota((16, 16), 1), owner, 0.0)
    code = jnp.sum(code, axis=1, keepdims=True)
    mine = (iota((16, 128), 1) & 15) == iota((16, 128), 0)
    code = jnp.sum(jnp.where(mine, code, 0.0), axis=0, keepdims=True)
    code = jnp.broadcast_to(code, (8, 128)).astype(BF16)
    for b in range(4):
        fetch[b].wait()
        for block in range(4 * b, 4 * b + 4):
            rows = amp[:, 16 * block:16 * block + 16, :].reshape(256, 256)
            turned = dot(swap, rows).astype(BF16)
            for part in range(8):
                quad, half = part // 2, part % 2
                out[8 * block + part, 0:64, :] = turned[64 * quad:64 * quad + 64, 128 * half:128 * half + 128]
                out[8 * block + part, 64:72, :] = code
        store[b].start()
    for copy in store:
        copy.wait()


def amplitude_pieces(frame_pos, amplitudes):
    return pl.pallas_call(
        pieces_kernel,
        in_specs=[BLOCK, ANYWHERE],
        out_specs=ANYWHERE,
        out_shape=jax.ShapeDtypeStruct((128, 72, 128), BF16),
        scratch_shapes=[
            pltpu.VMEM((16, 256, 256), BF16),
            pltpu.VMEM((128, 72, 128), BF16),
            pltpu.SemaphoreType.DMA((4,)),
            pltpu.SemaphoreType.DMA((4,)),
        ],
        compiler_params=params(60),
        name="amplitude_pieces",
    )(frame_pos.T, amplitudes)


def sums_kernel(dev_ref, in_ref, out_ref, count_ref, pieces, total_ref, number_ref, sem):
    fetch = [
        pltpu.make_async_copy(in_ref.at[pl.ds(32 * b, 32)], pieces.at[pl.ds(32 * b, 32)], sem.at[b])
        for b in range(4)
    ]
    for copy in fetch:
        copy.start()
    lane = iota((8, 128), 1)
    owner = iota((256, 128), 0).astype(F32)
    turn = picker(lambda o: (o % 8) * 32 + o // 8)
    for b in range(4):
        fetch[b].wait()
        members, values = [], []
        for t in range(4 * b, 4 * b + 4):
            code = jnp.zeros((8, 128), F32)
            for s in range(8):
                code = jnp.where((lane >> 4) == s, pieces[8 * t + s, 64:72, :].astype(F32), code)
            members.append((owner == jnp.tile(code, (32, 1))).astype(F32).astype(BF16))
            values.append(
                jnp.concatenate(
                    [pieces[8 * t:8 * t + 8, 16 * c:16 * c + 16, :].reshape(128, 128) for c in range(4)]
                    + [jnp.ones((128, 128), BF16)],
                    axis=1,
                )
            )
        total = dot(jnp.concatenate(members, axis=1), jnp.concatenate(values, axis=0))
        total_ref[...] = total if b == 0 else total_ref[...] + total
    for block in range(4):
        parts = []
        for w in range(2):
            rows = slice(128 * w + 32 * block, 128 * w + 32 * block + 32)
            mean = CENTRE * total_ref[rows, 512:640]
            for c in range(4):
                parts.append(total_ref[rows, 128 * c:128 * c + 128] - mean)
        stacked = jnp.concatenate(parts, axis=0).astype(BF16)
        out_ref[32 * block:32 * block + 32] = dot(turn, stacked).reshape(32, 8, 128).astype(BF16)
    number_ref[...] = total_ref[:, 512:640]
    for w in range(2):
        own = number_ref[pl.ds(dev_ref[0] + 128 * w, 1), :]
        count_ref[8 * w:8 * w + 8, :] = jnp.broadcast_to(own, (8, 128))


def window_sums(dev, arrived):
    return pl.pallas_call(
        sums_kernel,
        in_specs=[SCALAR, ANYWHERE],
        out_specs=[BLOCK] * 2,
        out_shape=[
            jax.ShapeDtypeStruct((128, 8, 128), BF16),
            jax.ShapeDtypeStruct((16, 128), F32),
        ],
        scratch_shapes=[
            pltpu.VMEM((128, 72, 128), BF16),
            pltpu.VMEM((256, 640), F32),
            pltpu.VMEM((256, 128), F32),
            pltpu.SemaphoreType.DMA((4,)),
        ],
        compiler_params=params(60),
        name="window_sums",
    )(dev, arrived)


def outbound_kernel(dev_ref, in_ref, *out_refs):
    dev = dev_ref[0]
    member = dev % 16
    shift = 8 * (dev // 16) + member // 2
    for s in range(4):
        for t in range(4):
            target = 4 * ((member // 4) ^ t) + (member + s) % 4
            for w in range(2):
                row = (shift + 2 * place_of(dev // 16, target) + w) % 32
                for part in range(2):
                    out_refs[s][t, w, part] = in_ref[part, row].astype(BF16)


def tiles_to_windows(dev, tiles):
    blocks = pl.pallas_call(
        outbound_kernel,
        in_specs=[SCALAR, BLOCK],
        out_specs=[BLOCK] * 4,
        out_shape=[jax.ShapeDtypeStruct((4, 2, 2, 32, 128), BF16)] * 4,
        compiler_params=params(),
        name="outbound_tiles",
    )(dev, tiles)
    blocks = list(blocks)
    for s in range(1, 4):
        blocks[s] = lax.ppermute(blocks[s], ALL, [(d, d // 4 * 4 + (d + s) % 4) for d in range(128)])
    return blocks


def windows_from_lines(blocks):
    blocks = [jnp.stack([block[t] for block in blocks]) for t in range(4)]
    for t in range(1, 4):
        blocks[t] = lax.ppermute(blocks[t], ALL, [(d, d ^ (4 * t)) for d in range(128)])
    return blocks


def to_far_field(image, probe_ref, forward_ref, inverse_ref):
    waves = []
    for w in range(2):
        real, imag = [image[w][part].astype(BF16).astype(F32) for part in range(2)]
        waves.append(
            [
                (probe_ref[0] * real - probe_ref[1] * imag).astype(BF16),
                (probe_ref[0] * imag + probe_ref[1] * real).astype(BF16),
            ]
        )
    wave = jnp.concatenate(
        [jnp.concatenate([waves[0][part], waves[1][part]], axis=1) for part in range(2)], axis=0
    )
    midway = dot(forward_ref[...], wave).astype(BF16)
    midway = jnp.concatenate(
        [
            jnp.concatenate([midway[:256, 256 * w:256 * w + 256], midway[256:, 256 * w:256 * w + 256]], axis=1)
            for w in range(2)
        ],
        axis=0,
    )
    return dot(midway, inverse_ref[...])


def from_far_field(far, totals, counts, image, probe_ref, forward_ref, inverse_ref):
    changes = []
    for w in range(2):
        real, imag = far[256 * w:256 * w + 256, :256], far[256 * w:256 * w + 256, 256:]
        power = jnp.maximum(real * real + imag * imag, FLOOR * FLOOR)
        scale = totals[w] * lax.rsqrt(power) - counts[w]
        changes.append([(real * scale).astype(BF16), (imag * scale).astype(BF16)])
    change = jnp.concatenate(
        [jnp.concatenate([changes[0][part], changes[1][part]], axis=1) for part in range(2)], axis=0
    )
    halfway = dot(inverse_ref[...], change).astype(BF16)
    halfway = jnp.concatenate(
        [
            jnp.concatenate([halfway[:256, 256 * w:256 * w + 256], halfway[256:, 256 * w:256 * w + 256]], axis=1)
            for w in range(2)
        ],
        axis=0,
    )
    returned = dot(halfway, forward_ref[...])
    intensity = probe_ref[0] * probe_ref[0] + probe_ref[1] * probe_ref[1]
    relaxed = []
    for w in range(2):
        real, imag = returned[256 * w:256 * w + 256, :256], returned[256 * w:256 * w + 256, 256:]
        weight = 1.0 / (counts[w] * intensity + DELTA)
        relaxed.append(
            [
                image[w][0] + (probe_ref[0] * real + probe_ref[1] * imag) * weight,
                image[w][1] + (probe_ref[0] * imag - probe_ref[1] * real) * weight,
            ]
        )
    return relaxed


def own_counts(count_ref):
    return [jnp.tile(count_ref[8 * w:8 * w + 8, :], (32, 2)) for w in range(2)]


def write_relaxed(dev, relaxed, relaxed_ref, own_ref, edge_refs):
    for w in range(2):
        for part in range(2):
            relaxed_ref[w, part] = relaxed[w][part]
    rows = columns_as_rows(
        [(relaxed[w][part], 255 * side) for w, side in ((0, 1), (1, 0), (1, 1), (0, 0)) for part in range(2)]
    )[:8]
    own_ref[...] = rows
    place = iota((8, 256), 0)
    ahead, behind = pltpu.roll(rows, 6, 0), pltpu.roll(rows, 4, 0)
    up, down = rows, pltpu.roll(rows, 6, 0)
    for w in range(2):
        for part in range(2):
            at = 2 * w + part
            up = jnp.where(place == at, pltpu.roll(relaxed[w][part][248:], (at - 7) % 8, 0), up)
            first = relaxed[w][part][:8]
            down = jnp.where(place == at, pltpu.roll(first, at, 0) if at else first, down)
    group, spot, _ = window_rows(dev)
    odd_group, odd_spot = (group & 1) == 1, (spot & 1) == 1
    for ref, odd, even_edge, odd_edge in (
        (edge_refs[0], odd_spot, behind, ahead),
        (edge_refs[1], odd_spot, ahead, behind),
        (edge_refs[2], odd_group, up, down),
        (edge_refs[3], odd_group, down, up),
        (edge_refs[4], odd_group, ahead, behind),
        (edge_refs[5], odd_group, behind, ahead),
    ):
        ref[...] = jnp.where(odd, odd_edge, even_edge)


def exchange_edges(edges):
    moves = []
    for odd in range(2):
        moves.append(lambda g, q, odd=odd: (g, q + 1 if q % 2 == odd else q - 1))
    for odd in range(2):
        moves.append(lambda g, q, odd=odd: (g + 1 if g % 2 == odd else g - 1, q))
    for odd in range(2):
        moves.append(lambda g, q, odd=odd: (g + 1, q - 1) if g % 2 == odd else (g - 1, q + 1))
    return [lax.ppermute(edge, ALL, partners(move)) for edge, move in zip(edges, moves)]


def descend(x, left, right, up, down, keep_left, keep_right, keep_up, keep_down):
    rows, lanes = x[0].shape
    lane, row, row8 = iota((rows, lanes), 1), iota((rows, lanes), 0), iota((8, lanes), 0)

    def wide(narrow):
        return jnp.concatenate([narrow] * (lanes // 128), axis=1)

    across, edge, below, top = [], [], [], []
    for part in range(2):
        next_lane = jnp.where(lane == lanes - 1, wide(right[part]), pltpu.roll(x[part], lanes - 1, 1))
        across.append(next_lane - x[part])
        edge.append(x[part][:, :128] - left[part])
        next_row = jnp.where(
            row == rows - 1, jnp.broadcast_to(down[part], (rows, lanes)), pltpu.roll(x[part], rows - 1, 0)
        )
        below.append(next_row - x[part])
        top.append(x[part][:8] - jnp.broadcast_to(up[part], (8, lanes)))
    across_weight, edge_weight, below_weight, top_weight = [
        lax.rsqrt(d[0] * d[0] + d[1] * d[1] + EPS) * keep
        for d, keep in ((across, keep_right), (edge, keep_left), (below, keep_down), (top, keep_up))
    ]
    result = []
    for part in range(2):
        to_right = across[part] * across_weight
        to_left = jnp.where(lane == 0, wide(edge[part] * edge_weight), pltpu.roll(to_right, 1, 1))
        to_below = below[part] * below_weight
        moved = pltpu.roll(to_below, 1, 0)
        to_above = jnp.concatenate(
            [jnp.where(row8 == 0, top[part] * top_weight, moved[:8]), moved[8:]], axis=0
        )
        result.append(x[part] - STEP * ((to_left - to_right) + (to_above - to_below)))
    return result


def to_lane(block, source, lane):
    shift = (lane - source) % 128
    return pltpu.roll(block, shift, 1) if shift else block


def smooth(dev, relaxed_ref, own_ref, halo_refs):
    group, spot, starts = window_rows(dev)
    odd_group, odd_spot = (group & 1) == 1, (spot & 1) == 1
    beside0, beside1, above0, above1, corner0, corner1 = [ref[...] for ref in halo_refs]
    extra = iota((8, 256), 0) >= 6
    up_own = jnp.where(extra, jnp.where(odd_spot, beside1, beside0), own_ref[...])
    down_own = jnp.where(extra, jnp.where(odd_spot, beside0, beside1), pltpu.roll(own_ref[...], 6, 0))
    up_in = jnp.where(extra, jnp.where(odd_group, corner0, corner1), jnp.where(odd_group, above0, above1))
    down_in = jnp.where(extra, jnp.where(odd_group, corner1, corner0), jnp.where(odd_group, above1, above0))
    lane8 = iota((8, 256), 1)
    left = jnp.where(lane8 < 32, pltpu.roll(up_in, 32, 1), pltpu.roll(up_own, 32, 1))
    right = jnp.where(lane8 >= 224, pltpu.roll(down_in, 224, 1), pltpu.roll(down_own, 224, 1))
    sides = jnp.concatenate([left, right, jnp.zeros((112, 256), F32)], axis=0).T
    lane, row = iota((256, 256), 1), iota((256, 256), 0)
    image = []
    for w in range(2):
        start = starts[w]
        wrapped = (row // 32 + start) >= 32
        column = (16 * group - 2 * start + jnp.where(wrapped, 64, 0)) & 127
        image.append(
            descend(
                [relaxed_ref[w, part] for part in range(2)],
                [to_lane(sides, 4 + 2 * w + part, 0) for part in range(2)],
                [to_lane(sides, 8 + 4 + 2 * (1 - w) + part, 127) for part in range(2)],
                [up_in[2 * w + part:2 * w + part + 1] for part in range(2)],
                [down_in[2 * w + part:2 * w + part + 1] for part in range(2)],
                (column[:, :128] != 0).astype(F32),
                jnp.logical_not((lane == 255) & (column == 126)).astype(F32),
                (start != 0).astype(F32),
                (((32 * start + row) & 1023) != 1023).astype(F32),
            )
        )
    return image


def first_far_kernel(
    dev_ref, in0_ref, in1_ref, in2_ref, in3_ref, probe_ref, forward_ref, inverse_ref, far_ref, image_ref, half_ref
):
    member = dev_ref[0] % 16
    for t, in_ref in enumerate((in0_ref, in1_ref, in2_ref, in3_ref)):
        for s in range(4):
            source = 4 * ((member // 4) ^ t) + (member - s) % 4
            rows = pl.ds(pl.multiple_of(source // 2 * 32, 32), 32)
            for w in range(2):
                for part in range(2):
                    half_ref[w, part, source % 2, rows, :] = in_ref[s, w, part]
    image = []
    for w in range(2):
        image.append([])
        for part in range(2):
            whole = jnp.concatenate([half_ref[w, part, 0], half_ref[w, part, 1]], axis=1)
            image_ref[w, part] = whole
            image[w].append(whole)
    far_ref[...] = to_far_field(image, probe_ref, forward_ref, inverse_ref)


def first_back_kernel(
    dev_ref, far_ref, image_ref, sums_ref, count_ref, probe_ref, forward_ref, inverse_ref, total_ref, relaxed_ref,
    own_ref, *edge_refs
):
    counts = own_counts(count_ref)

    def source(o):
        w, half, row = o // 128, (o // 64) % 2, o % 64
        return ((row // 4) * 2 + half) * 8 + w * 4 + row % 4

    place = picker(source)
    blocks = []
    for block in range(4):
        rows = sums_ref[32 * block:32 * block + 32].astype(F32).reshape(256, 128).astype(BF16)
        blocks.append(dot(place, rows))
    totals = []
    for w in range(2):
        total = jnp.concatenate(
            [
                jnp.concatenate([b[128 * w:128 * w + 64], b[128 * w + 64:128 * w + 128]], axis=1)
                for b in blocks
            ],
            axis=0,
        ) + CENTRE * counts[w]
        total_ref[w] = total
        totals.append(total)
    image = [[image_ref[w, part].astype(F32) for part in range(2)] for w in range(2)]
    relaxed = from_far_field(far_ref[...], totals, counts, image, probe_ref, forward_ref, inverse_ref)
    write_relaxed(dev_ref[0], relaxed, relaxed_ref, own_ref, edge_refs)


def columns_as_rows(columns):
    lane = iota((256, 128), 1)
    gathered = jnp.zeros((256, 128), F32)
    for place, (image, at) in enumerate(columns):
        block = image[:, at // 128 * 128:at // 128 * 128 + 128]
        gathered = jnp.where(lane == place, to_lane(block, at % 128, place), gathered)
    return gathered.T


def second_kernel(
    dev_ref, in_ref, own_in, in0, in1, in2, in3, in4, in5, total_ref, count_ref, probe_ref, forward_ref, inverse_ref,
    out_ref, extra_ref
):
    image = smooth(dev_ref[0], in_ref, own_in, (in0, in1, in2, in3, in4, in5))
    far = to_far_field(image, probe_ref, forward_ref, inverse_ref)
    totals = [total_ref[w] for w in range(2)]
    relaxed = from_far_field(far, totals, own_counts(count_ref), image, probe_ref, forward_ref, inverse_ref)
    planes = [relaxed[w][part] for w in range(2) for part in range(2)]
    rows = columns_as_rows([(plane, at) for at in (127, 255, 128, 0) for plane in planes])
    lines = {}
    place, lane = iota((8, 256), 0), iota((8, 128), 1)
    for names, both in (((127, 255), rows[0:8]), ((128, 0), rows[8:16])):
        skewed = both
        for q in range(1, 4):
            skewed = jnp.where((place & 3) == q, pltpu.roll(both, 32 * q, 1), skewed)
        for i in range(8):
            turned = (pltpu.roll(skewed, 256 - 32 * i, 1) if i else skewed)[:, :128]
            turned = jnp.where((lane >> 5) == (place[:, :128] & 3), turned, 0.0)
            for at, half in zip(names, (turned[0:4], turned[4:8])):
                lines[at, i] = jnp.sum(half, axis=0, keepdims=True)
    extra_ref[...] = jnp.zeros_like(extra_ref)
    for k in range(16):
        i, j = k // 2, k % 2
        across, other = slice(128 * j, 128 * j + 128), slice(128 - 128 * j, 256 - 128 * j)
        for q, plane in enumerate(planes):
            out_ref[k, 32 * q:32 * q + 32, :] = plane[32 * i:32 * i + 32, across].astype(BF16)
            if i > 0:
                extra_ref[k, q:q + 1, :] = plane[32 * i - 1:32 * i, across]
            if i < 7:
                extra_ref[k, 4 + q:5 + q, :] = plane[32 * i + 32:32 * i + 33, across]
            if k in (8, 9):
                extra_ref[k, 8 + q:9 + q, :] = plane[255:256, across]
            if k in (6, 7):
                extra_ref[k, 8 + q:9 + q, :] = plane[0:1, across]
        if j == 1:
            extra_ref[k, 12:13, :] = lines[127, i]
            if i < 7:
                extra_ref[k, 13:14, :] = lines[0, i + 1]
        else:
            if i > 0:
                extra_ref[k, 12:13, :] = lines[255, i - 1]
            extra_ref[k, 13:14, :] = lines[128, i]
        if k == 8:
            extra_ref[k, 14:15, :] = lines[255, 7]
        if k == 7:
            extra_ref[k, 14:15, :] = lines[0, 0]
        out_ref[k, 128:144, :] = extra_ref[k].astype(BF16)


def inner_kernel(dev_ref, in_ref, out_ref):
    dev = dev_ref[0]
    group, member = dev // 16, dev % 16
    i, j = member // 2, member % 2
    order = [member_of(group, place) for place in range(16)]
    extra = [in_ref[m, 128:144, :].astype(F32) for m in order]
    left = jnp.concatenate([e[12:13] for e in extra], axis=0)
    right = jnp.concatenate([e[13:14] for e in extra], axis=0)
    first_half = iota((16, 128), 1) < 64
    turned = pltpu.roll(left, 64, 1)
    left = jnp.where(j == 1, left, jnp.where(first_half, turned, pltpu.roll(turned, 15, 0)))
    turned = pltpu.roll(right, 64, 1)
    right = jnp.where(j == 0, right, jnp.where(first_half, pltpu.roll(turned, 1, 0), turned))
    fill = jnp.zeros((112, 128), F32)
    left = jnp.concatenate([left, fill], axis=0).T
    right = jnp.concatenate([right, fill], axis=0).T
    last_lane = (iota((32, 128), 1) == 127).astype(F32)
    last_row = (iota((32, 128), 0) == 31).astype(F32)
    for u in range(32):
        place, w = u // 2, u % 2
        tile_row = (u + 8 * group + i) % 32
        tile_column = (dev - 2 * tile_row) & 127
        near, q = extra[place], [2 * w, 2 * w + 1]
        image = descend(
            [in_ref[order[place], pl.ds(32 * at, 32), :].astype(F32) for at in q],
            [to_lane(left[32 * at:32 * at + 32], place, 0) for at in q],
            [to_lane(right[32 * at:32 * at + 32], place, 127) for at in q],
            [near[at:at + 1] for at in q],
            [near[4 + at:5 + at] for at in q],
            ((tile_column != 0) & (member != 0)).astype(F32),
            1.0 - last_lane * ((tile_column == 127) | (member == 15)).astype(F32),
            ((tile_row != 0) & (i != 0)).astype(F32),
            1.0 - last_row * ((tile_row == 31) | (i == 7)).astype(F32),
        )
        for part in range(2):
            out_ref[part, tile_row] = image[part]


def border_kernel(dev_ref, in_ref, beyond_ref, inner_ref, out_ref):
    dev = dev_ref[0]
    group, member = dev // 16, dev % 16
    out_ref[...] = inner_ref[...]
    tiles = []
    for u in range(32):
        tile_row = (u + 8 * group + member // 2) % 32
        at = [32 * (2 * (u % 2) + part) for part in range(2)]
        tiles.append((u // 2, u % 2, tile_row, (dev - 2 * tile_row) & 127, member_of(group, u // 2), at))

    def beyond(place):
        return beyond_ref[member_of(group + 1, place)].astype(F32)

    def pull(d, keep):
        weight = STEP * lax.rsqrt(d[0] * d[0] + d[1] * d[1] + EPS) * keep
        return [d[0] * weight, d[1] * weight]

    def rows(at_row, edge_row):
        here = iota((8, 128), 0) == at_row % 8
        start = at_row // 8 * 8
        for place, w, tile_row, _, source, at in tiles:
            block = beyond(place)
            d = []
            for part in range(2):
                own = in_ref[source, pl.ds(at[part] + start // 16 * 16, 16), :].astype(F32)
                row = 8 + 2 * w + part
                d.append(own[start % 16:start % 16 + 8] - jnp.broadcast_to(block[row:row + 1], (8, 128)))
            for part, change in enumerate(pull(d, (tile_row != edge_row).astype(F32))):
                slot = out_ref.at[part, tile_row]
                slot[start:start + 8, :] = slot[start:start + 8, :] - jnp.where(here, change, 0.0)

    def columns(at_lane, edge_column):
        here = iota((32, 128), 1) == at_lane
        side = jnp.concatenate([beyond(place)[14:15] for place in range(16)], axis=0)
        half = iota((16, 128), 1) < 64
        turned = pltpu.roll(side, 64, 1)
        if at_lane == 0:
            side = jnp.where(half, turned, pltpu.roll(turned, 15, 0))
        else:
            side = jnp.where(half, pltpu.roll(turned, 1, 0), turned)
        side = jnp.concatenate([side, jnp.zeros((112, 128), F32)], axis=0).T
        for place, w, tile_row, tile_column, source, at in tiles:
            d = []
            for part in range(2):
                own = in_ref[source, pl.ds(at[part], 32), :].astype(F32)
                d.append(own - to_lane(side[at[part]:at[part] + 32], place, at_lane))
            for part, change in enumerate(pull(d, (tile_column != edge_column).astype(F32))):
                out_ref[part, tile_row] = out_ref[part, tile_row] - jnp.where(here, change, 0.0)

    pl.when(member < 2)(lambda: rows(0, 0))
    pl.when(member >= 14)(lambda: rows(31, 31))
    pl.when(member == 0)(lambda: columns(0, 0))
    pl.when(member == 15)(lambda: columns(127, 127))


def shards(object_tiles, amplitudes, probe, frame_pos):
    dev = lax.axis_index(ALL).astype(jnp.int32).reshape(1)
    forward, inverse = dft_blocks()

    lines = tiles_to_windows(dev, object_tiles)
    pieces = lax.all_to_all(amplitude_pieces(frame_pos, amplitudes), ALL, 0, 0, tiled=True)
    sums, counts = window_sums(dev, pieces)
    lines, sums = lax.optimization_barrier((lines, sums))
    tiles = windows_from_lines(lines)
    far, image = pl.pallas_call(
        first_far_kernel,
        in_specs=[SCALAR] + [BLOCK] * 7,
        out_specs=[BLOCK] * 2,
        out_shape=[jax.ShapeDtypeStruct((512, 512), F32), jax.ShapeDtypeStruct((2, 2, SIDE, SIDE), BF16)],
        scratch_shapes=[pltpu.VMEM((2, 2, 2, SIDE, 128), BF16)],
        compiler_params=params(),
        name="first_far",
    )(dev, *tiles, probe, forward, inverse)
    sums = lax.all_to_all(sums, ALL, 0, 0, tiled=True)
    totals, relaxed, own, *edges = pl.pallas_call(
        first_back_kernel,
        in_specs=[SCALAR] + [BLOCK] * 7,
        out_specs=[BLOCK] * 9,
        out_shape=[jax.ShapeDtypeStruct((2, SIDE, SIDE), F32), PAIR] + [EDGE] * 7,
        compiler_params=params(),
        name="first_back",
    )(dev, far, image, sums, counts, probe, forward, inverse)
    tiles = pl.pallas_call(
        second_kernel,
        in_specs=[SCALAR] + [BLOCK] * 13,
        out_specs=BLOCK,
        out_shape=jax.ShapeDtypeStruct((16, 144, 128), BF16),
        scratch_shapes=[pltpu.VMEM((16, 16, 128), F32)],
        compiler_params=params(),
        name="second_sweep",
    )(dev, relaxed, own, *exchange_edges(edges), totals, counts, probe, forward, inverse)
    tiles = lax.all_to_all(tiles, ALL, 0, 0, axis_index_groups=GROUPS, tiled=True)
    turns = ((8, 16), (9, 17), (7, -1), (6, -2))
    beyond = lax.ppermute(
        tiles[:, 128:], ALL, [(16 * g + k, (16 * g + to) % 128) for g in range(8) for k, to in turns]
    )
    result = jax.ShapeDtypeStruct((2, 32, 32, 128), F32)
    inner = pl.pallas_call(
        inner_kernel,
        in_specs=[SCALAR, BLOCK],
        out_specs=BLOCK,
        out_shape=result,
        compiler_params=params(),
        name="last_smoothing",
    )(dev, tiles)
    return pl.pallas_call(
        border_kernel,
        in_specs=[SCALAR] + [BLOCK] * 3,
        out_specs=BLOCK,
        out_shape=result,
        compiler_params=params(),
        name="last_borders",
    )(dev, tiles, beyond, inner)


def solution(mesh):
    return jax.shard_map(
        shards,
        mesh=mesh,
        in_specs=(P(None, ALL, None, None), P(ALL, None, None), P(), P(ALL, None)),
        out_specs=P(None, ALL, None, None),
        check_vma=False,
    )
```

time: 130 us -> 115 us (0.88)
  waiting for transfers between devices: 59.8 us -> 45.2 us
  local copies, waits for them, and re-layouts: 6.31 us -> 0.07 us
  Pallas kernels: 13.2 us -> 18.2 us
  blocking collectives: 14.5 us -> 15.9 us
    all_to_all x1 -> x0, waiting for transfers between devices: 8.06 us -> none  [shards(): lax.all_to_all(outbound_tiles(dev, object_tiles), ALL, 0, 0, axis_index_g...]
    all_to_all x1, waiting for transfers between devices: 7.74 us -> 0.01 us  [shards(): sums = lax.all_to_all(sums, ALL, 0, 0, tiled=True)]
    unnamed x19 -> x10, local copies, waits for them, and re-layouts: 6.31 us -> 0.02 us
    ppermute x8 -> x13, waiting for transfers between devices: 12 us -> 18 us  [the longest x3 8.32 us: windows_from_lines(): lax.ppermute(blocks[t], ALL, [(d, d ^ 4 * t) for d in range(128)])]
    pallas_call x8, Pallas kernels: 13.2 us -> 18.2 us  [the longest x1 3.83 us: amplitude_pieces(): pl.pallas_call(pieces_kernel, in_specs=[BLOCK, ANYWHERE], out_specs=ANYWH...]
    all_to_all x1, waiting for transfers between devices: 32 us -> 27.2 us  [shards(): lax.all_to_all(amplitude_pieces(frame_pos, amplitudes), ALL, 0, 0, tiled=...]
    all_to_all x1 -> x0, starting transfers between devices: 4.25 us -> none  [shards(): lax.all_to_all(outbound_tiles(dev, object_tiles), ALL, 0, 0, axis_index_g...]
    ppermute x8 -> x13, starting transfers between devices: 14.9 us -> 17.7 us  [the longest x6 9.24 us: exchange_edges(): lax.ppermute(edge, ALL, partners(move))]
  transfers between devices with their start and end apart: 11 -> 15, of which waited for: 9 -> 7; matrix products, arithmetic and copies ran while one was open for 0% -> 0% of each run, Pallas kernels for 3% -> 7%
where the time goes in v2:
time: 115 us; the launch traced here: 114 us
  waiting for transfers between devices  45.2 us (39%)
  starting transfers between devices  34.8 us (30%)
  Pallas kernels  18.2 us (16%)
  blocking collectives  15.9 us (14%)
    all_to_all x1, waiting for transfers between devices, shards(): lax.all_to_all(amplitude_pieces(frame_pos, amplitudes), ALL, 0, 0, tiled=...  27.2 us
    all_to_all x1, blocking collectives, shards(): lax.all_to_all(tiles, ALL, 0, 0, axis_index_groups=GROUPS, tiled=True)  15.9 us
    all_to_all x1, starting transfers between devices, shards(): lax.all_to_all(amplitude_pieces(frame_pos, amplitudes), ALL, 0, 0, tiled=...  11.6 us
    ppermute x6, starting transfers between devices, exchange_edges(): lax.ppermute(edge, ALL, partners(move))  9.24 us
    ppermute x3, waiting for transfers between devices, windows_from_lines(): lax.ppermute(blocks[t], ALL, [(d, d ^ 4 * t) for d in range(128)])  8.32 us
    ppermute x1, waiting for transfers between devices, shards(): lax.ppermute(tiles[:, 128:], ALL, [(16 * g + k, (16 * g + to) % 128) for...  5.54 us
    all_to_all x1, starting transfers between devices, shards(): sums = lax.all_to_all(sums, ALL, 0, 0, tiled=True)  5.44 us
    ppermute x3, starting transfers between devices, tiles_to_windows(): lax.ppermute(blocks[s], ALL, [(d, d // 4 * 4 + (d + s) % 4) for d in rang...  5.1 us
  transfers between devices with their start and end apart: 15, of which 7 were waited for; matrix products, arithmetic and copies ran while one was open for 0% of the time, Pallas kernels for 7%

profile of v2, /device:TPU:0, one launch (start us, length us, event | category | flops | bytes accessed | tf_op | source)
XLA Modules:
  0.0 114.4 jit_solution(16110337883753380716)
XLA Ops:
  0.0 3.8 %amplitude_pieces.1 = bf16[128,72,128]{2,1,0:T(8,128)(2,1)} custom-call(s32[2,16]{1,0:T(2,128)} %bitcast.2, bf16[16,256,256]{2,1,0:T(8,128)(2,1)} %amp_ref.1), custom_call_target="tpu_custom_call" | custom-call | tf_op jit(solution)/shard_map/amplitude_pieces/pallas_call | solution.py:115
  3.9 11.6 %all-to-all-start = ((bf16[128,72,128]{2,1,0:T(8,128)(2,1)}), bf16[128,72,128]{2,1,0:T(8,128)(2,1)}, u32[]{:S(2)}, u32[]{:S(2)}) async-start(bf16[128,72,128]{2,1,0:T(8,128)(2,1)} %amplitude_pieces.1), calls=%async_computation | async-start | bytes 4718592 | tf_op jit(solution)/shard_map/all_to_all | solution.py:613
  15.8 1.0 collective-permute-start
  16.8 2.7 %collective-permute-start.1 = (bf16[4,2,2,32,128]{4,3,2,1,0:T(8,128)(2,1)S(1)}, bf16[4,2,2,32,128]{4,3,2,1,0:T(8,128)(2,1)S(1)}, u32[]{:S(2)}, u32[]{:S(2)}) collective-permute-start(bf16[4,2,2,32,128]{4,3,2,1,0:T(8,128)(2,1)S(1)} %get-tuple-element.29), channel_id=1, source_target_pairs={{0,2},{1,3},{2,0},{3,1},{4,6},{5,7},{6,4},{7,5},{8,10},{9,11},{10,... | collective-permute-start | bytes 393224 | tf_op jit(solution)/shard_map/ppermute | solution.py:217
  19.5 1.5 %collective-permute-start.2 = (bf16[4,2,2,32,128]{4,3,2,1,0:T(8,128)(2,1)S(1)}, bf16[4,2,2,32,128]{4,3,2,1,0:T(8,128)(2,1)S(1)}, u32[]{:S(2)}, u32[]{:S(2)}) collective-permute-start(bf16[4,2,2,32,128]{4,3,2,1,0:T(8,128)(2,1)S(1)} %get-tuple-element.30), channel_id=1, source_target_pairs={{0,3},{1,0},{2,1},{3,2},{4,7},{5,4},{6,5},{7,6},{8,11},{9,8},{10,9... | collective-permute-start | bytes 393224 | tf_op jit(solution)/shard_map/ppermute | solution.py:217
  20.9 27.2 %all-to-all-done.in_ref = bf16[128,72,128]{2,1,0:T(8,128)(2,1)} async-done(((bf16[128,72,128]{2,1,0:T(8,128)(2,1)}), bf16[128,72,128]{2,1,0:T(8,128)(2,1)}, u32[]{:S(2)}, u32[]{:S(2)}) %all-to-all-start) | async-done | bytes 2359328 | tf_op jit(solution)/shard_map/all_to_all | solution.py:613
  48.1 3.6 %window_sums.1 = (bf16[128,8,128]{2,1,0:T(8,128)(2,1)}, f32[16,128]{1,0:T(8,128)}) custom-call(s32[1]{0:T(128)} %bitcast.dev_ref, bf16[128,72,128]{2,1,0:T(8,128)(2,1)} %all-to-all-done.in_ref), custom_call_target="tpu_custom_call" | custom-call | tf_op jit(solution)/shard_map/window_sums/pallas_call | solution.py:174
  51.8 5.4 %all-to-all-start.1 = ((bf16[128,8,128]{2,1,0:T(8,128)(2,1)}), bf16[128,8,128]{2,1,0:T(8,128)(2,1)S(1)}, u32[]{:S(2)}, u32[]{:S(2)}) async-start(bf16[128,8,128]{2,1,0:T(8,128)(2,1)} %get-tuple-element.38), calls=%async_computation.1 | async-start | bytes 524288 | tf_op jit(solution)/shard_map/all_to_all | solution.py:626
  57.4 1.2 %collective-permute-start.4 = (bf16[4,2,2,32,128]{4,3,2,1,0:T(8,128)(2,1)S(1)}, bf16[4,2,2,32,128]{4,3,2,1,0:T(8,128)(2,1)S(1)}, u32[]{:S(2)}, u32[]{:S(2)}) collective-permute-start(bf16[4,2,2,32,128]{4,3,2,1,0:T(8,128)(2,1)S(1)} %pad_maximum_fusion.2), channel_id=1, source_target_pairs={{0,8},{1,9},{2,10},{3,11},{4,12},{5,13},{6,14},{7,15},{8,0},{9,1},... | collective-permute-start | bytes 393224 | tf_op jit(solution)/shard_map/ppermute | solution.py:224
  59.5 5.8 %collective-permute-done.4.in2_ref = bf16[4,2,2,32,128]{4,3,2,1,0:T(8,128)(2,1)S(1)} collective-permute-done((bf16[4,2,2,32,128]{4,3,2,1,0:T(8,128)(2,1)S(1)}, bf16[4,2,2,32,128]{4,3,2,1,0:T(8,128)(2,1)S(1)}, u32[]{:S(2)}, u32[]{:S(2)}) %collective-permute-start.4) | collective-permute-done | bytes 131104 | tf_op jit(solution)/shard_map/ppermute | solution.py:224
  65.3 2.5 %collective-permute-done.5.in3_ref = bf16[4,2,2,32,128]{4,3,2,1,0:T(8,128)(2,1)S(1)} collective-permute-done((bf16[4,2,2,32,128]{4,3,2,1,0:T(8,128)(2,1)S(1)}, bf16[4,2,2,32,128]{4,3,2,1,0:T(8,128)(2,1)S(1)}, u32[]{:S(2)}, u32[]{:S(2)}) %collective-permute-start.5) | collective-permute-done | bytes 131104 | tf_op jit(solution)/shard_map/ppermute | solution.py:224
  67.8 1.0 first_far.1
  68.8 1.5 %first_back.1 = (f32[2,256,256]{2,1,0:T(8,128)S(1)}, f32[2,2,256,256]{3,2,1,0:T(8,128)S(1)}, f32[8,256]{1,0:T(8,128)S(1)}, f32[8,256]{1,0:T(8,128)S(1)}, f32[8,2...) custom-call(s32[1]{0:T(128)} %bitcast.dev_ref, ...), custom_call_target="tpu_custom_call" | custom-call | tf_op jit(solution)/shard_map/first_back/pallas_call | solution.py:627
  71.2 2.3 %collective-permute-start.8 = (f32[8,256]{1,0:T(8,128)S(1)}, f32[8,256]{1,0:T(8,128)S(1)}, u32[]{:S(2)}, u32[]{:S(2)}) collective-permute-start(f32[8,256]{1,0:T(8,128)S(1)} %get-tuple-element.44), channel_id=1, source_target_pairs={{0,24},{1,25},{2,26},{3,27},{4,28},{5,29},{6,30},{7,31},{8,16},{9,... | collective-permute-start | bytes 24584 | tf_op jit(solution)/shard_map/ppermute | solution.py:327
  73.5 3.8 %collective-permute-start.9 = (f32[8,256]{1,0:T(8,128)S(1)}, f32[8,256]{1,0:T(8,128)S(1)}, u32[]{:S(2)}, u32[]{:S(2)}) collective-permute-start(f32[8,256]{1,0:T(8,128)S(1)} %get-tuple-element.45), channel_id=1, source_target_pairs={{0,120},{1,121},{2,122},{3,123},{4,124},{5,125},{6,126},{7,127},{8... | collective-permute-start | bytes 24584 | tf_op jit(solution)/shard_map/ppermute | solution.py:327
  77.3 2.2 %collective-permute-start.11 = (f32[8,256]{1,0:T(8,128)S(1)}, f32[8,256]{1,0:T(8,128)S(1)}, u32[]{:S(2)}, u32[]{:S(2)}) collective-permute-start(f32[8,256]{1,0:T(8,128)S(1)} %get-tuple-element.47), channel_id=1, source_target_pairs={{0,124},{1,122},{2,126},{3,115},{4,125},{5,121},{6,127},{7,123},{8... | collective-permute-start | bytes 24584 | tf_op jit(solution)/shard_map/ppermute | solution.py:327
  80.4 2.0 %collective-permute-done.10.in4 = f32[8,256]{1,0:T(8,128)S(1)} collective-permute-done((f32[8,256]{1,0:T(8,128)S(1)}, f32[8,256]{1,0:T(8,128)S(1)}, u32[]{:S(2)}, u32[]{:S(2)}) %collective-permute-start.10) | collective-permute-done | bytes 8224 | tf_op jit(solution)/shard_map/ppermute | solution.py:327
  82.4 1.2 %collective-permute-done.11.in5 = f32[8,256]{1,0:T(8,128)S(1)} collective-permute-done((f32[8,256]{1,0:T(8,128)S(1)}, f32[8,256]{1,0:T(8,128)S(1)}, u32[]{:S(2)}, u32[]{:S(2)}) %collective-permute-start.11) | collective-permute-done | bytes 8224 | tf_op jit(solution)/shard_map/ppermute | solution.py:327
  83.7 3.5 %second_sweep.1 = bf16[16,144,128]{2,1,0:T(8,128)(2,1)S(1)} custom-call(s32[1]{0:T(128)} %bitcast.dev_ref, f32[2,2,256,256]{3,2,1,0:T(8,128)S(1)} %get-tuple-element.40.in_ref, f32[8,256]{1,0:T(8,128)S(1)} %get-tuple-element.41.own_in, f32[8,256]{1,0:T(8,128)S(1)} %collective-permute-done.6.in0, f32[8,256]{1,0:T(8,128)S(1)} %collective-permute-done.7.in1, ...), custom_call_target="tpu_custom_call" | custom-call | tf_op jit(solution)/shard_map/second_sweep/pallas_call | solution.py:635
  87.2 15.9 %all_to_all.15.in_ref = bf16[16,144,128]{2,1,0:T(8,128)(2,1)S(1)} all-to-all(bf16[16,144,128]{2,1,0:T(8,128)(2,1)S(1)} %second_sweep.1), channel_id=1, replica_groups={{0,1,2,3,4,5,6,7,8,9,10,11,12,13,14,15},{16,17,18,19,20,21,22,23,24,25,..., dimensions={0} | all-to-all | bytes 1179648 | tf_op jit(solution)/shard_map/all_to_all | solution.py:644
  103.1 1.3 %collective-permute-start.12 = (bf16[16,16,128]{2,1,0:T(8,128)(2,1)S(1)}, bf16[16,16,128]{2,1,0:T(8,128)(2,1)S(1)}, u32[]{:S(2)}, u32[]{:S(2)}) collective-permute-start(bf16[16,16,128]{2,1,0:T(8,128)(2,1)S(1)} %slice.68), channel_id=1, source_target_pairs={{8,16},{9,17},{7,127},{6,126},{24,32},{25,33},{23,15},{22,14},{40,... | collective-permute-start | bytes 196616 | tf_op jit(solution)/shard_map/ppermute | solution.py:646
  104.4 2.6 %last_smoothing.1.inner_ref = f32[2,32,32,128]{3,2,1,0:T(8,128)S(1)} custom-call(s32[1]{0:T(128)} %bitcast.dev_ref, bf16[16,144,128]{2,1,0:T(8,128)(2,1)S(1)} %all_to_all.15.in_ref), custom_call_target="tpu_custom_call" | custom-call | tf_op jit(solution)/shard_map/last_smoothing/pallas_call | solution.py:650
  107.1 5.5 %collective-permute-done.12.beyond_ref = bf16[16,16,128]{2,1,0:T(8,128)(2,1)S(1)} collective-permute-done((bf16[16,16,128]{2,1,0:T(8,128)(2,1)S(1)}, bf16[16,16,128]{2,1,0:T(8,128)(2,1)S(1)}, u32[]{:S(2)}, u32[]{:S(2)}) %collective-permute-start.12) | collective-permute-done | bytes 65568 | tf_op jit(solution)/shard_map/ppermute | solution.py:646
  112.6 1.9 %last_borders.1 = f32[2,32,32,128]{3,2,1,0:T(8,128)} custom-call(s32[1]{0:T(128)} %bitcast.dev_ref, bf16[16,144,128]{2,1,0:T(8,128)(2,1)S(1)} %all_to_all.15.in_ref, bf16[16,16,128]{2,1,0:T(8,128)(2,1)S(1)} %collective-permute-done.12.beyond_ref, f32[2,32,32,128]{3,2,1,0:T(8,128)S(1)} %last_smoothing.1.inner_ref), custom_call_target="tpu_custom_call" | custom-call | tf_op jit(solution)/shard_map/last_borders/pallas_call | solution.py:658
  (32 shorter events, 3.2 us)
Async XLA Ops:
  3.8 11.6 %copy-start.3 = (f32[2,32,32,128]{3,2,1,0:T(8,128)S(1)}, f32[2,32,32,128]{3,2,1,0:T(8,128)}, u32[]{:S(2)}) copy-start(f32[2,32,32,128]{3,2,1,0:T(8,128)} %in_ref.1) | copy-start | bytes 3145732
  3.9 44.2 %all-to-all-start = ((bf16[128,72,128]{2,1,0:T(8,128)(2,1)}), bf16[128,72,128]{2,1,0:T(8,128)(2,1)}, u32[]{:S(2)}, u32[]{:S(2)}) async-start(bf16[128,72,128]{2,1,0:T(8,128)(2,1)} %amplitude_pieces.1), calls=%async_computation | async-start | bytes 4718592 | tf_op jit(solution)/shard_map/all_to_all | solution.py:613
  15.8 35.9 %collective-permute-start = (bf16[4,2,2,32,128]{4,3,2,1,0:T(8,128)(2,1)S(1)}, bf16[4,2,2,32,128]{4,3,2,1,0:T(8,128)(2,1)S(1)}, u32[]{:S(2)}, u32[]{:S(2)}) collective-permute-start(bf16[4,2,2,32,128]{4,3,2,1,0:T(8,128)(2,1)S(1)} %get-tuple-element.28), channel_id=1, source_target_pairs={{0,1},{1,2},{2,3},{3,0},{4,5},{5,6},{6,7},{7,4},{8,9},{9,10},{10,1... | collective-permute-start | bytes 393224 | tf_op jit(solution)/shard_map/ppermute | solution.py:217
  16.8 35.0 %collective-permute-start.1 = (bf16[4,2,2,32,128]{4,3,2,1,0:T(8,128)(2,1)S(1)}, bf16[4,2,2,32,128]{4,3,2,1,0:T(8,128)(2,1)S(1)}, u32[]{:S(2)}, u32[]{:S(2)}) collective-permute-start(bf16[4,2,2,32,128]{4,3,2,1,0:T(8,128)(2,1)S(1)} %get-tuple-element.29), channel_id=1, source_target_pairs={{0,2},{1,3},{2,0},{3,1},{4,6},{5,7},{6,4},{7,5},{8,10},{9,11},{10,... | collective-permute-start | bytes 393224 | tf_op jit(solution)/shard_map/ppermute | solution.py:217
  19.4 48.3 %copy-start = (f32[2,256,256]{2,1,0:T(8,128)S(1)}, f32[2,256,256]{2,1,0:T(8,128)}, u32[]{:S(2)}) copy-start(f32[2,256,256]{2,1,0:T(8,128)} %probe_ref.5) | copy-start | bytes 1572868
  19.5 48.3 %copy-start.1 = (bf16[512,512]{1,0:T(8,128)(2,1)S(1)}, bf16[512,512]{1,0:T(8,128)(2,1)}, u32[]{:S(2)}) copy-start(bf16[512,512]{1,0:T(8,128)(2,1)} %constant.21.inverse_ref) | copy-start | bytes 1572868
  19.5 48.3 %copy-start.2 = (bf16[512,512]{1,0:T(8,128)(2,1)S(1)}, bf16[512,512]{1,0:T(8,128)(2,1)}, u32[]{:S(2)}) copy-start(bf16[512,512]{1,0:T(8,128)(2,1)} %constant.20.forward_ref) | copy-start | bytes 1572868
  19.5 32.3 %collective-permute-start.2 = (bf16[4,2,2,32,128]{4,3,2,1,0:T(8,128)(2,1)S(1)}, bf16[4,2,2,32,128]{4,3,2,1,0:T(8,128)(2,1)S(1)}, u32[]{:S(2)}, u32[]{:S(2)}) collective-permute-start(bf16[4,2,2,32,128]{4,3,2,1,0:T(8,128)(2,1)S(1)} %get-tuple-element.30), channel_id=1, source_target_pairs={{0,3},{1,0},{2,1},{3,2},{4,7},{5,4},{6,5},{7,6},{8,11},{9,8},{10,9... | collective-permute-start | bytes 393224 | tf_op jit(solution)/shard_map/ppermute | solution.py:217
  51.7 17.0 %copy-start.4 = (f32[16,128]{1,0:T(8,128)S(1)}, f32[16,128]{1,0:T(8,128)}, u32[]{:S(2)}) copy-start(f32[16,128]{1,0:T(8,128)} %get-tuple-element.39.count_ref) | copy-start | bytes 24580
  51.8 17.0 %all-to-all-start.1 = ((bf16[128,8,128]{2,1,0:T(8,128)(2,1)}), bf16[128,8,128]{2,1,0:T(8,128)(2,1)S(1)}, u32[]{:S(2)}, u32[]{:S(2)}) async-start(bf16[128,8,128]{2,1,0:T(8,128)(2,1)} %get-tuple-element.38), calls=%async_computation.1 | async-start | bytes 524288 | tf_op jit(solution)/shard_map/all_to_all | solution.py:626
  57.3 2.2 %collective-permute-start.3 = (bf16[4,2,2,32,128]{4,3,2,1,0:T(8,128)(2,1)S(1)}, bf16[4,2,2,32,128]{4,3,2,1,0:T(8,128)(2,1)S(1)}, u32[]{:S(2)}, u32[]{:S(2)}) collective-permute-start(bf16[4,2,2,32,128]{4,3,2,1,0:T(8,128)(2,1)S(1)} %pad_maximum_fusion.1), channel_id=1, source_target_pairs={{0,4},{1,5},{2,6},{3,7},{4,0},{5,1},{6,2},{7,3},{8,12},{9,13},{10,... | collective-permute-start | bytes 393224 | tf_op jit(solution)/shard_map/ppermute | solution.py:224
  57.4 7.9 %collective-permute-start.4 = (bf16[4,2,2,32,128]{4,3,2,1,0:T(8,128)(2,1)S(1)}, bf16[4,2,2,32,128]{4,3,2,1,0:T(8,128)(2,1)S(1)}, u32[]{:S(2)}, u32[]{:S(2)}) collective-permute-start(bf16[4,2,2,32,128]{4,3,2,1,0:T(8,128)(2,1)S(1)} %pad_maximum_fusion.2), channel_id=1, source_target_pairs={{0,8},{1,9},{2,10},{3,11},{4,12},{5,13},{6,14},{7,15},{8,0},{9,1},... | collective-permute-start | bytes 393224 | tf_op jit(solution)/shard_map/ppermute | solution.py:224
  58.6 9.2 %collective-permute-start.5 = (bf16[4,2,2,32,128]{4,3,2,1,0:T(8,128)(2,1)S(1)}, bf16[4,2,2,32,128]{4,3,2,1,0:T(8,128)(2,1)S(1)}, u32[]{:S(2)}, u32[]{:S(2)}) collective-permute-start(bf16[4,2,2,32,128]{4,3,2,1,0:T(8,128)(2,1)S(1)} %pad_maximum_fusion.3), channel_id=1, source_target_pairs={{0,12},{1,13},{2,14},{3,15},{4,8},{5,9},{6,10},{7,11},{8,4},{9,5},... | collective-permute-start | bytes 393224 | tf_op jit(solution)/shard_map/ppermute | solution.py:224
  70.3 7.0 %collective-permute-start.6 = (f32[8,256]{1,0:T(8,128)S(1)}, f32[8,256]{1,0:T(8,128)S(1)}, u32[]{:S(2)}, u32[]{:S(2)}) collective-permute-start(f32[8,256]{1,0:T(8,128)S(1)} %get-tuple-element.42), channel_id=1, source_target_pairs={{0,4},{1,5},{2,6},{3,7},{4,0},{5,1},{6,2},{7,3},{8,12},{9,13},{10,... | collective-permute-start | bytes 24584 | tf_op jit(solution)/shard_map/ppermute | solution.py:327
  70.5 9.0 %collective-permute-start.7 = (f32[8,256]{1,0:T(8,128)S(1)}, f32[8,256]{1,0:T(8,128)S(1)}, u32[]{:S(2)}, u32[]{:S(2)}) collective-permute-start(f32[8,256]{1,0:T(8,128)S(1)} %get-tuple-element.43), channel_id=1, source_target_pairs={{0,8},{1,2},{2,1},{3,11},{4,5},{5,4},{6,7},{7,6},{8,0},{9,10},{10,... | collective-permute-start | bytes 24584 | tf_op jit(solution)/shard_map/ppermute | solution.py:327
  71.2 8.3 %collective-permute-start.8 = (f32[8,256]{1,0:T(8,128)S(1)}, f32[8,256]{1,0:T(8,128)S(1)}, u32[]{:S(2)}, u32[]{:S(2)}) collective-permute-start(f32[8,256]{1,0:T(8,128)S(1)} %get-tuple-element.44), channel_id=1, source_target_pairs={{0,24},{1,25},{2,26},{3,27},{4,28},{5,29},{6,30},{7,31},{8,16},{9,... | collective-permute-start | bytes 24584 | tf_op jit(solution)/shard_map/ppermute | solution.py:327
  73.5 7.0 %collective-permute-start.9 = (f32[8,256]{1,0:T(8,128)S(1)}, f32[8,256]{1,0:T(8,128)S(1)}, u32[]{:S(2)}, u32[]{:S(2)}) collective-permute-start(f32[8,256]{1,0:T(8,128)S(1)} %get-tuple-element.45), channel_id=1, source_target_pairs={{0,120},{1,121},{2,122},{3,123},{4,124},{5,125},{6,126},{7,127},{8... | collective-permute-start | bytes 24584 | tf_op jit(solution)/shard_map/ppermute | solution.py:327
  77.3 5.2 %collective-permute-start.10 = (f32[8,256]{1,0:T(8,128)S(1)}, f32[8,256]{1,0:T(8,128)S(1)}, u32[]{:S(2)}, u32[]{:S(2)}) collective-permute-start(f32[8,256]{1,0:T(8,128)S(1)} %get-tuple-element.46), channel_id=1, source_target_pairs={{0,16},{1,29},{2,25},{3,31},{4,24},{5,28},{6,26},{7,30},{8,20},{9,... | collective-permute-start | bytes 24584 | tf_op jit(solution)/shard_map/ppermute | solution.py:327
  77.3 6.4 %collective-permute-start.11 = (f32[8,256]{1,0:T(8,128)S(1)}, f32[8,256]{1,0:T(8,128)S(1)}, u32[]{:S(2)}, u32[]{:S(2)}) collective-permute-start(f32[8,256]{1,0:T(8,128)S(1)} %get-tuple-element.47), channel_id=1, source_target_pairs={{0,124},{1,122},{2,126},{3,115},{4,125},{5,121},{6,127},{7,123},{8... | collective-permute-start | bytes 24584 | tf_op jit(solution)/shard_map/ppermute | solution.py:327
  103.1 9.5 %collective-permute-start.12 = (bf16[16,16,128]{2,1,0:T(8,128)(2,1)S(1)}, bf16[16,16,128]{2,1,0:T(8,128)(2,1)S(1)}, u32[]{:S(2)}, u32[]{:S(2)}) collective-permute-start(bf16[16,16,128]{2,1,0:T(8,128)(2,1)S(1)} %slice.68), channel_id=1, source_target_pairs={{8,16},{9,17},{7,127},{6,126},{24,32},{25,33},{23,15},{22,14},{40,... | collective-permute-start | bytes 196616 | tf_op jit(solution)/shard_map/ppermute | solution.py:646

commit v3 on v2

--- a/solution.py
+++ b/solution.py
@@ -213,14 +213,14 @@
         name="outbound_tiles",
     )(dev, tiles)
     blocks = list(blocks)
-    for s in range(1, 4):
+    for s in (2, 1, 3):
         blocks[s] = lax.ppermute(blocks[s], ALL, [(d, d // 4 * 4 + (d + s) % 4) for d in range(128)])
     return blocks
 
 
 def windows_from_lines(blocks):
     blocks = [jnp.stack([block[t] for block in blocks]) for t in range(4)]
-    for t in range(1, 4):
+    for t in (3, 2, 1):
         blocks[t] = lax.ppermute(blocks[t], ALL, [(d, d ^ (4 * t)) for d in range(128)])
     return blocks
 
@@ -306,24 +306,24 @@
     group, spot, _ = window_rows(dev)
     odd_group, odd_spot = (group & 1) == 1, (spot & 1) == 1
     for ref, odd, even_edge, odd_edge in (
-        (edge_refs[0], odd_spot, behind, ahead),
-        (edge_refs[1], odd_spot, ahead, behind),
-        (edge_refs[2], odd_group, up, down),
-        (edge_refs[3], odd_group, down, up),
-        (edge_refs[4], odd_group, ahead, behind),
-        (edge_refs[5], odd_group, behind, ahead),
+        (edge_refs[0], odd_group, behind, ahead),
+        (edge_refs[1], odd_group, ahead, behind),
+        (edge_refs[2], odd_group, down, up),
+        (edge_refs[3], odd_group, up, down),
+        (edge_refs[4], odd_spot, ahead, behind),
+        (edge_refs[5], odd_spot, behind, ahead),
     ):
         ref[...] = jnp.where(odd, odd_edge, even_edge)
 
 
 def exchange_edges(edges):
     moves = []
-    for odd in range(2):
+    for odd in (1, 0):
+        moves.append(lambda g, q, odd=odd: (g + 1, q - 1) if g % 2 == odd else (g - 1, q + 1))
+    for odd in (1, 0):
+        moves.append(lambda g, q, odd=odd: (g + 1 if g % 2 == odd else g - 1, q))
+    for odd in (1, 0):
         moves.append(lambda g, q, odd=odd: (g, q + 1 if q % 2 == odd else q - 1))
-    for odd in range(2):
-        moves.append(lambda g, q, odd=odd: (g + 1 if g % 2 == odd else g - 1, q))
-    for odd in range(2):
-        moves.append(lambda g, q, odd=odd: (g + 1, q - 1) if g % 2 == odd else (g - 1, q + 1))
     return [lax.ppermute(edge, ALL, partners(move)) for edge, move in zip(edges, moves)]
 
 
@@ -369,7 +369,7 @@
 def smooth(dev, relaxed_ref, own_ref, halo_refs):
     group, spot, starts = window_rows(dev)
     odd_group, odd_spot = (group & 1) == 1, (spot & 1) == 1
-    beside0, beside1, above0, above1, corner0, corner1 = [ref[...] for ref in halo_refs]
+    corner1, corner0, above1, above0, beside1, beside0 = [ref[...] for ref in halo_refs]
     extra = iota((8, 256), 0) >= 6
     up_own = jnp.where(extra, jnp.where(odd_spot, beside1, beside0), own_ref[...])
     down_own = jnp.where(extra, jnp.where(odd_spot, beside0, beside1), pltpu.roll(own_ref[...], 6, 0))
@@ -401,9 +401,11 @@
     return image
 
 
-def first_far_kernel(
-    dev_ref, in0_ref, in1_ref, in2_ref, in3_ref, probe_ref, forward_ref, inverse_ref, far_ref, image_ref, half_ref
+def first_kernel(
+    dev_ref, in0_ref, in1_ref, in2_ref, in3_ref, sums_ref, count_ref, probe_ref, forward_ref, inverse_ref, total_ref,
+    relaxed_ref, own_ref, *more_refs
 ):
+    *edge_refs, half_ref = more_refs
     member = dev_ref[0] % 16
     for t, in_ref in enumerate((in0_ref, in1_ref, in2_ref, in3_ref)):
         for s in range(4):
@@ -412,20 +414,11 @@
             for w in range(2):
                 for part in range(2):
                     half_ref[w, part, source % 2, rows, :] = in_ref[s, w, part]
-    image = []
-    for w in range(2):
-        image.append([])
-        for part in range(2):
-            whole = jnp.concatenate([half_ref[w, part, 0], half_ref[w, part, 1]], axis=1)
-            image_ref[w, part] = whole
-            image[w].append(whole)
-    far_ref[...] = to_far_field(image, probe_ref, forward_ref, inverse_ref)
-
-
-def first_back_kernel(
-    dev_ref, far_ref, image_ref, sums_ref, count_ref, probe_ref, forward_ref, inverse_ref, total_ref, relaxed_ref,
-    own_ref, *edge_refs
-):
+    image = [
+        [jnp.concatenate([half_ref[w, part, 0], half_ref[w, part, 1]], axis=1).astype(F32) for part in range(2)]
+        for w in range(2)
+    ]
+    far = to_far_field(image, probe_ref, forward_ref, inverse_ref)
     counts = own_counts(count_ref)
 
     def source(o):
@@ -448,8 +441,7 @@
         ) + CENTRE * counts[w]
         total_ref[w] = total
         totals.append(total)
-    image = [[image_ref[w, part].astype(F32) for part in range(2)] for w in range(2)]
-    relaxed = from_far_field(far_ref[...], totals, counts, image, probe_ref, forward_ref, inverse_ref)
+    relaxed = from_far_field(far, totals, counts, image, probe_ref, forward_ref, inverse_ref)
     write_relaxed(dev_ref[0], relaxed, relaxed_ref, own_ref, edge_refs)
 
 
@@ -575,7 +567,7 @@
             d = []
             for part in range(2):
                 own = in_ref[source, pl.ds(at[part] + start // 16 * 16, 16), :].astype(F32)
-                row = 8 + 2 * w + part
+                row = 2 * w + part
                 d.append(own[start % 16:start % 16 + 8] - jnp.broadcast_to(block[row:row + 1], (8, 128)))
             for part, change in enumerate(pull(d, (tile_row != edge_row).astype(F32))):
                 slot = out_ref.at[part, tile_row]
@@ -583,7 +575,7 @@
 
     def columns(at_lane, edge_column):
         here = iota((32, 128), 1) == at_lane
-        side = jnp.concatenate([beyond(place)[14:15] for place in range(16)], axis=0)
+        side = jnp.concatenate([beyond(place)[6:7] for place in range(16)], axis=0)
         half = iota((16, 128), 1) < 64
         turned = pltpu.roll(side, 64, 1)
         if at_lane == 0:
@@ -614,24 +606,16 @@
     sums, counts = window_sums(dev, pieces)
     lines, sums = lax.optimization_barrier((lines, sums))
     tiles = windows_from_lines(lines)
-    far, image = pl.pallas_call(
-        first_far_kernel,
-        in_specs=[SCALAR] + [BLOCK] * 7,
-        out_specs=[BLOCK] * 2,
-        out_shape=[jax.ShapeDtypeStruct((512, 512), F32), jax.ShapeDtypeStruct((2, 2, SIDE, SIDE), BF16)],
+    sums = lax.all_to_all(sums, ALL, 0, 0, tiled=True)
+    totals, relaxed, own, *edges = pl.pallas_call(
+        first_kernel,
+        in_specs=[SCALAR] + [BLOCK] * 9,
+        out_specs=[BLOCK] * 9,
+        out_shape=[jax.ShapeDtypeStruct((2, SIDE, SIDE), F32), PAIR] + [EDGE] * 7,
         scratch_shapes=[pltpu.VMEM((2, 2, 2, SIDE, 128), BF16)],
         compiler_params=params(),
-        name="first_far",
-    )(dev, *tiles, probe, forward, inverse)
-    sums = lax.all_to_all(sums, ALL, 0, 0, tiled=True)
-    totals, relaxed, own, *edges = pl.pallas_call(
-        first_back_kernel,
-        in_specs=[SCALAR] + [BLOCK] * 7,
-        out_specs=[BLOCK] * 9,
-        out_shape=[jax.ShapeDtypeStruct((2, SIDE, SIDE), F32), PAIR] + [EDGE] * 7,
-        compiler_params=params(),
-        name="first_back",
-    )(dev, far, image, sums, counts, probe, forward, inverse)
+        name="first_sweep",
+    )(dev, *tiles, sums, counts, probe, forward, inverse)
     tiles = pl.pallas_call(
         second_kernel,
         in_specs=[SCALAR] + [BLOCK] * 13,
@@ -644,7 +628,7 @@
     tiles = lax.all_to_all(tiles, ALL, 0, 0, axis_index_groups=GROUPS, tiled=True)
     turns = ((8, 16), (9, 17), (7, -1), (6, -2))
     beyond = lax.ppermute(
-        tiles[:, 128:], ALL, [(16 * g + k, (16 * g + to) % 128) for g in range(8) for k, to in turns]
+        tiles[:, 136:], ALL, [(16 * g + k, (16 * g + to) % 128) for g in range(8) for k, to in turns]
     )
     result = jax.ShapeDtypeStruct((2, 32, 32, 128), F32)
     inner = pl.pallas_call(

time: 115 us -> 113 us (0.983)
    pallas_call x2 -> x1, Pallas kernels: 2.45 us -> 2.21 us  [shards(): pl.pallas_call(first_kernel, in_specs=[SCALAR] + [BLOCK] * 9, out_specs=[...]
  transfers between devices with their start and end apart: 15 -> 15, of which waited for: 7 -> 8; matrix products, arithmetic and copies ran while one was open for 0% -> 0% of each run, Pallas kernels for 7% -> 6%
where the time goes in v3:
time: 113 us
  waiting for transfers between devices  44.4 us (39%)
  starting transfers between devices  34.7 us (31%)
  Pallas kernels  18.1 us (16%)
  blocking collectives  15 us (13%)
    all_to_all x1, waiting for transfers between devices, shards(): lax.all_to_all(amplitude_pieces(frame_pos, amplitudes), ALL, 0, 0, tiled=...  27.2 us
    all_to_all x1, blocking collectives, shards(): lax.all_to_all(tiles, ALL, 0, 0, axis_index_groups=GROUPS, tiled=True)  15 us
    all_to_all x1, starting transfers between devices, shards(): lax.all_to_all(amplitude_pieces(frame_pos, amplitudes), ALL, 0, 0, tiled=...  11.6 us
    ppermute x6, starting transfers between devices, exchange_edges(): lax.ppermute(edge, ALL, partners(move))  9.18 us
    ppermute x3, waiting for transfers between devices, windows_from_lines(): lax.ppermute(blocks[t], ALL, [(d, d ^ 4 * t) for d in range(128)])  8.32 us
    all_to_all x1, starting transfers between devices, shards(): sums = lax.all_to_all(sums, ALL, 0, 0, tiled=True)  5.44 us
    ppermute x1, waiting for transfers between devices, shards(): lax.ppermute(tiles[:, 136:], ALL, [(16 * g + k, (16 * g + to) % 128) for...  5.19 us
    ppermute x3, starting transfers between devices, tiles_to_windows(): lax.ppermute(blocks[s], ALL, [(d, d // 4 * 4 + (d + s) % 4) for d in rang...  5.1 us
  transfers between devices with their start and end apart: 15, of which 8 were waited for; matrix products, arithmetic and copies ran while one was open for 0% of the time, Pallas kernels for 6%

profile of v3, /device:TPU:0, one launch (start us, length us, event | category | flops | bytes accessed | tf_op | source)
XLA Modules:
  0.0 112.6 jit_solution(17089956759222709209)
XLA Ops:
  0.0 3.8 %amplitude_pieces.1 = bf16[128,72,128]{2,1,0:T(8,128)(2,1)} custom-call(s32[2,16]{1,0:T(2,128)} %bitcast.2, bf16[16,256,256]{2,1,0:T(8,128)(2,1)} %amp_ref.1), custom_call_target="tpu_custom_call" | custom-call | tf_op jit(solution)/shard_map/amplitude_pieces/pallas_call | solution.py:115
  3.9 11.6 %all-to-all-start = ((bf16[128,72,128]{2,1,0:T(8,128)(2,1)}), bf16[128,72,128]{2,1,0:T(8,128)(2,1)}, u32[]{:S(2)}, u32[]{:S(2)}) async-start(bf16[128,72,128]{2,1,0:T(8,128)(2,1)} %amplitude_pieces.1), calls=%async_computation | async-start | bytes 4718592 | tf_op jit(solution)/shard_map/all_to_all | solution.py:605
  15.8 1.0 collective-permute-start
  16.8 2.7 %collective-permute-start.1 = (bf16[4,2,2,32,128]{4,3,2,1,0:T(8,128)(2,1)S(1)}, bf16[4,2,2,32,128]{4,3,2,1,0:T(8,128)(2,1)S(1)}, u32[]{:S(2)}, u32[]{:S(2)}) collective-permute-start(bf16[4,2,2,32,128]{4,3,2,1,0:T(8,128)(2,1)S(1)} %get-tuple-element.27), channel_id=1, source_target_pairs={{0,2},{1,3},{2,0},{3,1},{4,6},{5,7},{6,4},{7,5},{8,10},{9,11},{10,... | collective-permute-start | bytes 393224 | tf_op jit(solution)/shard_map/ppermute | solution.py:217
  19.5 1.5 %collective-permute-start.2 = (bf16[4,2,2,32,128]{4,3,2,1,0:T(8,128)(2,1)S(1)}, bf16[4,2,2,32,128]{4,3,2,1,0:T(8,128)(2,1)S(1)}, u32[]{:S(2)}, u32[]{:S(2)}) collective-permute-start(bf16[4,2,2,32,128]{4,3,2,1,0:T(8,128)(2,1)S(1)} %get-tuple-element.28), channel_id=1, source_target_pairs={{0,3},{1,0},{2,1},{3,2},{4,7},{5,4},{6,5},{7,6},{8,11},{9,8},{10,9... | collective-permute-start | bytes 393224 | tf_op jit(solution)/shard_map/ppermute | solution.py:217
  20.9 27.2 %all-to-all-done.in_ref = bf16[128,72,128]{2,1,0:T(8,128)(2,1)} async-done(((bf16[128,72,128]{2,1,0:T(8,128)(2,1)}), bf16[128,72,128]{2,1,0:T(8,128)(2,1)}, u32[]{:S(2)}, u32[]{:S(2)}) %all-to-all-start) | async-done | bytes 2359328 | tf_op jit(solution)/shard_map/all_to_all | solution.py:605
  48.1 3.6 %window_sums.1 = (bf16[128,8,128]{2,1,0:T(8,128)(2,1)}, f32[16,128]{1,0:T(8,128)}) custom-call(s32[1]{0:T(128)} %bitcast.dev_ref, bf16[128,72,128]{2,1,0:T(8,128)(2,1)} %all-to-all-done.in_ref), custom_call_target="tpu_custom_call" | custom-call | tf_op jit(solution)/shard_map/window_sums/pallas_call | solution.py:174
  51.8 5.4 %all-to-all-start.1 = ((bf16[128,8,128]{2,1,0:T(8,128)(2,1)}), bf16[128,8,128]{2,1,0:T(8,128)(2,1)S(1)}, u32[]{:S(2)}, u32[]{:S(2)}) async-start(bf16[128,8,128]{2,1,0:T(8,128)(2,1)} %get-tuple-element.34), calls=%async_computation.1 | async-start | bytes 524288 | tf_op jit(solution)/shard_map/all_to_all | solution.py:609
  57.4 1.2 %collective-permute-start.4 = (bf16[4,2,2,32,128]{4,3,2,1,0:T(8,128)(2,1)S(1)}, bf16[4,2,2,32,128]{4,3,2,1,0:T(8,128)(2,1)S(1)}, u32[]{:S(2)}, u32[]{:S(2)}) collective-permute-start(bf16[4,2,2,32,128]{4,3,2,1,0:T(8,128)(2,1)S(1)} %pad_maximum_fusion.2), channel_id=1, source_target_pairs={{0,8},{1,9},{2,10},{3,11},{4,12},{5,13},{6,14},{7,15},{8,0},{9,1},... | collective-permute-start | bytes 393224 | tf_op jit(solution)/shard_map/ppermute | solution.py:224
  58.6 0.8 collective-permute-start.5
  59.5 5.8 %collective-permute-done.4.in2_ref = bf16[4,2,2,32,128]{4,3,2,1,0:T(8,128)(2,1)S(1)} collective-permute-done((bf16[4,2,2,32,128]{4,3,2,1,0:T(8,128)(2,1)S(1)}, bf16[4,2,2,32,128]{4,3,2,1,0:T(8,128)(2,1)S(1)}, u32[]{:S(2)}, u32[]{:S(2)}) %collective-permute-start.4) | collective-permute-done | bytes 131104 | tf_op jit(solution)/shard_map/ppermute | solution.py:224
  65.3 2.5 %collective-permute-done.5.in3_ref = bf16[4,2,2,32,128]{4,3,2,1,0:T(8,128)(2,1)S(1)} collective-permute-done((bf16[4,2,2,32,128]{4,3,2,1,0:T(8,128)(2,1)S(1)}, bf16[4,2,2,32,128]{4,3,2,1,0:T(8,128)(2,1)S(1)}, u32[]{:S(2)}, u32[]{:S(2)}) %collective-permute-start.5) | collective-permute-done | bytes 131104 | tf_op jit(solution)/shard_map/ppermute | solution.py:224
  67.9 2.2 %first_sweep.1 = (f32[2,256,256]{2,1,0:T(8,128)S(1)}, f32[2,2,256,256]{3,2,1,0:T(8,128)S(1)}, f32[8,256]{1,0:T(8,128)S(1)}, f32[8,256]{1,0:T(8,128)S(1)}, f32[8,...) custom-call(s32[1]{0:T(128)} %bitcast.dev_ref, ...), custom_call_target="tpu_custom_call" | custom-call | tf_op jit(solution)/shard_map/first_sweep/pallas_call | solution.py:610
  70.1 4.7 %collective-permute-start.6 = (f32[8,256]{1,0:T(8,128)S(1)}, f32[8,256]{1,0:T(8,128)S(1)}, u32[]{:S(2)}, u32[]{:S(2)}) collective-permute-start(f32[8,256]{1,0:T(8,128)S(1)} %get-tuple-element.38), channel_id=1, source_target_pairs={{0,124},{1,122},{2,126},{3,115},{4,125},{5,121},{6,127},{7,123},{8... | collective-permute-start | bytes 24584 | tf_op jit(solution)/shard_map/ppermute | solution.py:327
  74.9 3.2 %collective-permute-start.8 = (f32[8,256]{1,0:T(8,128)S(1)}, f32[8,256]{1,0:T(8,128)S(1)}, u32[]{:S(2)}, u32[]{:S(2)}) collective-permute-start(f32[8,256]{1,0:T(8,128)S(1)} %get-tuple-element.40), channel_id=1, source_target_pairs={{0,120},{1,121},{2,122},{3,123},{4,124},{5,125},{6,126},{7,127},{8... | collective-permute-start | bytes 24584 | tf_op jit(solution)/shard_map/ppermute | solution.py:327
  78.4 0.9 collective-permute-start.11
  80.0 1.8 %collective-permute-done.8.in2 = f32[8,256]{1,0:T(8,128)S(1)} collective-permute-done((f32[8,256]{1,0:T(8,128)S(1)}, f32[8,256]{1,0:T(8,128)S(1)}, u32[]{:S(2)}, u32[]{:S(2)}) %collective-permute-start.8) | collective-permute-done | bytes 8224 | tf_op jit(solution)/shard_map/ppermute | solution.py:327
  81.8 1.1 collective-permute-done.9.in3
  82.9 3.6 %second_sweep.1 = bf16[16,144,128]{2,1,0:T(8,128)(2,1)S(1)} custom-call(s32[1]{0:T(128)} %bitcast.dev_ref, f32[2,2,256,256]{3,2,1,0:T(8,128)S(1)} %get-tuple-element.36.in_ref, f32[8,256]{1,0:T(8,128)S(1)} %get-tuple-element.37.own_in, f32[8,256]{1,0:T(8,128)S(1)} %collective-permute-done.6.in0, f32[8,256]{1,0:T(8,128)S(1)} %collective-permute-done.7.in1, ...), custom_call_target="tpu_custom_call" | custom-call | tf_op jit(solution)/shard_map/second_sweep/pallas_call | solution.py:619
  86.6 15.0 %all_to_all.15.in_ref = bf16[16,144,128]{2,1,0:T(8,128)(2,1)S(1)} all-to-all(bf16[16,144,128]{2,1,0:T(8,128)(2,1)S(1)} %second_sweep.1), channel_id=1, replica_groups={{0,1,2,3,4,5,6,7,8,9,10,11,12,13,14,15},{16,17,18,19,20,21,22,23,24,25,..., dimensions={0} | all-to-all | bytes 1179648 | tf_op jit(solution)/shard_map/all_to_all | solution.py:628
  101.6 1.3 %collective-permute-start.12 = (bf16[16,8,128]{2,1,0:T(8,128)(2,1)S(1)}, bf16[16,8,128]{2,1,0:T(8,128)(2,1)S(1)}, u32[]{:S(2)}, u32[]{:S(2)}) collective-permute-start(bf16[16,8,128]{2,1,0:T(8,128)(2,1)S(1)} %slice.68), channel_id=1, source_target_pairs={{8,16},{9,17},{7,127},{6,126},{24,32},{25,33},{23,15},{22,14},{40,... | collective-permute-start | bytes 98312 | tf_op jit(solution)/shard_map/ppermute | solution.py:630
  102.9 2.6 %last_smoothing.1.inner_ref = f32[2,32,32,128]{3,2,1,0:T(8,128)S(1)} custom-call(s32[1]{0:T(128)} %bitcast.dev_ref, bf16[16,144,128]{2,1,0:T(8,128)(2,1)S(1)} %all_to_all.15.in_ref), custom_call_target="tpu_custom_call" | custom-call | tf_op jit(solution)/shard_map/last_smoothing/pallas_call | solution.py:634
  105.5 5.2 %collective-permute-done.12.beyond_ref = bf16[16,8,128]{2,1,0:T(8,128)(2,1)S(1)} collective-permute-done((bf16[16,8,128]{2,1,0:T(8,128)(2,1)S(1)}, bf16[16,8,128]{2,1,0:T(8,128)(2,1)S(1)}, u32[]{:S(2)}, u32[]{:S(2)}) %collective-permute-start.12) | collective-permute-done | bytes 32800 | tf_op jit(solution)/shard_map/ppermute | solution.py:630
  110.7 1.9 %last_borders.1 = f32[2,32,32,128]{3,2,1,0:T(8,128)} custom-call(s32[1]{0:T(128)} %bitcast.dev_ref, bf16[16,144,128]{2,1,0:T(8,128)(2,1)S(1)} %all_to_all.15.in_ref, bf16[16,8,128]{2,1,0:T(8,128)(2,1)S(1)} %collective-permute-done.12.beyond_ref, f32[2,32,32,128]{3,2,1,0:T(8,128)S(1)} %last_smoothing.1.inner_ref), custom_call_target="tpu_custom_call" | custom-call | tf_op jit(solution)/shard_map/last_borders/pallas_call | solution.py:642
  (31 shorter events, 1.7 us)
Async XLA Ops:
  3.8 11.6 %copy-start.3 = (f32[2,32,32,128]{3,2,1,0:T(8,128)S(1)}, f32[2,32,32,128]{3,2,1,0:T(8,128)}, u32[]{:S(2)}) copy-start(f32[2,32,32,128]{3,2,1,0:T(8,128)} %in_ref.1) | copy-start | bytes 3145732
  3.9 44.2 %all-to-all-start = ((bf16[128,72,128]{2,1,0:T(8,128)(2,1)}), bf16[128,72,128]{2,1,0:T(8,128)(2,1)}, u32[]{:S(2)}, u32[]{:S(2)}) async-start(bf16[128,72,128]{2,1,0:T(8,128)(2,1)} %amplitude_pieces.1), calls=%async_computation | async-start | bytes 4718592 | tf_op jit(solution)/shard_map/all_to_all | solution.py:605
  15.8 35.9 %collective-permute-start = (bf16[4,2,2,32,128]{4,3,2,1,0:T(8,128)(2,1)S(1)}, bf16[4,2,2,32,128]{4,3,2,1,0:T(8,128)(2,1)S(1)}, u32[]{:S(2)}, u32[]{:S(2)}) collective-permute-start(bf16[4,2,2,32,128]{4,3,2,1,0:T(8,128)(2,1)S(1)} %get-tuple-element.26), channel_id=1, source_target_pairs={{0,1},{1,2},{2,3},{3,0},{4,5},{5,6},{6,7},{7,4},{8,9},{9,10},{10,1... | collective-permute-start | bytes 393224 | tf_op jit(solution)/shard_map/ppermute | solution.py:217
  16.8 35.0 %collective-permute-start.1 = (bf16[4,2,2,32,128]{4,3,2,1,0:T(8,128)(2,1)S(1)}, bf16[4,2,2,32,128]{4,3,2,1,0:T(8,128)(2,1)S(1)}, u32[]{:S(2)}, u32[]{:S(2)}) collective-permute-start(bf16[4,2,2,32,128]{4,3,2,1,0:T(8,128)(2,1)S(1)} %get-tuple-element.27), channel_id=1, source_target_pairs={{0,2},{1,3},{2,0},{3,1},{4,6},{5,7},{6,4},{7,5},{8,10},{9,11},{10,... | collective-permute-start | bytes 393224 | tf_op jit(solution)/shard_map/ppermute | solution.py:217
  19.5 48.4 %copy-start = (f32[2,256,256]{2,1,0:T(8,128)S(1)}, f32[2,256,256]{2,1,0:T(8,128)}, u32[]{:S(2)}) copy-start(f32[2,256,256]{2,1,0:T(8,128)} %probe_ref.3) | copy-start | bytes 1572868
  19.5 48.4 %copy-start.1 = (bf16[512,512]{1,0:T(8,128)(2,1)S(1)}, bf16[512,512]{1,0:T(8,128)(2,1)}, u32[]{:S(2)}) copy-start(bf16[512,512]{1,0:T(8,128)(2,1)} %constant.21.inverse_ref) | copy-start | bytes 1572868
  19.5 48.4 %copy-start.2 = (bf16[512,512]{1,0:T(8,128)(2,1)S(1)}, bf16[512,512]{1,0:T(8,128)(2,1)}, u32[]{:S(2)}) copy-start(bf16[512,512]{1,0:T(8,128)(2,1)} %constant.20.forward_ref) | copy-start | bytes 1572868
  19.5 32.3 %collective-permute-start.2 = (bf16[4,2,2,32,128]{4,3,2,1,0:T(8,128)(2,1)S(1)}, bf16[4,2,2,32,128]{4,3,2,1,0:T(8,128)(2,1)S(1)}, u32[]{:S(2)}, u32[]{:S(2)}) collective-permute-start(bf16[4,2,2,32,128]{4,3,2,1,0:T(8,128)(2,1)S(1)} %get-tuple-element.28), channel_id=1, source_target_pairs={{0,3},{1,0},{2,1},{3,2},{4,7},{5,4},{6,5},{7,6},{8,11},{9,8},{10,9... | collective-permute-start | bytes 393224 | tf_op jit(solution)/shard_map/ppermute | solution.py:217
  51.7 16.2 %copy-start.4 = (f32[16,128]{1,0:T(8,128)S(1)}, f32[16,128]{1,0:T(8,128)}, u32[]{:S(2)}) copy-start(f32[16,128]{1,0:T(8,128)} %get-tuple-element.35.count_ref) | copy-start | bytes 24580
  51.8 16.1 %all-to-all-start.1 = ((bf16[128,8,128]{2,1,0:T(8,128)(2,1)}), bf16[128,8,128]{2,1,0:T(8,128)(2,1)S(1)}, u32[]{:S(2)}, u32[]{:S(2)}) async-start(bf16[128,8,128]{2,1,0:T(8,128)(2,1)} %get-tuple-element.34), calls=%async_computation.1 | async-start | bytes 524288 | tf_op jit(solution)/shard_map/all_to_all | solution.py:609
  57.3 2.2 %collective-permute-start.3 = (bf16[4,2,2,32,128]{4,3,2,1,0:T(8,128)(2,1)S(1)}, bf16[4,2,2,32,128]{4,3,2,1,0:T(8,128)(2,1)S(1)}, u32[]{:S(2)}, u32[]{:S(2)}) collective-permute-start(bf16[4,2,2,32,128]{4,3,2,1,0:T(8,128)(2,1)S(1)} %pad_maximum_fusion.1), channel_id=1, source_target_pairs={{0,4},{1,5},{2,6},{3,7},{4,0},{5,1},{6,2},{7,3},{8,12},{9,13},{10,... | collective-permute-start | bytes 393224 | tf_op jit(solution)/shard_map/ppermute | solution.py:224
  57.4 7.9 %collective-permute-start.4 = (bf16[4,2,2,32,128]{4,3,2,1,0:T(8,128)(2,1)S(1)}, bf16[4,2,2,32,128]{4,3,2,1,0:T(8,128)(2,1)S(1)}, u32[]{:S(2)}, u32[]{:S(2)}) collective-permute-start(bf16[4,2,2,32,128]{4,3,2,1,0:T(8,128)(2,1)S(1)} %pad_maximum_fusion.2), channel_id=1, source_target_pairs={{0,8},{1,9},{2,10},{3,11},{4,12},{5,13},{6,14},{7,15},{8,0},{9,1},... | collective-permute-start | bytes 393224 | tf_op jit(solution)/shard_map/ppermute | solution.py:224
  58.6 9.2 %collective-permute-start.5 = (bf16[4,2,2,32,128]{4,3,2,1,0:T(8,128)(2,1)S(1)}, bf16[4,2,2,32,128]{4,3,2,1,0:T(8,128)(2,1)S(1)}, u32[]{:S(2)}, u32[]{:S(2)}) collective-permute-start(bf16[4,2,2,32,128]{4,3,2,1,0:T(8,128)(2,1)S(1)} %pad_maximum_fusion.3), channel_id=1, source_target_pairs={{0,12},{1,13},{2,14},{3,15},{4,8},{5,9},{6,10},{7,11},{8,4},{9,5},... | collective-permute-start | bytes 393224 | tf_op jit(solution)/shard_map/ppermute | solution.py:224
  70.1 8.2 %collective-permute-start.6 = (f32[8,256]{1,0:T(8,128)S(1)}, f32[8,256]{1,0:T(8,128)S(1)}, u32[]{:S(2)}, u32[]{:S(2)}) collective-permute-start(f32[8,256]{1,0:T(8,128)S(1)} %get-tuple-element.38), channel_id=1, source_target_pairs={{0,124},{1,122},{2,126},{3,115},{4,125},{5,121},{6,127},{7,123},{8... | collective-permute-start | bytes 24584 | tf_op jit(solution)/shard_map/ppermute | solution.py:327
  74.8 5.2 %collective-permute-start.7 = (f32[8,256]{1,0:T(8,128)S(1)}, f32[8,256]{1,0:T(8,128)S(1)}, u32[]{:S(2)}, u32[]{:S(2)}) collective-permute-start(f32[8,256]{1,0:T(8,128)S(1)} %get-tuple-element.39), channel_id=1, source_target_pairs={{0,16},{1,29},{2,25},{3,31},{4,24},{5,28},{6,26},{7,30},{8,20},{9,... | collective-permute-start | bytes 24584 | tf_op jit(solution)/shard_map/ppermute | solution.py:327
  74.9 7.0 %collective-permute-start.8 = (f32[8,256]{1,0:T(8,128)S(1)}, f32[8,256]{1,0:T(8,128)S(1)}, u32[]{:S(2)}, u32[]{:S(2)}) collective-permute-start(f32[8,256]{1,0:T(8,128)S(1)} %get-tuple-element.40), channel_id=1, source_target_pairs={{0,120},{1,121},{2,122},{3,123},{4,124},{5,125},{6,126},{7,127},{8... | collective-permute-start | bytes 24584 | tf_op jit(solution)/shard_map/ppermute | solution.py:327
  78.0 4.9 %collective-permute-start.9 = (f32[8,256]{1,0:T(8,128)S(1)}, f32[8,256]{1,0:T(8,128)S(1)}, u32[]{:S(2)}, u32[]{:S(2)}) collective-permute-start(f32[8,256]{1,0:T(8,128)S(1)} %get-tuple-element.41), channel_id=1, source_target_pairs={{0,24},{1,25},{2,26},{3,27},{4,28},{5,29},{6,30},{7,31},{8,16},{9,... | collective-permute-start | bytes 24584 | tf_op jit(solution)/shard_map/ppermute | solution.py:327
  78.1 4.8 %collective-permute-start.10 = (f32[8,256]{1,0:T(8,128)S(1)}, f32[8,256]{1,0:T(8,128)S(1)}, u32[]{:S(2)}, u32[]{:S(2)}) collective-permute-start(f32[8,256]{1,0:T(8,128)S(1)} %get-tuple-element.42), channel_id=1, source_target_pairs={{0,8},{1,2},{2,1},{3,11},{4,5},{5,4},{6,7},{7,6},{8,0},{9,10},{10,... | collective-permute-start | bytes 24584 | tf_op jit(solution)/shard_map/ppermute | solution.py:327
  78.4 4.5 %collective-permute-start.11 = (f32[8,256]{1,0:T(8,128)S(1)}, f32[8,256]{1,0:T(8,128)S(1)}, u32[]{:S(2)}, u32[]{:S(2)}) collective-permute-start(f32[8,256]{1,0:T(8,128)S(1)} %get-tuple-element.43), channel_id=1, source_target_pairs={{0,4},{1,5},{2,6},{3,7},{4,0},{5,1},{6,2},{7,3},{8,12},{9,13},{10,... | collective-permute-start | bytes 24584 | tf_op jit(solution)/shard_map/ppermute | solution.py:327
  101.6 9.1 %collective-permute-start.12 = (bf16[16,8,128]{2,1,0:T(8,128)(2,1)S(1)}, bf16[16,8,128]{2,1,0:T(8,128)(2,1)S(1)}, u32[]{:S(2)}, u32[]{:S(2)}) collective-permute-start(bf16[16,8,128]{2,1,0:T(8,128)(2,1)S(1)} %slice.68), channel_id=1, source_target_pairs={{8,16},{9,17},{7,127},{6,126},{24,32},{25,33},{23,15},{22,14},{40,... | collective-permute-start | bytes 98312 | tf_op jit(solution)/shard_map/ppermute | solution.py:630

commit v4 on v3

--- a/solution.py
+++ b/solution.py
@@ -18,6 +18,7 @@
 GROUPS = [list(range(16 * g, 16 * g + 16)) for g in range(8)]
 SCALAR = pl.BlockSpec(memory_space=pltpu.SMEM)
 BLOCK = pl.BlockSpec(memory_space=pltpu.VMEM)
+EARLY, LATE = (0, 6, 5, 7, 2, 3), (4, 1)
 ANYWHERE = pl.BlockSpec(memory_space=pl.ANY)
 PAIR = jax.ShapeDtypeStruct((2, 2, SIDE, SIDE), F32)
 EDGE = jax.ShapeDtypeStruct((8, SIDE), F32)
@@ -194,35 +195,42 @@
     dev = dev_ref[0]
     member = dev % 16
     shift = 8 * (dev // 16) + member // 2
-    for s in range(4):
-        for t in range(4):
-            target = 4 * ((member // 4) ^ t) + (member + s) % 4
+    for t in range(8):
+        for e in range(2):
+            target = member ^ (8 * (t // 4) + t % 4 + 4 * e)
             for w in range(2):
                 row = (shift + 2 * place_of(dev // 16, target) + w) % 32
                 for part in range(2):
-                    out_refs[s][t, w, part] = in_ref[part, row].astype(BF16)
+                    out_refs[t][e, w, part] = in_ref[part, row].astype(BF16)
 
 
 def tiles_to_windows(dev, tiles):
     blocks = pl.pallas_call(
         outbound_kernel,
         in_specs=[SCALAR, BLOCK],
-        out_specs=[BLOCK] * 4,
-        out_shape=[jax.ShapeDtypeStruct((4, 2, 2, 32, 128), BF16)] * 4,
+        out_specs=[BLOCK] * 8,
+        out_shape=[jax.ShapeDtypeStruct((2, 2, 2, 32, 128), BF16)] * 8,
         compiler_params=params(),
         name="outbound_tiles",
     )(dev, tiles)
     blocks = list(blocks)
-    for s in (2, 1, 3):
-        blocks[s] = lax.ppermute(blocks[s], ALL, [(d, d // 4 * 4 + (d + s) % 4) for d in range(128)])
+    for t in EARLY[1:]:
+        blocks[t] = across_chips(blocks[t], t)
     return blocks
 
 
+def across_chips(block, t):
+    return lax.ppermute(block, ALL, [(d, d ^ (8 * (t // 4) + t % 4)) for d in range(128)])
+
+
 def windows_from_lines(blocks):
-    blocks = [jnp.stack([block[t] for block in blocks]) for t in range(4)]
-    for t in (3, 2, 1):
-        blocks[t] = lax.ppermute(blocks[t], ALL, [(d, d ^ (4 * t)) for d in range(128)])
-    return blocks
+    for t in LATE:
+        blocks[t] = across_chips(blocks[t], t)
+    other = [
+        lax.ppermute(jnp.stack([blocks[t][1] for t in part]), ALL, [(d, d ^ 4) for d in range(128)])
+        for part in (EARLY, LATE)
+    ]
+    return blocks + other
 
 
 def to_far_field(image, probe_ref, forward_ref, inverse_ref):
@@ -401,19 +409,23 @@
     return image
 
 
-def first_kernel(
-    dev_ref, in0_ref, in1_ref, in2_ref, in3_ref, sums_ref, count_ref, probe_ref, forward_ref, inverse_ref, total_ref,
-    relaxed_ref, own_ref, *more_refs
-):
-    *edge_refs, half_ref = more_refs
+def first_kernel(dev_ref, *refs):
+    block_refs, other_refs, (sums_ref, count_ref, probe_ref, forward_ref, inverse_ref) = refs[:8], refs[8:10], refs[10:15]
+    total_ref, relaxed_ref, own_ref, *edge_refs, half_ref = refs[15:]
     member = dev_ref[0] % 16
-    for t, in_ref in enumerate((in0_ref, in1_ref, in2_ref, in3_ref)):
-        for s in range(4):
-            source = 4 * ((member // 4) ^ t) + (member - s) % 4
+    for t in range(8):
+        for e in range(2):
+            source = member ^ (8 * (t // 4) + t % 4 + 4 * e)
             rows = pl.ds(pl.multiple_of(source // 2 * 32, 32), 32)
             for w in range(2):
                 for part in range(2):
-                    half_ref[w, part, source % 2, rows, :] = in_ref[s, w, part]
+                    if e == 0:
+                        tile = block_refs[t][0, w, part]
+                    elif t in LATE:
+                        tile = other_refs[1][LATE.index(t), w, part]
+                    else:
+                        tile = other_refs[0][EARLY.index(t), w, part]
+                    half_ref[w, part, source % 2, rows, :] = tile
     image = [
         [jnp.concatenate([half_ref[w, part, 0], half_ref[w, part, 1]], axis=1).astype(F32) for part in range(2)]
         for w in range(2)
@@ -609,7 +621,7 @@
     sums = lax.all_to_all(sums, ALL, 0, 0, tiled=True)
     totals, relaxed, own, *edges = pl.pallas_call(
         first_kernel,
-        in_specs=[SCALAR] + [BLOCK] * 9,
+        in_specs=[SCALAR] + [BLOCK] * 15,
         out_specs=[BLOCK] * 9,
         out_shape=[jax.ShapeDtypeStruct((2, SIDE, SIDE), F32), PAIR] + [EDGE] * 7,
         scratch_shapes=[pltpu.VMEM((2, 2, 2, SIDE, 128), BF16)],

time: 113 us -> 112 us (level)
  waiting for transfers between devices: 44.4 us -> 39.1 us
  starting transfers between devices: 34.7 us -> 38.3 us
    ppermute x6 -> x9, starting transfers between devices: 7.18 us -> 12.8 us  [the longest x7 12.7 us: across_chips(): lax.ppermute(block, ALL, [(d, d ^ 8 * (t // 4) + t % 4) for d in range(12...]
    all_to_all x1, waiting for transfers between devices: 27.2 us -> 22.1 us  [shards(): lax.all_to_all(amplitude_pieces(frame_pos, amplitudes), ALL, 0, 0, tiled=...]
    ppermute x6 -> x9, waiting for transfers between devices: 8.33 us -> 5.15 us  [the longest x7 3.91 us: across_chips(): lax.ppermute(block, ALL, [(d, d ^ 8 * (t // 4) + t % 4) for d in range(12...]
    all_to_all x1, waiting for transfers between devices: 0.1 us -> 2.97 us  [shards(): sums = lax.all_to_all(sums, ALL, 0, 0, tiled=True)]
    ppermute x6, starting transfers between devices: 9.18 us -> 6.62 us  [exchange_edges(): lax.ppermute(edge, ALL, partners(move))]
  transfers between devices with their start and end apart: 15 -> 18, of which waited for: 8 -> 9; matrix products, arithmetic and copies ran while one was open for 0% -> 0% of each run, Pallas kernels for 6% -> 6%
where the time goes in v4:
time: 112 us; the launch traced here: 111 us
  waiting for transfers between devices  39.1 us (35%)
  starting transfers between devices  38.3 us (34%)
  Pallas kernels  17.9 us (16%)
  blocking collectives  14.8 us (13%)
    all_to_all x1, waiting for transfers between devices, shards(): lax.all_to_all(amplitude_pieces(frame_pos, amplitudes), ALL, 0, 0, tiled=...  22.1 us
    all_to_all x1, blocking collectives, shards(): lax.all_to_all(tiles, ALL, 0, 0, axis_index_groups=GROUPS, tiled=True)  14.8 us
    ppermute x7, starting transfers between devices, across_chips(): lax.ppermute(block, ALL, [(d, d ^ 8 * (t // 4) + t % 4) for d in range(12...  12.7 us
    all_to_all x1, starting transfers between devices, shards(): lax.all_to_all(amplitude_pieces(frame_pos, amplitudes), ALL, 0, 0, tiled=...  11.6 us
    ppermute x6, starting transfers between devices, exchange_edges(): lax.ppermute(edge, ALL, partners(move))  6.62 us
    all_to_all x1, starting transfers between devices, shards(): sums = lax.all_to_all(sums, ALL, 0, 0, tiled=True)  6 us
    ppermute x1, waiting for transfers between devices, shards(): lax.ppermute(tiles[:, 136:], ALL, [(16 * g + k, (16 * g + to) % 128) for...  5.19 us
    ppermute x7, waiting for transfers between devices, across_chips(): lax.ppermute(block, ALL, [(d, d ^ 8 * (t // 4) + t % 4) for d in range(12...  3.91 us
  transfers between devices with their start and end apart: 18, of which 9 were waited for; matrix products, arithmetic and copies ran while one was open for 0% of the time, Pallas kernels for 6%

profile of v4, /device:TPU:0, one launch (start us, length us, event | category | flops | bytes accessed | tf_op | source)
XLA Modules:
  0.0 111.2 jit_solution(4493100442657507145)
XLA Ops:
  0.0 3.8 %amplitude_pieces.1 = bf16[128,72,128]{2,1,0:T(8,128)(2,1)} custom-call(s32[2,16]{1,0:T(2,128)} %bitcast.2, bf16[16,256,256]{2,1,0:T(8,128)(2,1)} %amp_ref.1), custom_call_target="tpu_custom_call" | custom-call | tf_op jit(solution)/shard_map/amplitude_pieces/pallas_call | solution.py:116
  3.9 11.6 %all-to-all-start = ((bf16[128,72,128]{2,1,0:T(8,128)(2,1)}), bf16[128,72,128]{2,1,0:T(8,128)(2,1)}, u32[]{:S(2)}, u32[]{:S(2)}) async-start(bf16[128,72,128]{2,1,0:T(8,128)(2,1)} %amplitude_pieces.1), calls=%async_computation | async-start | bytes 4718592 | tf_op jit(solution)/shard_map/all_to_all | solution.py:617
  15.8 2.5 %collective-permute-start = (bf16[2,2,2,32,128]{4,3,2,1,0:T(8,128)(2,1)S(1)}, bf16[2,2,2,32,128]{4,3,2,1,0:T(8,128)(2,1)S(1)}, u32[]{:S(2)}, u32[]{:S(2)}) collective-permute-start(bf16[2,2,2,32,128]{4,3,2,1,0:T(8,128)(2,1)S(1)} %get-tuple-element.35), channel_id=1, source_target_pairs={{0,2},{1,3},{2,0},{3,1},{4,6},{5,7},{6,4},{7,5},{8,10},{9,11},{10,... | collective-permute-start | bytes 196616 | tf_op jit(solution)/shard_map/ppermute | solution.py:223
  18.3 1.2 %collective-permute-start.1 = (bf16[2,2,2,32,128]{4,3,2,1,0:T(8,128)(2,1)S(1)}, bf16[2,2,2,32,128]{4,3,2,1,0:T(8,128)(2,1)S(1)}, u32[]{:S(2)}, u32[]{:S(2)}) collective-permute-start(bf16[2,2,2,32,128]{4,3,2,1,0:T(8,128)(2,1)S(1)} %get-tuple-element.36), channel_id=1, source_target_pairs={{0,3},{1,2},{2,1},{3,0},{4,7},{5,6},{6,5},{7,4},{8,11},{9,10},{10,... | collective-permute-start | bytes 196616 | tf_op jit(solution)/shard_map/ppermute | solution.py:223
  19.8 4.1 %collective-permute-start.3 = (bf16[2,2,2,32,128]{4,3,2,1,0:T(8,128)(2,1)S(1)}, bf16[2,2,2,32,128]{4,3,2,1,0:T(8,128)(2,1)S(1)}, u32[]{:S(2)}, u32[]{:S(2)}) collective-permute-start(bf16[2,2,2,32,128]{4,3,2,1,0:T(8,128)(2,1)S(1)} %get-tuple-element.39), channel_id=1, source_target_pairs={{0,10},{1,11},{2,8},{3,9},{4,14},{5,15},{6,12},{7,13},{8,2},{9,3},... | collective-permute-start | bytes 196616 | tf_op jit(solution)/shard_map/ppermute | solution.py:223
  23.9 2.1 %collective-permute-start.4 = (bf16[2,2,2,32,128]{4,3,2,1,0:T(8,128)(2,1)S(1)}, bf16[2,2,2,32,128]{4,3,2,1,0:T(8,128)(2,1)S(1)}, u32[]{:S(2)}, u32[]{:S(2)}) collective-permute-start(bf16[2,2,2,32,128]{4,3,2,1,0:T(8,128)(2,1)S(1)} %get-tuple-element.40), channel_id=1, source_target_pairs={{0,11},{1,10},{2,9},{3,8},{4,15},{5,14},{6,13},{7,12},{8,3},{9,2},... | collective-permute-start | bytes 196616 | tf_op jit(solution)/shard_map/ppermute | solution.py:223
  26.0 22.1 %all-to-all-done.in_ref = bf16[128,72,128]{2,1,0:T(8,128)(2,1)} async-done(((bf16[128,72,128]{2,1,0:T(8,128)(2,1)}), bf16[128,72,128]{2,1,0:T(8,128)(2,1)}, u32[]{:S(2)}, u32[]{:S(2)}) %all-to-all-start) | async-done | bytes 2359328 | tf_op jit(solution)/shard_map/all_to_all | solution.py:617
  48.1 3.6 %window_sums.1 = (bf16[128,8,128]{2,1,0:T(8,128)(2,1)}, f32[16,128]{1,0:T(8,128)}) custom-call(s32[1]{0:T(128)} %bitcast.dev_ref, bf16[128,72,128]{2,1,0:T(8,128)(2,1)} %all-to-all-done.in_ref), custom_call_target="tpu_custom_call" | custom-call | tf_op jit(solution)/shard_map/window_sums/pallas_call | solution.py:175
  51.8 6.0 %all-to-all-start.1 = ((bf16[128,8,128]{2,1,0:T(8,128)(2,1)}), bf16[128,8,128]{2,1,0:T(8,128)(2,1)S(1)}, u32[]{:S(2)}, u32[]{:S(2)}) async-start(bf16[128,8,128]{2,1,0:T(8,128)(2,1)} %get-tuple-element.50), calls=%async_computation.1 | async-start | bytes 524288 | tf_op jit(solution)/shard_map/all_to_all | solution.py:621
  58.8 1.5 %collective-permute-start.6 = (bf16[2,2,2,32,128]{4,3,2,1,0:T(8,128)(2,1)S(1)}, bf16[2,2,2,32,128]{4,3,2,1,0:T(8,128)(2,1)S(1)}, u32[]{:S(2)}, u32[]{:S(2)}) collective-permute-start(bf16[2,2,2,32,128]{4,3,2,1,0:T(8,128)(2,1)S(1)} %get-tuple-element.46), channel_id=1, source_target_pairs={{0,8},{1,9},{2,10},{3,11},{4,12},{5,13},{6,14},{7,15},{8,0},{9,1},... | collective-permute-start | bytes 196616 | tf_op jit(solution)/shard_map/ppermute | solution.py:223
  60.4 2.8 %collective-permute-done.5.refs_1_ = bf16[2,2,2,32,128]{4,3,2,1,0:T(8,128)(2,1)S(1)} collective-permute-done((bf16[2,2,2,32,128]{4,3,2,1,0:T(8,128)(2,1)S(1)}, bf16[2,2,2,32,128]{4,3,2,1,0:T(8,128)(2,1)S(1)}, u32[]{:S(2)}, u32[]{:S(2)}) %collective-permute-start.5) | collective-permute-done | bytes 65568 | tf_op jit(solution)/shard_map/ppermute | solution.py:223
  64.5 1.2 %collective-permute-done.8.refs_9_ = bf16[2,2,2,32,128]{4,3,2,1,0:T(8,128)(2,1)S(1)} collective-permute-done((bf16[2,2,2,32,128]{4,3,2,1,0:T(8,128)(2,1)S(1)}, bf16[2,2,2,32,128]{4,3,2,1,0:T(8,128)(2,1)S(1)}, u32[]{:S(2)}, u32[]{:S(2)}) %collective-permute-start.8) | collective-permute-done | bytes 65568 | tf_op jit(solution)/shard_map/ppermute | solution.py:230
  65.7 3.0 %all-to-all-done.1.refs_10_ = bf16[128,8,128]{2,1,0:T(8,128)(2,1)S(1)} async-done(((bf16[128,8,128]{2,1,0:T(8,128)(2,1)}), bf16[128,8,128]{2,1,0:T(8,128)(2,1)S(1)}, u32[]{:S(2)}, u32[]{:S(2)}) %all-to-all-start.1) | async-done | bytes 262176 | tf_op jit(solution)/shard_map/all_to_all | solution.py:621
  69.4 2.2 %first_sweep.1 = (f32[2,256,256]{2,1,0:T(8,128)S(1)}, f32[2,2,256,256]{3,2,1,0:T(8,128)S(1)}, f32[8,256]{1,0:T(8,128)S(1)}, f32[8,256]{1,0:T(8,128)S(1)}, f32[8,...) custom-call(s32[1]{0:T(128)} %bitcast.dev_ref, ...), custom_call_target="tpu_custom_call" | custom-call | tf_op jit(solution)/shard_map/first_sweep/pallas_call | solution.py:622
  71.5 2.2 %collective-permute-start.9 = (f32[8,256]{1,0:T(8,128)S(1)}, f32[8,256]{1,0:T(8,128)S(1)}, u32[]{:S(2)}, u32[]{:S(2)}) collective-permute-start(f32[8,256]{1,0:T(8,128)S(1)} %get-tuple-element.54), channel_id=1, source_target_pairs={{0,124},{1,122},{2,126},{3,115},{4,125},{5,121},{6,127},{7,123},{8... | collective-permute-start | bytes 24584 | tf_op jit(solution)/shard_map/ppermute | solution.py:335
  73.7 3.3 %collective-permute-start.11 = (f32[8,256]{1,0:T(8,128)S(1)}, f32[8,256]{1,0:T(8,128)S(1)}, u32[]{:S(2)}, u32[]{:S(2)}) collective-permute-start(f32[8,256]{1,0:T(8,128)S(1)} %get-tuple-element.56), channel_id=1, source_target_pairs={{0,120},{1,121},{2,122},{3,123},{4,124},{5,125},{6,126},{7,127},{8... | collective-permute-start | bytes 24584 | tf_op jit(solution)/shard_map/ppermute | solution.py:335
  78.9 1.8 %collective-permute-done.11.in2 = f32[8,256]{1,0:T(8,128)S(1)} collective-permute-done((f32[8,256]{1,0:T(8,128)S(1)}, f32[8,256]{1,0:T(8,128)S(1)}, u32[]{:S(2)}, u32[]{:S(2)}) %collective-permute-start.11) | collective-permute-done | bytes 8224 | tf_op jit(solution)/shard_map/ppermute | solution.py:335
  80.7 1.2 %collective-permute-done.12.in3 = f32[8,256]{1,0:T(8,128)S(1)} collective-permute-done((f32[8,256]{1,0:T(8,128)S(1)}, f32[8,256]{1,0:T(8,128)S(1)}, u32[]{:S(2)}, u32[]{:S(2)}) %collective-permute-start.12) | collective-permute-done | bytes 8224 | tf_op jit(solution)/shard_map/ppermute | solution.py:335
  81.9 3.5 %second_sweep.1 = bf16[16,144,128]{2,1,0:T(8,128)(2,1)S(1)} custom-call(s32[1]{0:T(128)} %bitcast.dev_ref, f32[2,2,256,256]{3,2,1,0:T(8,128)S(1)} %get-tuple-element.52.in_ref, f32[8,256]{1,0:T(8,128)S(1)} %get-tuple-element.53.own_in, f32[8,256]{1,0:T(8,128)S(1)} %collective-permute-done.9.in0, f32[8,256]{1,0:T(8,128)S(1)} %collective-permute-done.10.in1, ...), custom_call_target="tpu_custom_call" | custom-call | tf_op jit(solution)/shard_map/second_sweep/pallas_call | solution.py:631
  85.4 14.8 %all_to_all.15.in_ref = bf16[16,144,128]{2,1,0:T(8,128)(2,1)S(1)} all-to-all(bf16[16,144,128]{2,1,0:T(8,128)(2,1)S(1)} %second_sweep.1), channel_id=1, replica_groups={{0,1,2,3,4,5,6,7,8,9,10,11,12,13,14,15},{16,17,18,19,20,21,22,23,24,25,..., dimensions={0} | all-to-all | bytes 1179648 | tf_op jit(solution)/shard_map/all_to_all | solution.py:640
  100.3 1.3 %collective-permute-start.15 = (bf16[16,8,128]{2,1,0:T(8,128)(2,1)S(1)}, bf16[16,8,128]{2,1,0:T(8,128)(2,1)S(1)}, u32[]{:S(2)}, u32[]{:S(2)}) collective-permute-start(bf16[16,8,128]{2,1,0:T(8,128)(2,1)S(1)} %slice.38), channel_id=1, source_target_pairs={{8,16},{9,17},{7,127},{6,126},{24,32},{25,33},{23,15},{22,14},{40,... | collective-permute-start | bytes 98312 | tf_op jit(solution)/shard_map/ppermute | solution.py:642
  101.5 2.6 %last_smoothing.1.inner_ref = f32[2,32,32,128]{3,2,1,0:T(8,128)S(1)} custom-call(s32[1]{0:T(128)} %bitcast.dev_ref, bf16[16,144,128]{2,1,0:T(8,128)(2,1)S(1)} %all_to_all.15.in_ref), custom_call_target="tpu_custom_call" | custom-call | tf_op jit(solution)/shard_map/last_smoothing/pallas_call | solution.py:646
  104.2 5.2 %collective-permute-done.15.beyond_ref = bf16[16,8,128]{2,1,0:T(8,128)(2,1)S(1)} collective-permute-done((bf16[16,8,128]{2,1,0:T(8,128)(2,1)S(1)}, bf16[16,8,128]{2,1,0:T(8,128)(2,1)S(1)}, u32[]{:S(2)}, u32[]{:S(2)}) %collective-permute-start.15) | collective-permute-done | bytes 32800 | tf_op jit(solution)/shard_map/ppermute | solution.py:642
  109.4 1.9 %last_borders.1 = f32[2,32,32,128]{3,2,1,0:T(8,128)} custom-call(s32[1]{0:T(128)} %bitcast.dev_ref, bf16[16,144,128]{2,1,0:T(8,128)(2,1)S(1)} %all_to_all.15.in_ref, bf16[16,8,128]{2,1,0:T(8,128)(2,1)S(1)} %collective-permute-done.15.beyond_ref, f32[2,32,32,128]{3,2,1,0:T(8,128)S(1)} %last_smoothing.1.inner_ref), custom_call_target="tpu_custom_call" | custom-call | tf_op jit(solution)/shard_map/last_borders/pallas_call | solution.py:654
  (40 shorter events, 5.6 us)
Async XLA Ops:
  3.8 11.7 %copy-start.3 = (f32[2,32,32,128]{3,2,1,0:T(8,128)S(1)}, f32[2,32,32,128]{3,2,1,0:T(8,128)}, u32[]{:S(2)}) copy-start(f32[2,32,32,128]{3,2,1,0:T(8,128)} %in_ref.1) | copy-start | bytes 3145732
  3.9 44.2 %all-to-all-start = ((bf16[128,72,128]{2,1,0:T(8,128)(2,1)}), bf16[128,72,128]{2,1,0:T(8,128)(2,1)}, u32[]{:S(2)}, u32[]{:S(2)}) async-start(bf16[128,72,128]{2,1,0:T(8,128)(2,1)} %amplitude_pieces.1), calls=%async_computation | async-start | bytes 4718592 | tf_op jit(solution)/shard_map/all_to_all | solution.py:617
  15.5 53.2 %copy-start = (f32[2,256,256]{2,1,0:T(8,128)S(1)}, f32[2,256,256]{2,1,0:T(8,128)}, u32[]{:S(2)}) copy-start(f32[2,256,256]{2,1,0:T(8,128)} %probe_ref.1) | copy-start | bytes 1572868
  15.5 53.2 %copy-start.1 = (bf16[512,512]{1,0:T(8,128)(2,1)S(1)}, bf16[512,512]{1,0:T(8,128)(2,1)}, u32[]{:S(2)}) copy-start(bf16[512,512]{1,0:T(8,128)(2,1)} %constant.21.refs_14_.inverse_ref) | copy-start | bytes 1572868
  15.5 53.2 %copy-start.2 = (bf16[512,512]{1,0:T(8,128)(2,1)S(1)}, bf16[512,512]{1,0:T(8,128)(2,1)}, u32[]{:S(2)}) copy-start(bf16[512,512]{1,0:T(8,128)(2,1)} %constant.20.refs_13_.forward_ref) | copy-start | bytes 1572868
  15.8 35.9 %collective-permute-start = (bf16[2,2,2,32,128]{4,3,2,1,0:T(8,128)(2,1)S(1)}, bf16[2,2,2,32,128]{4,3,2,1,0:T(8,128)(2,1)S(1)}, u32[]{:S(2)}, u32[]{:S(2)}) collective-permute-start(bf16[2,2,2,32,128]{4,3,2,1,0:T(8,128)(2,1)S(1)} %get-tuple-element.35), channel_id=1, source_target_pairs={{0,2},{1,3},{2,0},{3,1},{4,6},{5,7},{6,4},{7,5},{8,10},{9,11},{10,... | collective-permute-start | bytes 196616 | tf_op jit(solution)/shard_map/ppermute | solution.py:223
  18.3 33.4 %collective-permute-start.1 = (bf16[2,2,2,32,128]{4,3,2,1,0:T(8,128)(2,1)S(1)}, bf16[2,2,2,32,128]{4,3,2,1,0:T(8,128)(2,1)S(1)}, u32[]{:S(2)}, u32[]{:S(2)}) collective-permute-start(bf16[2,2,2,32,128]{4,3,2,1,0:T(8,128)(2,1)S(1)} %get-tuple-element.36), channel_id=1, source_target_pairs={{0,3},{1,2},{2,1},{3,0},{4,7},{5,6},{6,5},{7,4},{8,11},{9,10},{10,... | collective-permute-start | bytes 196616 | tf_op jit(solution)/shard_map/ppermute | solution.py:223
  19.5 32.3 %collective-permute-start.2 = (bf16[2,2,2,32,128]{4,3,2,1,0:T(8,128)(2,1)S(1)}, bf16[2,2,2,32,128]{4,3,2,1,0:T(8,128)(2,1)S(1)}, u32[]{:S(2)}, u32[]{:S(2)}) collective-permute-start(bf16[2,2,2,32,128]{4,3,2,1,0:T(8,128)(2,1)S(1)} %get-tuple-element.38), channel_id=1, source_target_pairs={{0,9},{1,8},{2,11},{3,10},{4,13},{5,12},{6,15},{7,14},{8,1},{9,0},... | collective-permute-start | bytes 196616 | tf_op jit(solution)/shard_map/ppermute | solution.py:223
  19.8 32.0 %collective-permute-start.3 = (bf16[2,2,2,32,128]{4,3,2,1,0:T(8,128)(2,1)S(1)}, bf16[2,2,2,32,128]{4,3,2,1,0:T(8,128)(2,1)S(1)}, u32[]{:S(2)}, u32[]{:S(2)}) collective-permute-start(bf16[2,2,2,32,128]{4,3,2,1,0:T(8,128)(2,1)S(1)} %get-tuple-element.39), channel_id=1, source_target_pairs={{0,10},{1,11},{2,8},{3,9},{4,14},{5,15},{6,12},{7,13},{8,2},{9,3},... | collective-permute-start | bytes 196616 | tf_op jit(solution)/shard_map/ppermute | solution.py:223
  23.9 27.8 %collective-permute-start.4 = (bf16[2,2,2,32,128]{4,3,2,1,0:T(8,128)(2,1)S(1)}, bf16[2,2,2,32,128]{4,3,2,1,0:T(8,128)(2,1)S(1)}, u32[]{:S(2)}, u32[]{:S(2)}) collective-permute-start(bf16[2,2,2,32,128]{4,3,2,1,0:T(8,128)(2,1)S(1)} %get-tuple-element.40), channel_id=1, source_target_pairs={{0,11},{1,10},{2,9},{3,8},{4,15},{5,14},{6,13},{7,12},{8,3},{9,2},... | collective-permute-start | bytes 196616 | tf_op jit(solution)/shard_map/ppermute | solution.py:223
  51.8 16.9 %all-to-all-start.1 = ((bf16[128,8,128]{2,1,0:T(8,128)(2,1)}), bf16[128,8,128]{2,1,0:T(8,128)(2,1)S(1)}, u32[]{:S(2)}, u32[]{:S(2)}) async-start(bf16[128,8,128]{2,1,0:T(8,128)(2,1)} %get-tuple-element.50), calls=%async_computation.1 | async-start | bytes 524288 | tf_op jit(solution)/shard_map/all_to_all | solution.py:621
  57.8 5.5 %collective-permute-start.5 = (bf16[2,2,2,32,128]{4,3,2,1,0:T(8,128)(2,1)S(1)}, bf16[2,2,2,32,128]{4,3,2,1,0:T(8,128)(2,1)S(1)}, u32[]{:S(2)}, u32[]{:S(2)}) collective-permute-start(bf16[2,2,2,32,128]{4,3,2,1,0:T(8,128)(2,1)S(1)} %get-tuple-element.43), channel_id=1, source_target_pairs={{0,1},{1,0},{2,3},{3,2},{4,5},{5,4},{6,7},{7,6},{8,9},{9,8},{10,11... | collective-permute-start | bytes 196616 | tf_op jit(solution)/shard_map/ppermute | solution.py:223
  58.8 5.5 %collective-permute-start.6 = (bf16[2,2,2,32,128]{4,3,2,1,0:T(8,128)(2,1)S(1)}, bf16[2,2,2,32,128]{4,3,2,1,0:T(8,128)(2,1)S(1)}, u32[]{:S(2)}, u32[]{:S(2)}) collective-permute-start(bf16[2,2,2,32,128]{4,3,2,1,0:T(8,128)(2,1)S(1)} %get-tuple-element.46), channel_id=1, source_target_pairs={{0,8},{1,9},{2,10},{3,11},{4,12},{5,13},{6,14},{7,15},{8,0},{9,1},... | collective-permute-start | bytes 196616 | tf_op jit(solution)/shard_map/ppermute | solution.py:223
  60.4 5.3 %collective-permute-start.7 = (bf16[6,2,2,32,128]{4,3,2,1,0:T(8,128)(2,1)S(1)}, bf16[6,2,2,32,128]{4,3,2,1,0:T(8,128)(2,1)S(1)}, u32[]{:S(2)}, u32[]{:S(2)}) collective-permute-start(bf16[6,2,2,32,128]{4,3,2,1,0:T(8,128)(2,1)S(1)} %slice_dynamic-update-slice_fusion), channel_id=1, source_target_pairs={{0,4},{1,5},{2,6},{3,7},{4,0},{5,1},{6,2},{7,3},{8,12},{9,13},{10,... | collective-permute-start | bytes 589832 | tf_op jit(solution)/shard_map/ppermute | solution.py:230
  64.4 1.3 %collective-permute-start.8 = (bf16[2,2,2,32,128]{4,3,2,1,0:T(8,128)(2,1)S(1)}, bf16[2,2,2,32,128]{4,3,2,1,0:T(8,128)(2,1)S(1)}, u32[]{:S(2)}, u32[]{:S(2)}) collective-permute-start(bf16[2,2,2,32,128]{4,3,2,1,0:T(8,128)(2,1)S(1)} %pad_maximum_fusion), channel_id=1, source_target_pairs={{0,4},{1,5},{2,6},{3,7},{4,0},{5,1},{6,2},{7,3},{8,12},{9,13},{10,... | collective-permute-start | bytes 196616 | tf_op jit(solution)/shard_map/ppermute | solution.py:230
  68.7 0.7 copy-start.4
  71.5 6.5 %collective-permute-start.9 = (f32[8,256]{1,0:T(8,128)S(1)}, f32[8,256]{1,0:T(8,128)S(1)}, u32[]{:S(2)}, u32[]{:S(2)}) collective-permute-start(f32[8,256]{1,0:T(8,128)S(1)} %get-tuple-element.54), channel_id=1, source_target_pairs={{0,124},{1,122},{2,126},{3,115},{4,125},{5,121},{6,127},{7,123},{8... | collective-permute-start | bytes 24584 | tf_op jit(solution)/shard_map/ppermute | solution.py:335
  73.7 5.2 %collective-permute-start.10 = (f32[8,256]{1,0:T(8,128)S(1)}, f32[8,256]{1,0:T(8,128)S(1)}, u32[]{:S(2)}, u32[]{:S(2)}) collective-permute-start(f32[8,256]{1,0:T(8,128)S(1)} %get-tuple-element.55), channel_id=1, source_target_pairs={{0,16},{1,29},{2,25},{3,31},{4,24},{5,28},{6,26},{7,30},{8,20},{9,... | collective-permute-start | bytes 24584 | tf_op jit(solution)/shard_map/ppermute | solution.py:335
  73.7 7.0 %collective-permute-start.11 = (f32[8,256]{1,0:T(8,128)S(1)}, f32[8,256]{1,0:T(8,128)S(1)}, u32[]{:S(2)}, u32[]{:S(2)}) collective-permute-start(f32[8,256]{1,0:T(8,128)S(1)} %get-tuple-element.56), channel_id=1, source_target_pairs={{0,120},{1,121},{2,122},{3,123},{4,124},{5,125},{6,126},{7,127},{8... | collective-permute-start | bytes 24584 | tf_op jit(solution)/shard_map/ppermute | solution.py:335
  77.0 4.9 %collective-permute-start.12 = (f32[8,256]{1,0:T(8,128)S(1)}, f32[8,256]{1,0:T(8,128)S(1)}, u32[]{:S(2)}, u32[]{:S(2)}) collective-permute-start(f32[8,256]{1,0:T(8,128)S(1)} %get-tuple-element.57), channel_id=1, source_target_pairs={{0,24},{1,25},{2,26},{3,27},{4,28},{5,29},{6,30},{7,31},{8,16},{9,... | collective-permute-start | bytes 24584 | tf_op jit(solution)/shard_map/ppermute | solution.py:335
  77.0 4.9 %collective-permute-start.13 = (f32[8,256]{1,0:T(8,128)S(1)}, f32[8,256]{1,0:T(8,128)S(1)}, u32[]{:S(2)}, u32[]{:S(2)}) collective-permute-start(f32[8,256]{1,0:T(8,128)S(1)} %get-tuple-element.58), channel_id=1, source_target_pairs={{0,8},{1,2},{2,1},{3,11},{4,5},{5,4},{6,7},{7,6},{8,0},{9,10},{10,... | collective-permute-start | bytes 24584 | tf_op jit(solution)/shard_map/ppermute | solution.py:335
  78.0 3.9 %collective-permute-start.14 = (f32[8,256]{1,0:T(8,128)S(1)}, f32[8,256]{1,0:T(8,128)S(1)}, u32[]{:S(2)}, u32[]{:S(2)}) collective-permute-start(f32[8,256]{1,0:T(8,128)S(1)} %get-tuple-element.59), channel_id=1, source_target_pairs={{0,4},{1,5},{2,6},{3,7},{4,0},{5,1},{6,2},{7,3},{8,12},{9,13},{10,... | collective-permute-start | bytes 24584 | tf_op jit(solution)/shard_map/ppermute | solution.py:335
  100.3 9.1 %collective-permute-start.15 = (bf16[16,8,128]{2,1,0:T(8,128)(2,1)S(1)}, bf16[16,8,128]{2,1,0:T(8,128)(2,1)S(1)}, u32[]{:S(2)}, u32[]{:S(2)}) collective-permute-start(bf16[16,8,128]{2,1,0:T(8,128)(2,1)S(1)} %slice.38), channel_id=1, source_target_pairs={{8,16},{9,17},{7,127},{6,126},{24,32},{25,33},{23,15},{22,14},{40,... | collective-permute-start | bytes 98312 | tf_op jit(solution)/shard_map/ppermute | solution.py:642

commit v5 on v4

--- a/solution.py
+++ b/solution.py
@@ -291,7 +291,7 @@
 
 
 def own_counts(count_ref):
-    return [jnp.tile(count_ref[8 * w:8 * w + 8, :], (32, 2)) for w in range(2)]
+    return [jnp.tile(count_ref[8 * w:8 * w + 8, :], (32, 1)) for w in range(2)]
 
 
 def write_relaxed(dev, relaxed, relaxed_ref, own_ref, edge_refs):
@@ -616,6 +616,7 @@
     lines = tiles_to_windows(dev, object_tiles)
     pieces = lax.all_to_all(amplitude_pieces(frame_pos, amplitudes), ALL, 0, 0, tiled=True)
     sums, counts = window_sums(dev, pieces)
+    counts = jnp.concatenate([counts, counts], axis=1)
     lines, sums = lax.optimization_barrier((lines, sums))
     tiles = windows_from_lines(lines)
     sums = lax.all_to_all(sums, ALL, 0, 0, tiled=True)

time: 112 us -> 111 us (level)
  waiting for transfers between devices: 39.1 us -> 37.8 us
  transfers between devices with their start and end apart: 18 -> 18, of which waited for: 9 -> 9; matrix products, arithmetic and copies ran while one was open for 0% -> 1% of each run, Pallas kernels for 6% -> 6%
where the time goes in v5:
time: 111 us
  starting transfers between devices  38.2 us (34%)
  waiting for transfers between devices  37.8 us (34%)
  Pallas kernels  18 us (16%)
  blocking collectives  14.8 us (13%)
  local copies, waits for them, and re-layouts  1.49 us (1%)
    all_to_all x1, waiting for transfers between devices, shards(): lax.all_to_all(amplitude_pieces(frame_pos, amplitudes), ALL, 0, 0, tiled=...  22.1 us
    all_to_all x1, blocking collectives, shards(): lax.all_to_all(tiles, ALL, 0, 0, axis_index_groups=GROUPS, tiled=True)  14.8 us
    ppermute x7, starting transfers between devices, across_chips(): lax.ppermute(block, ALL, [(d, d ^ 8 * (t // 4) + t % 4) for d in range(12...  12.7 us
    all_to_all x1, starting transfers between devices, shards(): lax.all_to_all(amplitude_pieces(frame_pos, amplitudes), ALL, 0, 0, tiled=...  11.6 us
    ppermute x6, starting transfers between devices, exchange_edges(): lax.ppermute(edge, ALL, partners(move))  6.61 us
    all_to_all x1, starting transfers between devices, shards(): sums = lax.all_to_all(sums, ALL, 0, 0, tiled=True)  6 us
    ppermute x1, waiting for transfers between devices, shards(): lax.ppermute(tiles[:, 136:], ALL, [(16 * g + k, (16 * g + to) % 128) for...  5.19 us
    pallas_call x1, Pallas kernels, amplitude_pieces(): pl.pallas_call(pieces_kernel, in_specs=[BLOCK, ANYWHERE], out_specs=ANYWH...  3.83 us
  transfers between devices with their start and end apart: 18, of which 9 were waited for; matrix products, arithmetic and copies ran while one was open for 1% of the time, Pallas kernels for 6%

profile of v5, /device:TPU:0, one launch (start us, length us, event | category | flops | bytes accessed | tf_op | source)
XLA Modules:
  0.0 110.6 jit_solution(10769363058360825087)
XLA Ops:
  0.0 3.8 %amplitude_pieces.1 = bf16[128,72,128]{2,1,0:T(8,128)(2,1)} custom-call(s32[2,16]{1,0:T(2,128)} %bitcast.2, bf16[16,256,256]{2,1,0:T(8,128)(2,1)} %amp_ref.1), custom_call_target="tpu_custom_call" | custom-call | tf_op jit(solution)/shard_map/amplitude_pieces/pallas_call | solution.py:116
  3.9 11.6 %all-to-all-start = ((bf16[128,72,128]{2,1,0:T(8,128)(2,1)}), bf16[128,72,128]{2,1,0:T(8,128)(2,1)}, u32[]{:S(2)}, u32[]{:S(2)}) async-start(bf16[128,72,128]{2,1,0:T(8,128)(2,1)} %amplitude_pieces.1), calls=%async_computation | async-start | bytes 4718592 | tf_op jit(solution)/shard_map/all_to_all | solution.py:617
  15.8 2.5 %collective-permute-start = (bf16[2,2,2,32,128]{4,3,2,1,0:T(8,128)(2,1)S(1)}, bf16[2,2,2,32,128]{4,3,2,1,0:T(8,128)(2,1)S(1)}, u32[]{:S(2)}, u32[]{:S(2)}) collective-permute-start(bf16[2,2,2,32,128]{4,3,2,1,0:T(8,128)(2,1)S(1)} %get-tuple-element.35), channel_id=1, source_target_pairs={{0,2},{1,3},{2,0},{3,1},{4,6},{5,7},{6,4},{7,5},{8,10},{9,11},{10,... | collective-permute-start | bytes 196616 | tf_op jit(solution)/shard_map/ppermute | solution.py:223
  18.3 1.2 %collective-permute-start.1 = (bf16[2,2,2,32,128]{4,3,2,1,0:T(8,128)(2,1)S(1)}, bf16[2,2,2,32,128]{4,3,2,1,0:T(8,128)(2,1)S(1)}, u32[]{:S(2)}, u32[]{:S(2)}) collective-permute-start(bf16[2,2,2,32,128]{4,3,2,1,0:T(8,128)(2,1)S(1)} %get-tuple-element.36), channel_id=1, source_target_pairs={{0,3},{1,2},{2,1},{3,0},{4,7},{5,6},{6,5},{7,4},{8,11},{9,10},{10,... | collective-permute-start | bytes 196616 | tf_op jit(solution)/shard_map/ppermute | solution.py:223
  19.8 4.1 %collective-permute-start.3 = (bf16[2,2,2,32,128]{4,3,2,1,0:T(8,128)(2,1)S(1)}, bf16[2,2,2,32,128]{4,3,2,1,0:T(8,128)(2,1)S(1)}, u32[]{:S(2)}, u32[]{:S(2)}) collective-permute-start(bf16[2,2,2,32,128]{4,3,2,1,0:T(8,128)(2,1)S(1)} %get-tuple-element.39), channel_id=1, source_target_pairs={{0,10},{1,11},{2,8},{3,9},{4,14},{5,15},{6,12},{7,13},{8,2},{9,3},... | collective-permute-start | bytes 196616 | tf_op jit(solution)/shard_map/ppermute | solution.py:223
  23.9 2.1 %collective-permute-start.4 = (bf16[2,2,2,32,128]{4,3,2,1,0:T(8,128)(2,1)S(1)}, bf16[2,2,2,32,128]{4,3,2,1,0:T(8,128)(2,1)S(1)}, u32[]{:S(2)}, u32[]{:S(2)}) collective-permute-start(bf16[2,2,2,32,128]{4,3,2,1,0:T(8,128)(2,1)S(1)} %get-tuple-element.40), channel_id=1, source_target_pairs={{0,11},{1,10},{2,9},{3,8},{4,15},{5,14},{6,13},{7,12},{8,3},{9,2},... | collective-permute-start | bytes 196616 | tf_op jit(solution)/shard_map/ppermute | solution.py:223
  26.0 22.1 %all-to-all-done.in_ref = bf16[128,72,128]{2,1,0:T(8,128)(2,1)} async-done(((bf16[128,72,128]{2,1,0:T(8,128)(2,1)}), bf16[128,72,128]{2,1,0:T(8,128)(2,1)}, u32[]{:S(2)}, u32[]{:S(2)}) %all-to-all-start) | async-done | bytes 2359328 | tf_op jit(solution)/shard_map/all_to_all | solution.py:617
  48.1 3.6 %window_sums.1 = (bf16[128,8,128]{2,1,0:T(8,128)(2,1)}, f32[16,128]{1,0:T(8,128)}) custom-call(s32[1]{0:T(128)} %bitcast.dev_ref, bf16[128,72,128]{2,1,0:T(8,128)(2,1)} %all-to-all-done.in_ref), custom_call_target="tpu_custom_call" | custom-call | tf_op jit(solution)/shard_map/window_sums/pallas_call | solution.py:175
  51.8 6.0 %all-to-all-start.1 = ((bf16[128,8,128]{2,1,0:T(8,128)(2,1)}), bf16[128,8,128]{2,1,0:T(8,128)(2,1)S(1)}, u32[]{:S(2)}, u32[]{:S(2)}) async-start(bf16[128,8,128]{2,1,0:T(8,128)(2,1)} %get-tuple-element.50), calls=%async_computation.1 | async-start | bytes 524288 | tf_op jit(solution)/shard_map/all_to_all | solution.py:622
  58.8 1.5 %collective-permute-start.6 = (bf16[2,2,2,32,128]{4,3,2,1,0:T(8,128)(2,1)S(1)}, bf16[2,2,2,32,128]{4,3,2,1,0:T(8,128)(2,1)S(1)}, u32[]{:S(2)}, u32[]{:S(2)}) collective-permute-start(bf16[2,2,2,32,128]{4,3,2,1,0:T(8,128)(2,1)S(1)} %get-tuple-element.46), channel_id=1, source_target_pairs={{0,8},{1,9},{2,10},{3,11},{4,12},{5,13},{6,14},{7,15},{8,0},{9,1},... | collective-permute-start | bytes 196616 | tf_op jit(solution)/shard_map/ppermute | solution.py:223
  61.1 2.2 %collective-permute-done.5.refs_1_ = bf16[2,2,2,32,128]{4,3,2,1,0:T(8,128)(2,1)S(1)} collective-permute-done((bf16[2,2,2,32,128]{4,3,2,1,0:T(8,128)(2,1)S(1)}, bf16[2,2,2,32,128]{4,3,2,1,0:T(8,128)(2,1)S(1)}, u32[]{:S(2)}, u32[]{:S(2)}) %collective-permute-start.5) | collective-permute-done | bytes 65568 | tf_op jit(solution)/shard_map/ppermute | solution.py:223
  63.3 1.1 collective-permute-done.6.refs_4_
  65.7 3.0 %all-to-all-done.1.refs_10_ = bf16[128,8,128]{2,1,0:T(8,128)(2,1)S(1)} async-done(((bf16[128,8,128]{2,1,0:T(8,128)(2,1)}), bf16[128,8,128]{2,1,0:T(8,128)(2,1)S(1)}, u32[]{:S(2)}, u32[]{:S(2)}) %all-to-all-start.1) | async-done | bytes 262176 | tf_op jit(solution)/shard_map/all_to_all | solution.py:622
  68.7 2.2 %first_sweep.1 = (f32[2,256,256]{2,1,0:T(8,128)S(1)}, f32[2,2,256,256]{3,2,1,0:T(8,128)S(1)}, f32[8,256]{1,0:T(8,128)S(1)}, f32[8,256]{1,0:T(8,128)S(1)}, f32[8,...) custom-call(s32[1]{0:T(128)} %bitcast.dev_ref, ...), custom_call_target="tpu_custom_call" | custom-call | tf_op jit(solution)/shard_map/first_sweep/pallas_call | solution.py:623
  70.9 2.2 %collective-permute-start.9 = (f32[8,256]{1,0:T(8,128)S(1)}, f32[8,256]{1,0:T(8,128)S(1)}, u32[]{:S(2)}, u32[]{:S(2)}) collective-permute-start(f32[8,256]{1,0:T(8,128)S(1)} %get-tuple-element.54), channel_id=1, source_target_pairs={{0,124},{1,122},{2,126},{3,115},{4,125},{5,121},{6,127},{7,123},{8... | collective-permute-start | bytes 24584 | tf_op jit(solution)/shard_map/ppermute | solution.py:335
  73.1 3.3 %collective-permute-start.11 = (f32[8,256]{1,0:T(8,128)S(1)}, f32[8,256]{1,0:T(8,128)S(1)}, u32[]{:S(2)}, u32[]{:S(2)}) collective-permute-start(f32[8,256]{1,0:T(8,128)S(1)} %get-tuple-element.56), channel_id=1, source_target_pairs={{0,120},{1,121},{2,122},{3,123},{4,124},{5,125},{6,126},{7,127},{8... | collective-permute-start | bytes 24584 | tf_op jit(solution)/shard_map/ppermute | solution.py:335
  78.3 1.8 %collective-permute-done.11.in2 = f32[8,256]{1,0:T(8,128)S(1)} collective-permute-done((f32[8,256]{1,0:T(8,128)S(1)}, f32[8,256]{1,0:T(8,128)S(1)}, u32[]{:S(2)}, u32[]{:S(2)}) %collective-permute-start.11) | collective-permute-done | bytes 8224 | tf_op jit(solution)/shard_map/ppermute | solution.py:335
  80.0 1.2 %collective-permute-done.12.in3 = f32[8,256]{1,0:T(8,128)S(1)} collective-permute-done((f32[8,256]{1,0:T(8,128)S(1)}, f32[8,256]{1,0:T(8,128)S(1)}, u32[]{:S(2)}, u32[]{:S(2)}) %collective-permute-start.12) | collective-permute-done | bytes 8224 | tf_op jit(solution)/shard_map/ppermute | solution.py:335
  81.2 3.5 %second_sweep.1 = bf16[16,144,128]{2,1,0:T(8,128)(2,1)S(1)} custom-call(s32[1]{0:T(128)} %bitcast.dev_ref, f32[2,2,256,256]{3,2,1,0:T(8,128)S(1)} %get-tuple-element.52.in_ref, f32[8,256]{1,0:T(8,128)S(1)} %get-tuple-element.53.own_in, f32[8,256]{1,0:T(8,128)S(1)} %collective-permute-done.9.in0, f32[8,256]{1,0:T(8,128)S(1)} %collective-permute-done.10.in1, ...), custom_call_target="tpu_custom_call" | custom-call | tf_op jit(solution)/shard_map/second_sweep/pallas_call | solution.py:632
  84.8 14.8 %all_to_all.15.in_ref = bf16[16,144,128]{2,1,0:T(8,128)(2,1)S(1)} all-to-all(bf16[16,144,128]{2,1,0:T(8,128)(2,1)S(1)} %second_sweep.1), channel_id=1, replica_groups={{0,1,2,3,4,5,6,7,8,9,10,11,12,13,14,15},{16,17,18,19,20,21,22,23,24,25,..., dimensions={0} | all-to-all | bytes 1179648 | tf_op jit(solution)/shard_map/all_to_all | solution.py:641
  99.6 1.3 %collective-permute-start.15 = (bf16[16,8,128]{2,1,0:T(8,128)(2,1)S(1)}, bf16[16,8,128]{2,1,0:T(8,128)(2,1)S(1)}, u32[]{:S(2)}, u32[]{:S(2)}) collective-permute-start(bf16[16,8,128]{2,1,0:T(8,128)(2,1)S(1)} %slice.38), channel_id=1, source_target_pairs={{8,16},{9,17},{7,127},{6,126},{24,32},{25,33},{23,15},{22,14},{40,... | collective-permute-start | bytes 98312 | tf_op jit(solution)/shard_map/ppermute | solution.py:643
  100.9 2.6 %last_smoothing.1.inner_ref = f32[2,32,32,128]{3,2,1,0:T(8,128)S(1)} custom-call(s32[1]{0:T(128)} %bitcast.dev_ref, bf16[16,144,128]{2,1,0:T(8,128)(2,1)S(1)} %all_to_all.15.in_ref), custom_call_target="tpu_custom_call" | custom-call | tf_op jit(solution)/shard_map/last_smoothing/pallas_call | solution.py:647
  103.5 5.2 %collective-permute-done.15.beyond_ref = bf16[16,8,128]{2,1,0:T(8,128)(2,1)S(1)} collective-permute-done((bf16[16,8,128]{2,1,0:T(8,128)(2,1)S(1)}, bf16[16,8,128]{2,1,0:T(8,128)(2,1)S(1)}, u32[]{:S(2)}, u32[]{:S(2)}) %collective-permute-start.15) | collective-permute-done | bytes 32800 | tf_op jit(solution)/shard_map/ppermute | solution.py:643
  108.7 1.9 %last_borders.1 = f32[2,32,32,128]{3,2,1,0:T(8,128)} custom-call(s32[1]{0:T(128)} %bitcast.dev_ref, bf16[16,144,128]{2,1,0:T(8,128)(2,1)S(1)} %all_to_all.15.in_ref, bf16[16,8,128]{2,1,0:T(8,128)(2,1)S(1)} %collective-permute-done.15.beyond_ref, f32[2,32,32,128]{3,2,1,0:T(8,128)S(1)} %last_smoothing.1.inner_ref), custom_call_target="tpu_custom_call" | custom-call | tf_op jit(solution)/shard_map/last_borders/pallas_call | solution.py:655
  (40 shorter events, 5.7 us)
Async XLA Ops:
  3.8 11.7 %copy-start.3 = (f32[2,32,32,128]{3,2,1,0:T(8,128)S(1)}, f32[2,32,32,128]{3,2,1,0:T(8,128)}, u32[]{:S(2)}) copy-start(f32[2,32,32,128]{3,2,1,0:T(8,128)} %in_ref.1) | copy-start | bytes 3145732
  3.9 44.2 %all-to-all-start = ((bf16[128,72,128]{2,1,0:T(8,128)(2,1)}), bf16[128,72,128]{2,1,0:T(8,128)(2,1)}, u32[]{:S(2)}, u32[]{:S(2)}) async-start(bf16[128,72,128]{2,1,0:T(8,128)(2,1)} %amplitude_pieces.1), calls=%async_computation | async-start | bytes 4718592 | tf_op jit(solution)/shard_map/all_to_all | solution.py:617
  15.5 53.2 %copy-start = (f32[2,256,256]{2,1,0:T(8,128)S(1)}, f32[2,256,256]{2,1,0:T(8,128)}, u32[]{:S(2)}) copy-start(f32[2,256,256]{2,1,0:T(8,128)} %probe_ref.1) | copy-start | bytes 1572868
  15.5 53.2 %copy-start.1 = (bf16[512,512]{1,0:T(8,128)(2,1)S(1)}, bf16[512,512]{1,0:T(8,128)(2,1)}, u32[]{:S(2)}) copy-start(bf16[512,512]{1,0:T(8,128)(2,1)} %constant.21.refs_14_.inverse_ref) | copy-start | bytes 1572868
  15.5 53.2 %copy-start.2 = (bf16[512,512]{1,0:T(8,128)(2,1)S(1)}, bf16[512,512]{1,0:T(8,128)(2,1)}, u32[]{:S(2)}) copy-start(bf16[512,512]{1,0:T(8,128)(2,1)} %constant.20.refs_13_.forward_ref) | copy-start | bytes 1572868
  15.8 35.9 %collective-permute-start = (bf16[2,2,2,32,128]{4,3,2,1,0:T(8,128)(2,1)S(1)}, bf16[2,2,2,32,128]{4,3,2,1,0:T(8,128)(2,1)S(1)}, u32[]{:S(2)}, u32[]{:S(2)}) collective-permute-start(bf16[2,2,2,32,128]{4,3,2,1,0:T(8,128)(2,1)S(1)} %get-tuple-element.35), channel_id=1, source_target_pairs={{0,2},{1,3},{2,0},{3,1},{4,6},{5,7},{6,4},{7,5},{8,10},{9,11},{10,... | collective-permute-start | bytes 196616 | tf_op jit(solution)/shard_map/ppermute | solution.py:223
  18.3 33.4 %collective-permute-start.1 = (bf16[2,2,2,32,128]{4,3,2,1,0:T(8,128)(2,1)S(1)}, bf16[2,2,2,32,128]{4,3,2,1,0:T(8,128)(2,1)S(1)}, u32[]{:S(2)}, u32[]{:S(2)}) collective-permute-start(bf16[2,2,2,32,128]{4,3,2,1,0:T(8,128)(2,1)S(1)} %get-tuple-element.36), channel_id=1, source_target_pairs={{0,3},{1,2},{2,1},{3,0},{4,7},{5,6},{6,5},{7,4},{8,11},{9,10},{10,... | collective-permute-start | bytes 196616 | tf_op jit(solution)/shard_map/ppermute | solution.py:223
  19.5 32.3 %collective-permute-start.2 = (bf16[2,2,2,32,128]{4,3,2,1,0:T(8,128)(2,1)S(1)}, bf16[2,2,2,32,128]{4,3,2,1,0:T(8,128)(2,1)S(1)}, u32[]{:S(2)}, u32[]{:S(2)}) collective-permute-start(bf16[2,2,2,32,128]{4,3,2,1,0:T(8,128)(2,1)S(1)} %get-tuple-element.38), channel_id=1, source_target_pairs={{0,9},{1,8},{2,11},{3,10},{4,13},{5,12},{6,15},{7,14},{8,1},{9,0},... | collective-permute-start | bytes 196616 | tf_op jit(solution)/shard_map/ppermute | solution.py:223
  19.8 32.0 %collective-permute-start.3 = (bf16[2,2,2,32,128]{4,3,2,1,0:T(8,128)(2,1)S(1)}, bf16[2,2,2,32,128]{4,3,2,1,0:T(8,128)(2,1)S(1)}, u32[]{:S(2)}, u32[]{:S(2)}) collective-permute-start(bf16[2,2,2,32,128]{4,3,2,1,0:T(8,128)(2,1)S(1)} %get-tuple-element.39), channel_id=1, source_target_pairs={{0,10},{1,11},{2,8},{3,9},{4,14},{5,15},{6,12},{7,13},{8,2},{9,3},... | collective-permute-start | bytes 196616 | tf_op jit(solution)/shard_map/ppermute | solution.py:223
  23.9 27.8 %collective-permute-start.4 = (bf16[2,2,2,32,128]{4,3,2,1,0:T(8,128)(2,1)S(1)}, bf16[2,2,2,32,128]{4,3,2,1,0:T(8,128)(2,1)S(1)}, u32[]{:S(2)}, u32[]{:S(2)}) collective-permute-start(bf16[2,2,2,32,128]{4,3,2,1,0:T(8,128)(2,1)S(1)} %get-tuple-element.40), channel_id=1, source_target_pairs={{0,11},{1,10},{2,9},{3,8},{4,15},{5,14},{6,13},{7,12},{8,3},{9,2},... | collective-permute-start | bytes 196616 | tf_op jit(solution)/shard_map/ppermute | solution.py:223
  51.8 16.9 %all-to-all-start.1 = ((bf16[128,8,128]{2,1,0:T(8,128)(2,1)}), bf16[128,8,128]{2,1,0:T(8,128)(2,1)S(1)}, u32[]{:S(2)}, u32[]{:S(2)}) async-start(bf16[128,8,128]{2,1,0:T(8,128)(2,1)} %get-tuple-element.50), calls=%async_computation.1 | async-start | bytes 524288 | tf_op jit(solution)/shard_map/all_to_all | solution.py:622
  57.8 5.5 %collective-permute-start.5 = (bf16[2,2,2,32,128]{4,3,2,1,0:T(8,128)(2,1)S(1)}, bf16[2,2,2,32,128]{4,3,2,1,0:T(8,128)(2,1)S(1)}, u32[]{:S(2)}, u32[]{:S(2)}) collective-permute-start(bf16[2,2,2,32,128]{4,3,2,1,0:T(8,128)(2,1)S(1)} %get-tuple-element.43), channel_id=1, source_target_pairs={{0,1},{1,0},{2,3},{3,2},{4,5},{5,4},{6,7},{7,6},{8,9},{9,8},{10,11... | collective-permute-start | bytes 196616 | tf_op jit(solution)/shard_map/ppermute | solution.py:223
  58.8 5.5 %collective-permute-start.6 = (bf16[2,2,2,32,128]{4,3,2,1,0:T(8,128)(2,1)S(1)}, bf16[2,2,2,32,128]{4,3,2,1,0:T(8,128)(2,1)S(1)}, u32[]{:S(2)}, u32[]{:S(2)}) collective-permute-start(bf16[2,2,2,32,128]{4,3,2,1,0:T(8,128)(2,1)S(1)} %get-tuple-element.46), channel_id=1, source_target_pairs={{0,8},{1,9},{2,10},{3,11},{4,12},{5,13},{6,14},{7,15},{8,0},{9,1},... | collective-permute-start | bytes 196616 | tf_op jit(solution)/shard_map/ppermute | solution.py:223
  61.1 4.6 %collective-permute-start.7 = (bf16[6,2,2,32,128]{4,3,2,1,0:T(8,128)(2,1)S(1)}, bf16[6,2,2,32,128]{4,3,2,1,0:T(8,128)(2,1)S(1)}, u32[]{:S(2)}, u32[]{:S(2)}) collective-permute-start(bf16[6,2,2,32,128]{4,3,2,1,0:T(8,128)(2,1)S(1)} %slice_dynamic-update-slice_fusion), channel_id=1, source_target_pairs={{0,4},{1,5},{2,6},{3,7},{4,0},{5,1},{6,2},{7,3},{8,12},{9,13},{10,... | collective-permute-start | bytes 589832 | tf_op jit(solution)/shard_map/ppermute | solution.py:230
  64.4 1.3 %collective-permute-start.8 = (bf16[2,2,2,32,128]{4,3,2,1,0:T(8,128)(2,1)S(1)}, bf16[2,2,2,32,128]{4,3,2,1,0:T(8,128)(2,1)S(1)}, u32[]{:S(2)}, u32[]{:S(2)}) collective-permute-start(bf16[2,2,2,32,128]{4,3,2,1,0:T(8,128)(2,1)S(1)} %pad_maximum_fusion), channel_id=1, source_target_pairs={{0,4},{1,5},{2,6},{3,7},{4,0},{5,1},{6,2},{7,3},{8,12},{9,13},{10,... | collective-permute-start | bytes 196616 | tf_op jit(solution)/shard_map/ppermute | solution.py:230
  70.9 6.5 %collective-permute-start.9 = (f32[8,256]{1,0:T(8,128)S(1)}, f32[8,256]{1,0:T(8,128)S(1)}, u32[]{:S(2)}, u32[]{:S(2)}) collective-permute-start(f32[8,256]{1,0:T(8,128)S(1)} %get-tuple-element.54), channel_id=1, source_target_pairs={{0,124},{1,122},{2,126},{3,115},{4,125},{5,121},{6,127},{7,123},{8... | collective-permute-start | bytes 24584 | tf_op jit(solution)/shard_map/ppermute | solution.py:335
  73.1 5.2 %collective-permute-start.10 = (f32[8,256]{1,0:T(8,128)S(1)}, f32[8,256]{1,0:T(8,128)S(1)}, u32[]{:S(2)}, u32[]{:S(2)}) collective-permute-start(f32[8,256]{1,0:T(8,128)S(1)} %get-tuple-element.55), channel_id=1, source_target_pairs={{0,16},{1,29},{2,25},{3,31},{4,24},{5,28},{6,26},{7,30},{8,20},{9,... | collective-permute-start | bytes 24584 | tf_op jit(solution)/shard_map/ppermute | solution.py:335
  73.1 7.0 %collective-permute-start.11 = (f32[8,256]{1,0:T(8,128)S(1)}, f32[8,256]{1,0:T(8,128)S(1)}, u32[]{:S(2)}, u32[]{:S(2)}) collective-permute-start(f32[8,256]{1,0:T(8,128)S(1)} %get-tuple-element.56), channel_id=1, source_target_pairs={{0,120},{1,121},{2,122},{3,123},{4,124},{5,125},{6,126},{7,127},{8... | collective-permute-start | bytes 24584 | tf_op jit(solution)/shard_map/ppermute | solution.py:335
  76.4 4.9 %collective-permute-start.12 = (f32[8,256]{1,0:T(8,128)S(1)}, f32[8,256]{1,0:T(8,128)S(1)}, u32[]{:S(2)}, u32[]{:S(2)}) collective-permute-start(f32[8,256]{1,0:T(8,128)S(1)} %get-tuple-element.57), channel_id=1, source_target_pairs={{0,24},{1,25},{2,26},{3,27},{4,28},{5,29},{6,30},{7,31},{8,16},{9,... | collective-permute-start | bytes 24584 | tf_op jit(solution)/shard_map/ppermute | solution.py:335
  76.4 4.9 %collective-permute-start.13 = (f32[8,256]{1,0:T(8,128)S(1)}, f32[8,256]{1,0:T(8,128)S(1)}, u32[]{:S(2)}, u32[]{:S(2)}) collective-permute-start(f32[8,256]{1,0:T(8,128)S(1)} %get-tuple-element.58), channel_id=1, source_target_pairs={{0,8},{1,2},{2,1},{3,11},{4,5},{5,4},{6,7},{7,6},{8,0},{9,10},{10,... | collective-permute-start | bytes 24584 | tf_op jit(solution)/shard_map/ppermute | solution.py:335
  77.3 3.9 %collective-permute-start.14 = (f32[8,256]{1,0:T(8,128)S(1)}, f32[8,256]{1,0:T(8,128)S(1)}, u32[]{:S(2)}, u32[]{:S(2)}) collective-permute-start(f32[8,256]{1,0:T(8,128)S(1)} %get-tuple-element.59), channel_id=1, source_target_pairs={{0,4},{1,5},{2,6},{3,7},{4,0},{5,1},{6,2},{7,3},{8,12},{9,13},{10,... | collective-permute-start | bytes 24584 | tf_op jit(solution)/shard_map/ppermute | solution.py:335
  99.6 9.1 %collective-permute-start.15 = (bf16[16,8,128]{2,1,0:T(8,128)(2,1)S(1)}, bf16[16,8,128]{2,1,0:T(8,128)(2,1)S(1)}, u32[]{:S(2)}, u32[]{:S(2)}) collective-permute-start(bf16[16,8,128]{2,1,0:T(8,128)(2,1)S(1)} %slice.38), channel_id=1, source_target_pairs={{8,16},{9,17},{7,127},{6,126},{24,32},{25,33},{23,15},{22,14},{40,... | collective-permute-start | bytes 98312 | tf_op jit(solution)/shard_map/ppermute | solution.py:643

commit v6 on v5

--- a/solution.py
+++ b/solution.py
@@ -314,11 +314,11 @@
     group, spot, _ = window_rows(dev)
     odd_group, odd_spot = (group & 1) == 1, (spot & 1) == 1
     for ref, odd, even_edge, odd_edge in (
-        (edge_refs[0], odd_group, behind, ahead),
-        (edge_refs[1], odd_group, ahead, behind),
-        (edge_refs[2], odd_group, down, up),
+        (edge_refs[0], odd_group, down, up),
+        (edge_refs[1], odd_group, behind, ahead),
+        (edge_refs[2], odd_spot, ahead, behind),
         (edge_refs[3], odd_group, up, down),
-        (edge_refs[4], odd_spot, ahead, behind),
+        (edge_refs[4], odd_group, ahead, behind),
         (edge_refs[5], odd_spot, behind, ahead),
     ):
         ref[...] = jnp.where(odd, odd_edge, even_edge)
@@ -327,10 +327,8 @@
 def exchange_edges(edges):
     moves = []
     for odd in (1, 0):
+        moves.append(lambda g, q, odd=odd: (g + 1 if g % 2 == odd else g - 1, q))
         moves.append(lambda g, q, odd=odd: (g + 1, q - 1) if g % 2 == odd else (g - 1, q + 1))
-    for odd in (1, 0):
-        moves.append(lambda g, q, odd=odd: (g + 1 if g % 2 == odd else g - 1, q))
-    for odd in (1, 0):
         moves.append(lambda g, q, odd=odd: (g, q + 1 if q % 2 == odd else q - 1))
     return [lax.ppermute(edge, ALL, partners(move)) for edge, move in zip(edges, moves)]
 
@@ -377,7 +375,7 @@
 def smooth(dev, relaxed_ref, own_ref, halo_refs):
     group, spot, starts = window_rows(dev)
     odd_group, odd_spot = (group & 1) == 1, (spot & 1) == 1
-    corner1, corner0, above1, above0, beside1, beside0 = [ref[...] for ref in halo_refs]
+    above1, corner1, beside1, above0, corner0, beside0 = [ref[...] for ref in halo_refs]
     extra = iota((8, 256), 0) >= 6
     up_own = jnp.where(extra, jnp.where(odd_spot, beside1, beside0), own_ref[...])
     down_own = jnp.where(extra, jnp.where(odd_spot, beside0, beside1), pltpu.roll(own_ref[...], 6, 0))

time: 111 us -> 113 us (1.018)
  starting transfers between devices: 38.2 us -> 41.3 us
  waiting for transfers between devices: 37.8 us -> 35.9 us
    ppermute x6, starting transfers between devices: 6.61 us -> 9.62 us  [exchange_edges(): lax.ppermute(edge, ALL, partners(move))]
    ppermute x6, waiting for transfers between devices: 3.74 us -> 1.8 us  [exchange_edges(): lax.ppermute(edge, ALL, partners(move))]
  transfers between devices with their start and end apart: 18 -> 18, of which waited for: 9 -> 8; matrix products, arithmetic and copies ran while one was open for 1% -> 1% of each run, Pallas kernels for 6% -> 6%
where the time goes in v6:
time: 113 us; the launch traced here: 112 us
  starting transfers between devices  41.3 us (37%)
  waiting for transfers between devices  35.9 us (32%)
  Pallas kernels  18 us (16%)
  blocking collectives  15.4 us (14%)
  local copies, waits for them, and re-layouts  1.49 us (1%)
    all_to_all x1, waiting for transfers between devices, shards(): lax.all_to_all(amplitude_pieces(frame_pos, amplitudes), ALL, 0, 0, tiled=...  22.1 us
    all_to_all x1, blocking collectives, shards(): lax.all_to_all(tiles, ALL, 0, 0, axis_index_groups=GROUPS, tiled=True)  15.4 us
    ppermute x7, starting transfers between devices, across_chips(): lax.ppermute(block, ALL, [(d, d ^ 8 * (t // 4) + t % 4) for d in range(12...  12.7 us
    all_to_all x1, starting transfers between devices, shards(): lax.all_to_all(amplitude_pieces(frame_pos, amplitudes), ALL, 0, 0, tiled=...  11.6 us
    ppermute x6, starting transfers between devices, exchange_edges(): lax.ppermute(edge, ALL, partners(move))  9.62 us
    all_to_all x1, starting transfers between devices, shards(): sums = lax.all_to_all(sums, ALL, 0, 0, tiled=True)  6 us
    ppermute x1, waiting for transfers between devices, shards(): lax.ppermute(tiles[:, 136:], ALL, [(16 * g + k, (16 * g + to) % 128) for...  5.19 us
    pallas_call x1, Pallas kernels, amplitude_pieces(): pl.pallas_call(pieces_kernel, in_specs=[BLOCK, ANYWHERE], out_specs=ANYWH...  3.83 us
  transfers between devices with their start and end apart: 18, of which 8 were waited for; matrix products, arithmetic and copies ran while one was open for 1% of the time, Pallas kernels for 6%

profile of v6, /device:TPU:0, one launch (start us, length us, event | category | flops | bytes accessed | tf_op | source)
XLA Modules:
  0.0 112.2 jit_solution(16170885104019951834)
XLA Ops:
  0.0 3.8 %amplitude_pieces.1 = bf16[128,72,128]{2,1,0:T(8,128)(2,1)} custom-call(s32[2,16]{1,0:T(2,128)} %bitcast.2, bf16[16,256,256]{2,1,0:T(8,128)(2,1)} %amp_ref.1), custom_call_target="tpu_custom_call" | custom-call | tf_op jit(solution)/shard_map/amplitude_pieces/pallas_call | solution.py:116
  3.9 11.6 %all-to-all-start = ((bf16[128,72,128]{2,1,0:T(8,128)(2,1)}), bf16[128,72,128]{2,1,0:T(8,128)(2,1)}, u32[]{:S(2)}, u32[]{:S(2)}) async-start(bf16[128,72,128]{2,1,0:T(8,128)(2,1)} %amplitude_pieces.1), calls=%async_computation | async-start | bytes 4718592 | tf_op jit(solution)/shard_map/all_to_all | solution.py:615
  15.8 2.5 %collective-permute-start = (bf16[2,2,2,32,128]{4,3,2,1,0:T(8,128)(2,1)S(1)}, bf16[2,2,2,32,128]{4,3,2,1,0:T(8,128)(2,1)S(1)}, u32[]{:S(2)}, u32[]{:S(2)}) collective-permute-start(bf16[2,2,2,32,128]{4,3,2,1,0:T(8,128)(2,1)S(1)} %get-tuple-element.35), channel_id=1, source_target_pairs={{0,2},{1,3},{2,0},{3,1},{4,6},{5,7},{6,4},{7,5},{8,10},{9,11},{10,... | collective-permute-start | bytes 196616 | tf_op jit(solution)/shard_map/ppermute | solution.py:223
  18.3 1.2 %collective-permute-start.1 = (bf16[2,2,2,32,128]{4,3,2,1,0:T(8,128)(2,1)S(1)}, bf16[2,2,2,32,128]{4,3,2,1,0:T(8,128)(2,1)S(1)}, u32[]{:S(2)}, u32[]{:S(2)}) collective-permute-start(bf16[2,2,2,32,128]{4,3,2,1,0:T(8,128)(2,1)S(1)} %get-tuple-element.36), channel_id=1, source_target_pairs={{0,3},{1,2},{2,1},{3,0},{4,7},{5,6},{6,5},{7,4},{8,11},{9,10},{10,... | collective-permute-start | bytes 196616 | tf_op jit(solution)/shard_map/ppermute | solution.py:223
  19.8 4.1 %collective-permute-start.3 = (bf16[2,2,2,32,128]{4,3,2,1,0:T(8,128)(2,1)S(1)}, bf16[2,2,2,32,128]{4,3,2,1,0:T(8,128)(2,1)S(1)}, u32[]{:S(2)}, u32[]{:S(2)}) collective-permute-start(bf16[2,2,2,32,128]{4,3,2,1,0:T(8,128)(2,1)S(1)} %get-tuple-element.39), channel_id=1, source_target_pairs={{0,10},{1,11},{2,8},{3,9},{4,14},{5,15},{6,12},{7,13},{8,2},{9,3},... | collective-permute-start | bytes 196616 | tf_op jit(solution)/shard_map/ppermute | solution.py:223
  23.9 2.1 %collective-permute-start.4 = (bf16[2,2,2,32,128]{4,3,2,1,0:T(8,128)(2,1)S(1)}, bf16[2,2,2,32,128]{4,3,2,1,0:T(8,128)(2,1)S(1)}, u32[]{:S(2)}, u32[]{:S(2)}) collective-permute-start(bf16[2,2,2,32,128]{4,3,2,1,0:T(8,128)(2,1)S(1)} %get-tuple-element.40), channel_id=1, source_target_pairs={{0,11},{1,10},{2,9},{3,8},{4,15},{5,14},{6,13},{7,12},{8,3},{9,2},... | collective-permute-start | bytes 196616 | tf_op jit(solution)/shard_map/ppermute | solution.py:223
  26.0 22.1 %all-to-all-done.in_ref = bf16[128,72,128]{2,1,0:T(8,128)(2,1)} async-done(((bf16[128,72,128]{2,1,0:T(8,128)(2,1)}), bf16[128,72,128]{2,1,0:T(8,128)(2,1)}, u32[]{:S(2)}, u32[]{:S(2)}) %all-to-all-start) | async-done | bytes 2359328 | tf_op jit(solution)/shard_map/all_to_all | solution.py:615
  48.1 3.6 %window_sums.1 = (bf16[128,8,128]{2,1,0:T(8,128)(2,1)}, f32[16,128]{1,0:T(8,128)}) custom-call(s32[1]{0:T(128)} %bitcast.dev_ref, bf16[128,72,128]{2,1,0:T(8,128)(2,1)} %all-to-all-done.in_ref), custom_call_target="tpu_custom_call" | custom-call | tf_op jit(solution)/shard_map/window_sums/pallas_call | solution.py:175
  51.8 6.0 %all-to-all-start.1 = ((bf16[128,8,128]{2,1,0:T(8,128)(2,1)}), bf16[128,8,128]{2,1,0:T(8,128)(2,1)S(1)}, u32[]{:S(2)}, u32[]{:S(2)}) async-start(bf16[128,8,128]{2,1,0:T(8,128)(2,1)} %get-tuple-element.50), calls=%async_computation.1 | async-start | bytes 524288 | tf_op jit(solution)/shard_map/all_to_all | solution.py:620
  58.8 1.5 %collective-permute-start.6 = (bf16[2,2,2,32,128]{4,3,2,1,0:T(8,128)(2,1)S(1)}, bf16[2,2,2,32,128]{4,3,2,1,0:T(8,128)(2,1)S(1)}, u32[]{:S(2)}, u32[]{:S(2)}) collective-permute-start(bf16[2,2,2,32,128]{4,3,2,1,0:T(8,128)(2,1)S(1)} %get-tuple-element.46), channel_id=1, source_target_pairs={{0,8},{1,9},{2,10},{3,11},{4,12},{5,13},{6,14},{7,15},{8,0},{9,1},... | collective-permute-start | bytes 196616 | tf_op jit(solution)/shard_map/ppermute | solution.py:223
  61.1 2.2 %collective-permute-done.5.refs_1_ = bf16[2,2,2,32,128]{4,3,2,1,0:T(8,128)(2,1)S(1)} collective-permute-done((bf16[2,2,2,32,128]{4,3,2,1,0:T(8,128)(2,1)S(1)}, bf16[2,2,2,32,128]{4,3,2,1,0:T(8,128)(2,1)S(1)}, u32[]{:S(2)}, u32[]{:S(2)}) %collective-permute-start.5) | collective-permute-done | bytes 65568 | tf_op jit(solution)/shard_map/ppermute | solution.py:223
  65.7 3.0 %all-to-all-done.1.refs_10_ = bf16[128,8,128]{2,1,0:T(8,128)(2,1)S(1)} async-done(((bf16[128,8,128]{2,1,0:T(8,128)(2,1)}), bf16[128,8,128]{2,1,0:T(8,128)(2,1)S(1)}, u32[]{:S(2)}, u32[]{:S(2)}) %all-to-all-start.1) | async-done | bytes 262176 | tf_op jit(solution)/shard_map/all_to_all | solution.py:620
  68.7 2.2 %first_sweep.1 = (f32[2,256,256]{2,1,0:T(8,128)S(1)}, f32[2,2,256,256]{3,2,1,0:T(8,128)S(1)}, f32[8,256]{1,0:T(8,128)S(1)}, f32[8,256]{1,0:T(8,128)S(1)}, f32[8,...) custom-call(s32[1]{0:T(128)} %bitcast.dev_ref, ...), custom_call_target="tpu_custom_call" | custom-call | tf_op jit(solution)/shard_map/first_sweep/pallas_call | solution.py:621
  70.9 2.4 %collective-permute-start.9 = (f32[8,256]{1,0:T(8,128)S(1)}, f32[8,256]{1,0:T(8,128)S(1)}, u32[]{:S(2)}, u32[]{:S(2)}) collective-permute-start(f32[8,256]{1,0:T(8,128)S(1)} %get-tuple-element.54), channel_id=1, source_target_pairs={{0,120},{1,121},{2,122},{3,123},{4,124},{5,125},{6,126},{7,127},{8... | collective-permute-start | bytes 24584 | tf_op jit(solution)/shard_map/ppermute | solution.py:333
  73.3 2.5 %collective-permute-start.10 = (f32[8,256]{1,0:T(8,128)S(1)}, f32[8,256]{1,0:T(8,128)S(1)}, u32[]{:S(2)}, u32[]{:S(2)}) collective-permute-start(f32[8,256]{1,0:T(8,128)S(1)} %get-tuple-element.55), channel_id=1, source_target_pairs={{0,124},{1,122},{2,126},{3,115},{4,125},{5,121},{6,127},{7,123},{8... | collective-permute-start | bytes 24584 | tf_op jit(solution)/shard_map/ppermute | solution.py:333
  75.8 1.4 %collective-permute-start.11 = (f32[8,256]{1,0:T(8,128)S(1)}, f32[8,256]{1,0:T(8,128)S(1)}, u32[]{:S(2)}, u32[]{:S(2)}) collective-permute-start(f32[8,256]{1,0:T(8,128)S(1)} %get-tuple-element.56), channel_id=1, source_target_pairs={{0,8},{1,2},{2,1},{3,11},{4,5},{5,4},{6,7},{7,6},{8,0},{9,10},{10,... | collective-permute-start | bytes 24584 | tf_op jit(solution)/shard_map/ppermute | solution.py:333
  77.2 2.7 %collective-permute-start.13 = (f32[8,256]{1,0:T(8,128)S(1)}, f32[8,256]{1,0:T(8,128)S(1)}, u32[]{:S(2)}, u32[]{:S(2)}) collective-permute-start(f32[8,256]{1,0:T(8,128)S(1)} %get-tuple-element.58), channel_id=1, source_target_pairs={{0,16},{1,29},{2,25},{3,31},{4,24},{5,28},{6,26},{7,30},{8,20},{9,... | collective-permute-start | bytes 24584 | tf_op jit(solution)/shard_map/ppermute | solution.py:333
  80.5 1.5 %collective-permute-done.12.in3 = f32[8,256]{1,0:T(8,128)S(1)} collective-permute-done((f32[8,256]{1,0:T(8,128)S(1)}, f32[8,256]{1,0:T(8,128)S(1)}, u32[]{:S(2)}, u32[]{:S(2)}) %collective-permute-start.12) | collective-permute-done | bytes 8224 | tf_op jit(solution)/shard_map/ppermute | solution.py:333
  82.3 3.5 %second_sweep.1 = bf16[16,144,128]{2,1,0:T(8,128)(2,1)S(1)} custom-call(s32[1]{0:T(128)} %bitcast.dev_ref, f32[2,2,256,256]{3,2,1,0:T(8,128)S(1)} %get-tuple-element.52.in_ref, f32[8,256]{1,0:T(8,128)S(1)} %get-tuple-element.53.own_in, f32[8,256]{1,0:T(8,128)S(1)} %collective-permute-done.9.in0, f32[8,256]{1,0:T(8,128)S(1)} %collective-permute-done.10.in1, ...), custom_call_target="tpu_custom_call" | custom-call | tf_op jit(solution)/shard_map/second_sweep/pallas_call | solution.py:630
  85.9 15.4 %all_to_all.15.in_ref = bf16[16,144,128]{2,1,0:T(8,128)(2,1)S(1)} all-to-all(bf16[16,144,128]{2,1,0:T(8,128)(2,1)S(1)} %second_sweep.1), channel_id=1, replica_groups={{0,1,2,3,4,5,6,7,8,9,10,11,12,13,14,15},{16,17,18,19,20,21,22,23,24,25,..., dimensions={0} | all-to-all | bytes 1179648 | tf_op jit(solution)/shard_map/all_to_all | solution.py:639
  101.2 1.3 %collective-permute-start.15 = (bf16[16,8,128]{2,1,0:T(8,128)(2,1)S(1)}, bf16[16,8,128]{2,1,0:T(8,128)(2,1)S(1)}, u32[]{:S(2)}, u32[]{:S(2)}) collective-permute-start(bf16[16,8,128]{2,1,0:T(8,128)(2,1)S(1)} %slice.38), channel_id=1, source_target_pairs={{8,16},{9,17},{7,127},{6,126},{24,32},{25,33},{23,15},{22,14},{40,... | collective-permute-start | bytes 98312 | tf_op jit(solution)/shard_map/ppermute | solution.py:641
  102.5 2.6 %last_smoothing.1.inner_ref = f32[2,32,32,128]{3,2,1,0:T(8,128)S(1)} custom-call(s32[1]{0:T(128)} %bitcast.dev_ref, bf16[16,144,128]{2,1,0:T(8,128)(2,1)S(1)} %all_to_all.15.in_ref), custom_call_target="tpu_custom_call" | custom-call | tf_op jit(solution)/shard_map/last_smoothing/pallas_call | solution.py:645
  105.2 5.2 %collective-permute-done.15.beyond_ref = bf16[16,8,128]{2,1,0:T(8,128)(2,1)S(1)} collective-permute-done((bf16[16,8,128]{2,1,0:T(8,128)(2,1)S(1)}, bf16[16,8,128]{2,1,0:T(8,128)(2,1)S(1)}, u32[]{:S(2)}, u32[]{:S(2)}) %collective-permute-start.15) | collective-permute-done | bytes 32800 | tf_op jit(solution)/shard_map/ppermute | solution.py:641
  110.4 1.9 %last_borders.1 = f32[2,32,32,128]{3,2,1,0:T(8,128)} custom-call(s32[1]{0:T(128)} %bitcast.dev_ref, bf16[16,144,128]{2,1,0:T(8,128)(2,1)S(1)} %all_to_all.15.in_ref, bf16[16,8,128]{2,1,0:T(8,128)(2,1)S(1)} %collective-permute-done.15.beyond_ref, f32[2,32,32,128]{3,2,1,0:T(8,128)S(1)} %last_smoothing.1.inner_ref), custom_call_target="tpu_custom_call" | custom-call | tf_op jit(solution)/shard_map/last_borders/pallas_call | solution.py:653
  (40 shorter events, 5.8 us)
Async XLA Ops:
  3.8 11.7 %copy-start.3 = (f32[2,32,32,128]{3,2,1,0:T(8,128)S(1)}, f32[2,32,32,128]{3,2,1,0:T(8,128)}, u32[]{:S(2)}) copy-start(f32[2,32,32,128]{3,2,1,0:T(8,128)} %in_ref.1) | copy-start | bytes 3145732
  3.9 44.2 %all-to-all-start = ((bf16[128,72,128]{2,1,0:T(8,128)(2,1)}), bf16[128,72,128]{2,1,0:T(8,128)(2,1)}, u32[]{:S(2)}, u32[]{:S(2)}) async-start(bf16[128,72,128]{2,1,0:T(8,128)(2,1)} %amplitude_pieces.1), calls=%async_computation | async-start | bytes 4718592 | tf_op jit(solution)/shard_map/all_to_all | solution.py:615
  15.5 53.2 %copy-start = (f32[2,256,256]{2,1,0:T(8,128)S(1)}, f32[2,256,256]{2,1,0:T(8,128)}, u32[]{:S(2)}) copy-start(f32[2,256,256]{2,1,0:T(8,128)} %probe_ref.1) | copy-start | bytes 1572868
  15.5 53.2 %copy-start.1 = (bf16[512,512]{1,0:T(8,128)(2,1)S(1)}, bf16[512,512]{1,0:T(8,128)(2,1)}, u32[]{:S(2)}) copy-start(bf16[512,512]{1,0:T(8,128)(2,1)} %constant.21.refs_14_.inverse_ref) | copy-start | bytes 1572868
  15.5 53.2 %copy-start.2 = (bf16[512,512]{1,0:T(8,128)(2,1)S(1)}, bf16[512,512]{1,0:T(8,128)(2,1)}, u32[]{:S(2)}) copy-start(bf16[512,512]{1,0:T(8,128)(2,1)} %constant.20.refs_13_.forward_ref) | copy-start | bytes 1572868
  15.8 35.9 %collective-permute-start = (bf16[2,2,2,32,128]{4,3,2,1,0:T(8,128)(2,1)S(1)}, bf16[2,2,2,32,128]{4,3,2,1,0:T(8,128)(2,1)S(1)}, u32[]{:S(2)}, u32[]{:S(2)}) collective-permute-start(bf16[2,2,2,32,128]{4,3,2,1,0:T(8,128)(2,1)S(1)} %get-tuple-element.35), channel_id=1, source_target_pairs={{0,2},{1,3},{2,0},{3,1},{4,6},{5,7},{6,4},{7,5},{8,10},{9,11},{10,... | collective-permute-start | bytes 196616 | tf_op jit(solution)/shard_map/ppermute | solution.py:223
  18.3 33.4 %collective-permute-start.1 = (bf16[2,2,2,32,128]{4,3,2,1,0:T(8,128)(2,1)S(1)}, bf16[2,2,2,32,128]{4,3,2,1,0:T(8,128)(2,1)S(1)}, u32[]{:S(2)}, u32[]{:S(2)}) collective-permute-start(bf16[2,2,2,32,128]{4,3,2,1,0:T(8,128)(2,1)S(1)} %get-tuple-element.36), channel_id=1, source_target_pairs={{0,3},{1,2},{2,1},{3,0},{4,7},{5,6},{6,5},{7,4},{8,11},{9,10},{10,... | collective-permute-start | bytes 196616 | tf_op jit(solution)/shard_map/ppermute | solution.py:223
  19.5 32.3 %collective-permute-start.2 = (bf16[2,2,2,32,128]{4,3,2,1,0:T(8,128)(2,1)S(1)}, bf16[2,2,2,32,128]{4,3,2,1,0:T(8,128)(2,1)S(1)}, u32[]{:S(2)}, u32[]{:S(2)}) collective-permute-start(bf16[2,2,2,32,128]{4,3,2,1,0:T(8,128)(2,1)S(1)} %get-tuple-element.38), channel_id=1, source_target_pairs={{0,9},{1,8},{2,11},{3,10},{4,13},{5,12},{6,15},{7,14},{8,1},{9,0},... | collective-permute-start | bytes 196616 | tf_op jit(solution)/shard_map/ppermute | solution.py:223
  19.8 32.0 %collective-permute-start.3 = (bf16[2,2,2,32,128]{4,3,2,1,0:T(8,128)(2,1)S(1)}, bf16[2,2,2,32,128]{4,3,2,1,0:T(8,128)(2,1)S(1)}, u32[]{:S(2)}, u32[]{:S(2)}) collective-permute-start(bf16[2,2,2,32,128]{4,3,2,1,0:T(8,128)(2,1)S(1)} %get-tuple-element.39), channel_id=1, source_target_pairs={{0,10},{1,11},{2,8},{3,9},{4,14},{5,15},{6,12},{7,13},{8,2},{9,3},... | collective-permute-start | bytes 196616 | tf_op jit(solution)/shard_map/ppermute | solution.py:223
  23.9 27.8 %collective-permute-start.4 = (bf16[2,2,2,32,128]{4,3,2,1,0:T(8,128)(2,1)S(1)}, bf16[2,2,2,32,128]{4,3,2,1,0:T(8,128)(2,1)S(1)}, u32[]{:S(2)}, u32[]{:S(2)}) collective-permute-start(bf16[2,2,2,32,128]{4,3,2,1,0:T(8,128)(2,1)S(1)} %get-tuple-element.40), channel_id=1, source_target_pairs={{0,11},{1,10},{2,9},{3,8},{4,15},{5,14},{6,13},{7,12},{8,3},{9,2},... | collective-permute-start | bytes 196616 | tf_op jit(solution)/shard_map/ppermute | solution.py:223
  51.8 16.9 %all-to-all-start.1 = ((bf16[128,8,128]{2,1,0:T(8,128)(2,1)}), bf16[128,8,128]{2,1,0:T(8,128)(2,1)S(1)}, u32[]{:S(2)}, u32[]{:S(2)}) async-start(bf16[128,8,128]{2,1,0:T(8,128)(2,1)} %get-tuple-element.50), calls=%async_computation.1 | async-start | bytes 524288 | tf_op jit(solution)/shard_map/all_to_all | solution.py:620
  57.8 5.5 %collective-permute-start.5 = (bf16[2,2,2,32,128]{4,3,2,1,0:T(8,128)(2,1)S(1)}, bf16[2,2,2,32,128]{4,3,2,1,0:T(8,128)(2,1)S(1)}, u32[]{:S(2)}, u32[]{:S(2)}) collective-permute-start(bf16[2,2,2,32,128]{4,3,2,1,0:T(8,128)(2,1)S(1)} %get-tuple-element.43), channel_id=1, source_target_pairs={{0,1},{1,0},{2,3},{3,2},{4,5},{5,4},{6,7},{7,6},{8,9},{9,8},{10,11... | collective-permute-start | bytes 196616 | tf_op jit(solution)/shard_map/ppermute | solution.py:223
  58.8 5.5 %collective-permute-start.6 = (bf16[2,2,2,32,128]{4,3,2,1,0:T(8,128)(2,1)S(1)}, bf16[2,2,2,32,128]{4,3,2,1,0:T(8,128)(2,1)S(1)}, u32[]{:S(2)}, u32[]{:S(2)}) collective-permute-start(bf16[2,2,2,32,128]{4,3,2,1,0:T(8,128)(2,1)S(1)} %get-tuple-element.46), channel_id=1, source_target_pairs={{0,8},{1,9},{2,10},{3,11},{4,12},{5,13},{6,14},{7,15},{8,0},{9,1},... | collective-permute-start | bytes 196616 | tf_op jit(solution)/shard_map/ppermute | solution.py:223
  61.1 4.6 %collective-permute-start.7 = (bf16[6,2,2,32,128]{4,3,2,1,0:T(8,128)(2,1)S(1)}, bf16[6,2,2,32,128]{4,3,2,1,0:T(8,128)(2,1)S(1)}, u32[]{:S(2)}, u32[]{:S(2)}) collective-permute-start(bf16[6,2,2,32,128]{4,3,2,1,0:T(8,128)(2,1)S(1)} %slice_dynamic-update-slice_fusion), channel_id=1, source_target_pairs={{0,4},{1,5},{2,6},{3,7},{4,0},{5,1},{6,2},{7,3},{8,12},{9,13},{10,... | collective-permute-start | bytes 589832 | tf_op jit(solution)/shard_map/ppermute | solution.py:230
  64.4 1.3 %collective-permute-start.8 = (bf16[2,2,2,32,128]{4,3,2,1,0:T(8,128)(2,1)S(1)}, bf16[2,2,2,32,128]{4,3,2,1,0:T(8,128)(2,1)S(1)}, u32[]{:S(2)}, u32[]{:S(2)}) collective-permute-start(bf16[2,2,2,32,128]{4,3,2,1,0:T(8,128)(2,1)S(1)} %pad_maximum_fusion), channel_id=1, source_target_pairs={{0,4},{1,5},{2,6},{3,7},{4,0},{5,1},{6,2},{7,3},{8,12},{9,13},{10,... | collective-permute-start | bytes 196616 | tf_op jit(solution)/shard_map/ppermute | solution.py:230
  70.9 9.0 %collective-permute-start.9 = (f32[8,256]{1,0:T(8,128)S(1)}, f32[8,256]{1,0:T(8,128)S(1)}, u32[]{:S(2)}, u32[]{:S(2)}) collective-permute-start(f32[8,256]{1,0:T(8,128)S(1)} %get-tuple-element.54), channel_id=1, source_target_pairs={{0,120},{1,121},{2,122},{3,123},{4,124},{5,125},{6,126},{7,127},{8... | collective-permute-start | bytes 24584 | tf_op jit(solution)/shard_map/ppermute | solution.py:333
  73.3 7.2 %collective-permute-start.10 = (f32[8,256]{1,0:T(8,128)S(1)}, f32[8,256]{1,0:T(8,128)S(1)}, u32[]{:S(2)}, u32[]{:S(2)}) collective-permute-start(f32[8,256]{1,0:T(8,128)S(1)} %get-tuple-element.55), channel_id=1, source_target_pairs={{0,124},{1,122},{2,126},{3,115},{4,125},{5,121},{6,127},{7,123},{8... | collective-permute-start | bytes 24584 | tf_op jit(solution)/shard_map/ppermute | solution.py:333
  75.8 4.8 %collective-permute-start.11 = (f32[8,256]{1,0:T(8,128)S(1)}, f32[8,256]{1,0:T(8,128)S(1)}, u32[]{:S(2)}, u32[]{:S(2)}) collective-permute-start(f32[8,256]{1,0:T(8,128)S(1)} %get-tuple-element.56), channel_id=1, source_target_pairs={{0,8},{1,2},{2,1},{3,11},{4,5},{5,4},{6,7},{7,6},{8,0},{9,10},{10,... | collective-permute-start | bytes 24584 | tf_op jit(solution)/shard_map/ppermute | solution.py:333
  77.2 4.9 %collective-permute-start.12 = (f32[8,256]{1,0:T(8,128)S(1)}, f32[8,256]{1,0:T(8,128)S(1)}, u32[]{:S(2)}, u32[]{:S(2)}) collective-permute-start(f32[8,256]{1,0:T(8,128)S(1)} %get-tuple-element.57), channel_id=1, source_target_pairs={{0,24},{1,25},{2,26},{3,27},{4,28},{5,29},{6,30},{7,31},{8,16},{9,... | collective-permute-start | bytes 24584 | tf_op jit(solution)/shard_map/ppermute | solution.py:333
  77.2 5.2 %collective-permute-start.13 = (f32[8,256]{1,0:T(8,128)S(1)}, f32[8,256]{1,0:T(8,128)S(1)}, u32[]{:S(2)}, u32[]{:S(2)}) collective-permute-start(f32[8,256]{1,0:T(8,128)S(1)} %get-tuple-element.58), channel_id=1, source_target_pairs={{0,16},{1,29},{2,25},{3,31},{4,24},{5,28},{6,26},{7,30},{8,20},{9,... | collective-permute-start | bytes 24584 | tf_op jit(solution)/shard_map/ppermute | solution.py:333
  79.9 2.5 %collective-permute-start.14 = (f32[8,256]{1,0:T(8,128)S(1)}, f32[8,256]{1,0:T(8,128)S(1)}, u32[]{:S(2)}, u32[]{:S(2)}) collective-permute-start(f32[8,256]{1,0:T(8,128)S(1)} %get-tuple-element.59), channel_id=1, source_target_pairs={{0,4},{1,5},{2,6},{3,7},{4,0},{5,1},{6,2},{7,3},{8,12},{9,13},{10,... | collective-permute-start | bytes 24584 | tf_op jit(solution)/shard_map/ppermute | solution.py:333
  101.2 9.1 %collective-permute-start.15 = (bf16[16,8,128]{2,1,0:T(8,128)(2,1)S(1)}, bf16[16,8,128]{2,1,0:T(8,128)(2,1)S(1)}, u32[]{:S(2)}, u32[]{:S(2)}) collective-permute-start(bf16[16,8,128]{2,1,0:T(8,128)(2,1)S(1)} %slice.38), channel_id=1, source_target_pairs={{8,16},{9,17},{7,127},{6,126},{24,32},{25,33},{23,15},{22,14},{40,... | collective-permute-start | bytes 98312 | tf_op jit(solution)/shard_map/ppermute | solution.py:641

commit v7 on v5

--- a/solution.py
+++ b/solution.py
@@ -315,8 +315,8 @@
     odd_group, odd_spot = (group & 1) == 1, (spot & 1) == 1
     for ref, odd, even_edge, odd_edge in (
         (edge_refs[0], odd_group, behind, ahead),
-        (edge_refs[1], odd_group, ahead, behind),
-        (edge_refs[2], odd_group, down, up),
+        (edge_refs[1], odd_group, down, up),
+        (edge_refs[2], odd_group, ahead, behind),
         (edge_refs[3], odd_group, up, down),
         (edge_refs[4], odd_spot, ahead, behind),
         (edge_refs[5], odd_spot, behind, ahead),
@@ -328,7 +328,6 @@
     moves = []
     for odd in (1, 0):
         moves.append(lambda g, q, odd=odd: (g + 1, q - 1) if g % 2 == odd else (g - 1, q + 1))
-    for odd in (1, 0):
         moves.append(lambda g, q, odd=odd: (g + 1 if g % 2 == odd else g - 1, q))
     for odd in (1, 0):
         moves.append(lambda g, q, odd=odd: (g, q + 1 if q % 2 == odd else q - 1))
@@ -377,7 +376,7 @@
 def smooth(dev, relaxed_ref, own_ref, halo_refs):
     group, spot, starts = window_rows(dev)
     odd_group, odd_spot = (group & 1) == 1, (spot & 1) == 1
-    corner1, corner0, above1, above0, beside1, beside0 = [ref[...] for ref in halo_refs]
+    corner1, above1, corner0, above0, beside1, beside0 = [ref[...] for ref in halo_refs]
     extra = iota((8, 256), 0) >= 6
     up_own = jnp.where(extra, jnp.where(odd_spot, beside1, beside0), own_ref[...])
     down_own = jnp.where(extra, jnp.where(odd_spot, beside0, beside1), pltpu.roll(own_ref[...], 6, 0))

time: 111 us -> 112 us (level)
  starting transfers between devices: 38.2 us -> 40.6 us
    ppermute x6, starting transfers between devices: 6.61 us -> 8.97 us  [exchange_edges(): lax.ppermute(edge, ALL, partners(move))]
where the time goes in v7:
time: 112 us
  starting transfers between devices  40.6 us (36%)
  waiting for transfers between devices  36.9 us (33%)
  Pallas kernels  18 us (16%)
  blocking collectives  14.8 us (13%)
  local copies, waits for them, and re-layouts  1.49 us (1%)
    all_to_all x1, waiting for transfers between devices, shards(): lax.all_to_all(amplitude_pieces(frame_pos, amplitudes), ALL, 0, 0, tiled=...  22.1 us
    all_to_all x1, blocking collectives, shards(): lax.all_to_all(tiles, ALL, 0, 0, axis_index_groups=GROUPS, tiled=True)  14.8 us
    ppermute x7, starting transfers between devices, across_chips(): lax.ppermute(block, ALL, [(d, d ^ 8 * (t // 4) + t % 4) for d in range(12...  12.7 us
    all_to_all x1, starting transfers between devices, shards(): lax.all_to_all(amplitude_pieces(frame_pos, amplitudes), ALL, 0, 0, tiled=...  11.6 us
    ppermute x6, starting transfers between devices, exchange_edges(): lax.ppermute(edge, ALL, partners(move))  8.97 us
    all_to_all x1, starting transfers between devices, shards(): sums = lax.all_to_all(sums, ALL, 0, 0, tiled=True)  6 us
    ppermute x1, waiting for transfers between devices, shards(): lax.ppermute(tiles[:, 136:], ALL, [(16 * g + k, (16 * g + to) % 128) for...  5.19 us
    pallas_call x1, Pallas kernels, amplitude_pieces(): pl.pallas_call(pieces_kernel, in_specs=[BLOCK, ANYWHERE], out_specs=ANYWH...  3.83 us
  transfers between devices with their start and end apart: 18, of which 9 were waited for; matrix products, arithmetic and copies ran while one was open for 1% of the time, Pallas kernels for 6%

profile of v7, /device:TPU:0, one launch (start us, length us, event | category | flops | bytes accessed | tf_op | source)
XLA Modules:
  0.0 112.0 jit_solution(4340084614941795505)
XLA Ops:
  0.0 3.8 %amplitude_pieces.1 = bf16[128,72,128]{2,1,0:T(8,128)(2,1)} custom-call(s32[2,16]{1,0:T(2,128)} %bitcast.2, bf16[16,256,256]{2,1,0:T(8,128)(2,1)} %amp_ref.1), custom_call_target="tpu_custom_call" | custom-call | tf_op jit(solution)/shard_map/amplitude_pieces/pallas_call | solution.py:116
  3.9 11.6 %all-to-all-start = ((bf16[128,72,128]{2,1,0:T(8,128)(2,1)}), bf16[128,72,128]{2,1,0:T(8,128)(2,1)}, u32[]{:S(2)}, u32[]{:S(2)}) async-start(bf16[128,72,128]{2,1,0:T(8,128)(2,1)} %amplitude_pieces.1), calls=%async_computation | async-start | bytes 4718592 | tf_op jit(solution)/shard_map/all_to_all | solution.py:616
  15.8 2.5 %collective-permute-start = (bf16[2,2,2,32,128]{4,3,2,1,0:T(8,128)(2,1)S(1)}, bf16[2,2,2,32,128]{4,3,2,1,0:T(8,128)(2,1)S(1)}, u32[]{:S(2)}, u32[]{:S(2)}) collective-permute-start(bf16[2,2,2,32,128]{4,3,2,1,0:T(8,128)(2,1)S(1)} %get-tuple-element.35), channel_id=1, source_target_pairs={{0,2},{1,3},{2,0},{3,1},{4,6},{5,7},{6,4},{7,5},{8,10},{9,11},{10,... | collective-permute-start | bytes 196616 | tf_op jit(solution)/shard_map/ppermute | solution.py:223
  18.3 1.2 %collective-permute-start.1 = (bf16[2,2,2,32,128]{4,3,2,1,0:T(8,128)(2,1)S(1)}, bf16[2,2,2,32,128]{4,3,2,1,0:T(8,128)(2,1)S(1)}, u32[]{:S(2)}, u32[]{:S(2)}) collective-permute-start(bf16[2,2,2,32,128]{4,3,2,1,0:T(8,128)(2,1)S(1)} %get-tuple-element.36), channel_id=1, source_target_pairs={{0,3},{1,2},{2,1},{3,0},{4,7},{5,6},{6,5},{7,4},{8,11},{9,10},{10,... | collective-permute-start | bytes 196616 | tf_op jit(solution)/shard_map/ppermute | solution.py:223
  19.8 4.1 %collective-permute-start.3 = (bf16[2,2,2,32,128]{4,3,2,1,0:T(8,128)(2,1)S(1)}, bf16[2,2,2,32,128]{4,3,2,1,0:T(8,128)(2,1)S(1)}, u32[]{:S(2)}, u32[]{:S(2)}) collective-permute-start(bf16[2,2,2,32,128]{4,3,2,1,0:T(8,128)(2,1)S(1)} %get-tuple-element.39), channel_id=1, source_target_pairs={{0,10},{1,11},{2,8},{3,9},{4,14},{5,15},{6,12},{7,13},{8,2},{9,3},... | collective-permute-start | bytes 196616 | tf_op jit(solution)/shard_map/ppermute | solution.py:223
  23.9 2.1 %collective-permute-start.4 = (bf16[2,2,2,32,128]{4,3,2,1,0:T(8,128)(2,1)S(1)}, bf16[2,2,2,32,128]{4,3,2,1,0:T(8,128)(2,1)S(1)}, u32[]{:S(2)}, u32[]{:S(2)}) collective-permute-start(bf16[2,2,2,32,128]{4,3,2,1,0:T(8,128)(2,1)S(1)} %get-tuple-element.40), channel_id=1, source_target_pairs={{0,11},{1,10},{2,9},{3,8},{4,15},{5,14},{6,13},{7,12},{8,3},{9,2},... | collective-permute-start | bytes 196616 | tf_op jit(solution)/shard_map/ppermute | solution.py:223
  26.0 22.1 %all-to-all-done.in_ref = bf16[128,72,128]{2,1,0:T(8,128)(2,1)} async-done(((bf16[128,72,128]{2,1,0:T(8,128)(2,1)}), bf16[128,72,128]{2,1,0:T(8,128)(2,1)}, u32[]{:S(2)}, u32[]{:S(2)}) %all-to-all-start) | async-done | bytes 2359328 | tf_op jit(solution)/shard_map/all_to_all | solution.py:616
  48.1 3.6 %window_sums.1 = (bf16[128,8,128]{2,1,0:T(8,128)(2,1)}, f32[16,128]{1,0:T(8,128)}) custom-call(s32[1]{0:T(128)} %bitcast.dev_ref, bf16[128,72,128]{2,1,0:T(8,128)(2,1)} %all-to-all-done.in_ref), custom_call_target="tpu_custom_call" | custom-call | tf_op jit(solution)/shard_map/window_sums/pallas_call | solution.py:175
  51.8 6.0 %all-to-all-start.1 = ((bf16[128,8,128]{2,1,0:T(8,128)(2,1)}), bf16[128,8,128]{2,1,0:T(8,128)(2,1)S(1)}, u32[]{:S(2)}, u32[]{:S(2)}) async-start(bf16[128,8,128]{2,1,0:T(8,128)(2,1)} %get-tuple-element.50), calls=%async_computation.1 | async-start | bytes 524288 | tf_op jit(solution)/shard_map/all_to_all | solution.py:621
  58.8 1.5 %collective-permute-start.6 = (bf16[2,2,2,32,128]{4,3,2,1,0:T(8,128)(2,1)S(1)}, bf16[2,2,2,32,128]{4,3,2,1,0:T(8,128)(2,1)S(1)}, u32[]{:S(2)}, u32[]{:S(2)}) collective-permute-start(bf16[2,2,2,32,128]{4,3,2,1,0:T(8,128)(2,1)S(1)} %get-tuple-element.46), channel_id=1, source_target_pairs={{0,8},{1,9},{2,10},{3,11},{4,12},{5,13},{6,14},{7,15},{8,0},{9,1},... | collective-permute-start | bytes 196616 | tf_op jit(solution)/shard_map/ppermute | solution.py:223
  61.1 2.2 %collective-permute-done.5.refs_1_ = bf16[2,2,2,32,128]{4,3,2,1,0:T(8,128)(2,1)S(1)} collective-permute-done((bf16[2,2,2,32,128]{4,3,2,1,0:T(8,128)(2,1)S(1)}, bf16[2,2,2,32,128]{4,3,2,1,0:T(8,128)(2,1)S(1)}, u32[]{:S(2)}, u32[]{:S(2)}) %collective-permute-start.5) | collective-permute-done | bytes 65568 | tf_op jit(solution)/shard_map/ppermute | solution.py:223
  65.7 3.0 %all-to-all-done.1.refs_10_ = bf16[128,8,128]{2,1,0:T(8,128)(2,1)S(1)} async-done(((bf16[128,8,128]{2,1,0:T(8,128)(2,1)}), bf16[128,8,128]{2,1,0:T(8,128)(2,1)S(1)}, u32[]{:S(2)}, u32[]{:S(2)}) %all-to-all-start.1) | async-done | bytes 262176 | tf_op jit(solution)/shard_map/all_to_all | solution.py:621
  68.7 2.2 %first_sweep.1 = (f32[2,256,256]{2,1,0:T(8,128)S(1)}, f32[2,2,256,256]{3,2,1,0:T(8,128)S(1)}, f32[8,256]{1,0:T(8,128)S(1)}, f32[8,256]{1,0:T(8,128)S(1)}, f32[8,...) custom-call(s32[1]{0:T(128)} %bitcast.dev_ref, ...), custom_call_target="tpu_custom_call" | custom-call | tf_op jit(solution)/shard_map/first_sweep/pallas_call | solution.py:622
  70.9 2.2 %collective-permute-start.9 = (f32[8,256]{1,0:T(8,128)S(1)}, f32[8,256]{1,0:T(8,128)S(1)}, u32[]{:S(2)}, u32[]{:S(2)}) collective-permute-start(f32[8,256]{1,0:T(8,128)S(1)} %get-tuple-element.54), channel_id=1, source_target_pairs={{0,124},{1,122},{2,126},{3,115},{4,125},{5,121},{6,127},{7,123},{8... | collective-permute-start | bytes 24584 | tf_op jit(solution)/shard_map/ppermute | solution.py:334
  73.1 3.3 %collective-permute-start.10 = (f32[8,256]{1,0:T(8,128)S(1)}, f32[8,256]{1,0:T(8,128)S(1)}, u32[]{:S(2)}, u32[]{:S(2)}) collective-permute-start(f32[8,256]{1,0:T(8,128)S(1)} %get-tuple-element.55), channel_id=1, source_target_pairs={{0,120},{1,121},{2,122},{3,123},{4,124},{5,125},{6,126},{7,127},{8... | collective-permute-start | bytes 24584 | tf_op jit(solution)/shard_map/ppermute | solution.py:334
  76.4 2.6 %collective-permute-start.12 = (f32[8,256]{1,0:T(8,128)S(1)}, f32[8,256]{1,0:T(8,128)S(1)}, u32[]{:S(2)}, u32[]{:S(2)}) collective-permute-start(f32[8,256]{1,0:T(8,128)S(1)} %get-tuple-element.57), channel_id=1, source_target_pairs={{0,24},{1,25},{2,26},{3,27},{4,28},{5,29},{6,30},{7,31},{8,16},{9,... | collective-permute-start | bytes 24584 | tf_op jit(solution)/shard_map/ppermute | solution.py:334
  80.0 1.5 %collective-permute-done.11.in2 = f32[8,256]{1,0:T(8,128)S(1)} collective-permute-done((f32[8,256]{1,0:T(8,128)S(1)}, f32[8,256]{1,0:T(8,128)S(1)}, u32[]{:S(2)}, u32[]{:S(2)}) %collective-permute-start.11) | collective-permute-done | bytes 8224 | tf_op jit(solution)/shard_map/ppermute | solution.py:334
  81.5 1.1 collective-permute-done.13.in4
  82.6 3.5 %second_sweep.1 = bf16[16,144,128]{2,1,0:T(8,128)(2,1)S(1)} custom-call(s32[1]{0:T(128)} %bitcast.dev_ref, f32[2,2,256,256]{3,2,1,0:T(8,128)S(1)} %get-tuple-element.52.in_ref, f32[8,256]{1,0:T(8,128)S(1)} %get-tuple-element.53.own_in, f32[8,256]{1,0:T(8,128)S(1)} %collective-permute-done.9.in0, f32[8,256]{1,0:T(8,128)S(1)} %collective-permute-done.10.in1, ...), custom_call_target="tpu_custom_call" | custom-call | tf_op jit(solution)/shard_map/second_sweep/pallas_call | solution.py:631
  86.2 14.8 %all_to_all.15.in_ref = bf16[16,144,128]{2,1,0:T(8,128)(2,1)S(1)} all-to-all(bf16[16,144,128]{2,1,0:T(8,128)(2,1)S(1)} %second_sweep.1), channel_id=1, replica_groups={{0,1,2,3,4,5,6,7,8,9,10,11,12,13,14,15},{16,17,18,19,20,21,22,23,24,25,..., dimensions={0} | all-to-all | bytes 1179648 | tf_op jit(solution)/shard_map/all_to_all | solution.py:640
  101.0 1.3 %collective-permute-start.15 = (bf16[16,8,128]{2,1,0:T(8,128)(2,1)S(1)}, bf16[16,8,128]{2,1,0:T(8,128)(2,1)S(1)}, u32[]{:S(2)}, u32[]{:S(2)}) collective-permute-start(bf16[16,8,128]{2,1,0:T(8,128)(2,1)S(1)} %slice.38), channel_id=1, source_target_pairs={{8,16},{9,17},{7,127},{6,126},{24,32},{25,33},{23,15},{22,14},{40,... | collective-permute-start | bytes 98312 | tf_op jit(solution)/shard_map/ppermute | solution.py:642
  102.3 2.6 %last_smoothing.1.inner_ref = f32[2,32,32,128]{3,2,1,0:T(8,128)S(1)} custom-call(s32[1]{0:T(128)} %bitcast.dev_ref, bf16[16,144,128]{2,1,0:T(8,128)(2,1)S(1)} %all_to_all.15.in_ref), custom_call_target="tpu_custom_call" | custom-call | tf_op jit(solution)/shard_map/last_smoothing/pallas_call | solution.py:646
  104.9 5.2 %collective-permute-done.15.beyond_ref = bf16[16,8,128]{2,1,0:T(8,128)(2,1)S(1)} collective-permute-done((bf16[16,8,128]{2,1,0:T(8,128)(2,1)S(1)}, bf16[16,8,128]{2,1,0:T(8,128)(2,1)S(1)}, u32[]{:S(2)}, u32[]{:S(2)}) %collective-permute-start.15) | collective-permute-done | bytes 32800 | tf_op jit(solution)/shard_map/ppermute | solution.py:642
  110.1 1.9 %last_borders.1 = f32[2,32,32,128]{3,2,1,0:T(8,128)} custom-call(s32[1]{0:T(128)} %bitcast.dev_ref, bf16[16,144,128]{2,1,0:T(8,128)(2,1)S(1)} %all_to_all.15.in_ref, bf16[16,8,128]{2,1,0:T(8,128)(2,1)S(1)} %collective-permute-done.15.beyond_ref, f32[2,32,32,128]{3,2,1,0:T(8,128)S(1)} %last_smoothing.1.inner_ref), custom_call_target="tpu_custom_call" | custom-call | tf_op jit(solution)/shard_map/last_borders/pallas_call | solution.py:654
  (40 shorter events, 5.9 us)
Async XLA Ops:
  3.8 11.7 %copy-start.3 = (f32[2,32,32,128]{3,2,1,0:T(8,128)S(1)}, f32[2,32,32,128]{3,2,1,0:T(8,128)}, u32[]{:S(2)}) copy-start(f32[2,32,32,128]{3,2,1,0:T(8,128)} %in_ref.1) | copy-start | bytes 3145732
  3.9 44.2 %all-to-all-start = ((bf16[128,72,128]{2,1,0:T(8,128)(2,1)}), bf16[128,72,128]{2,1,0:T(8,128)(2,1)}, u32[]{:S(2)}, u32[]{:S(2)}) async-start(bf16[128,72,128]{2,1,0:T(8,128)(2,1)} %amplitude_pieces.1), calls=%async_computation | async-start | bytes 4718592 | tf_op jit(solution)/shard_map/all_to_all | solution.py:616
  15.5 53.2 %copy-start = (f32[2,256,256]{2,1,0:T(8,128)S(1)}, f32[2,256,256]{2,1,0:T(8,128)}, u32[]{:S(2)}) copy-start(f32[2,256,256]{2,1,0:T(8,128)} %probe_ref.1) | copy-start | bytes 1572868
  15.5 53.2 %copy-start.1 = (bf16[512,512]{1,0:T(8,128)(2,1)S(1)}, bf16[512,512]{1,0:T(8,128)(2,1)}, u32[]{:S(2)}) copy-start(bf16[512,512]{1,0:T(8,128)(2,1)} %constant.21.refs_14_.inverse_ref) | copy-start | bytes 1572868
  15.5 53.2 %copy-start.2 = (bf16[512,512]{1,0:T(8,128)(2,1)S(1)}, bf16[512,512]{1,0:T(8,128)(2,1)}, u32[]{:S(2)}) copy-start(bf16[512,512]{1,0:T(8,128)(2,1)} %constant.20.refs_13_.forward_ref) | copy-start | bytes 1572868
  15.8 35.9 %collective-permute-start = (bf16[2,2,2,32,128]{4,3,2,1,0:T(8,128)(2,1)S(1)}, bf16[2,2,2,32,128]{4,3,2,1,0:T(8,128)(2,1)S(1)}, u32[]{:S(2)}, u32[]{:S(2)}) collective-permute-start(bf16[2,2,2,32,128]{4,3,2,1,0:T(8,128)(2,1)S(1)} %get-tuple-element.35), channel_id=1, source_target_pairs={{0,2},{1,3},{2,0},{3,1},{4,6},{5,7},{6,4},{7,5},{8,10},{9,11},{10,... | collective-permute-start | bytes 196616 | tf_op jit(solution)/shard_map/ppermute | solution.py:223
  18.3 33.4 %collective-permute-start.1 = (bf16[2,2,2,32,128]{4,3,2,1,0:T(8,128)(2,1)S(1)}, bf16[2,2,2,32,128]{4,3,2,1,0:T(8,128)(2,1)S(1)}, u32[]{:S(2)}, u32[]{:S(2)}) collective-permute-start(bf16[2,2,2,32,128]{4,3,2,1,0:T(8,128)(2,1)S(1)} %get-tuple-element.36), channel_id=1, source_target_pairs={{0,3},{1,2},{2,1},{3,0},{4,7},{5,6},{6,5},{7,4},{8,11},{9,10},{10,... | collective-permute-start | bytes 196616 | tf_op jit(solution)/shard_map/ppermute | solution.py:223
  19.5 32.3 %collective-permute-start.2 = (bf16[2,2,2,32,128]{4,3,2,1,0:T(8,128)(2,1)S(1)}, bf16[2,2,2,32,128]{4,3,2,1,0:T(8,128)(2,1)S(1)}, u32[]{:S(2)}, u32[]{:S(2)}) collective-permute-start(bf16[2,2,2,32,128]{4,3,2,1,0:T(8,128)(2,1)S(1)} %get-tuple-element.38), channel_id=1, source_target_pairs={{0,9},{1,8},{2,11},{3,10},{4,13},{5,12},{6,15},{7,14},{8,1},{9,0},... | collective-permute-start | bytes 196616 | tf_op jit(solution)/shard_map/ppermute | solution.py:223
  19.8 32.0 %collective-permute-start.3 = (bf16[2,2,2,32,128]{4,3,2,1,0:T(8,128)(2,1)S(1)}, bf16[2,2,2,32,128]{4,3,2,1,0:T(8,128)(2,1)S(1)}, u32[]{:S(2)}, u32[]{:S(2)}) collective-permute-start(bf16[2,2,2,32,128]{4,3,2,1,0:T(8,128)(2,1)S(1)} %get-tuple-element.39), channel_id=1, source_target_pairs={{0,10},{1,11},{2,8},{3,9},{4,14},{5,15},{6,12},{7,13},{8,2},{9,3},... | collective-permute-start | bytes 196616 | tf_op jit(solution)/shard_map/ppermute | solution.py:223
  23.9 27.8 %collective-permute-start.4 = (bf16[2,2,2,32,128]{4,3,2,1,0:T(8,128)(2,1)S(1)}, bf16[2,2,2,32,128]{4,3,2,1,0:T(8,128)(2,1)S(1)}, u32[]{:S(2)}, u32[]{:S(2)}) collective-permute-start(bf16[2,2,2,32,128]{4,3,2,1,0:T(8,128)(2,1)S(1)} %get-tuple-element.40), channel_id=1, source_target_pairs={{0,11},{1,10},{2,9},{3,8},{4,15},{5,14},{6,13},{7,12},{8,3},{9,2},... | collective-permute-start | bytes 196616 | tf_op jit(solution)/shard_map/ppermute | solution.py:223
  51.8 16.9 %all-to-all-start.1 = ((bf16[128,8,128]{2,1,0:T(8,128)(2,1)}), bf16[128,8,128]{2,1,0:T(8,128)(2,1)S(1)}, u32[]{:S(2)}, u32[]{:S(2)}) async-start(bf16[128,8,128]{2,1,0:T(8,128)(2,1)} %get-tuple-element.50), calls=%async_computation.1 | async-start | bytes 524288 | tf_op jit(solution)/shard_map/all_to_all | solution.py:621
  57.8 5.5 %collective-permute-start.5 = (bf16[2,2,2,32,128]{4,3,2,1,0:T(8,128)(2,1)S(1)}, bf16[2,2,2,32,128]{4,3,2,1,0:T(8,128)(2,1)S(1)}, u32[]{:S(2)}, u32[]{:S(2)}) collective-permute-start(bf16[2,2,2,32,128]{4,3,2,1,0:T(8,128)(2,1)S(1)} %get-tuple-element.43), channel_id=1, source_target_pairs={{0,1},{1,0},{2,3},{3,2},{4,5},{5,4},{6,7},{7,6},{8,9},{9,8},{10,11... | collective-permute-start | bytes 196616 | tf_op jit(solution)/shard_map/ppermute | solution.py:223
  58.8 5.5 %collective-permute-start.6 = (bf16[2,2,2,32,128]{4,3,2,1,0:T(8,128)(2,1)S(1)}, bf16[2,2,2,32,128]{4,3,2,1,0:T(8,128)(2,1)S(1)}, u32[]{:S(2)}, u32[]{:S(2)}) collective-permute-start(bf16[2,2,2,32,128]{4,3,2,1,0:T(8,128)(2,1)S(1)} %get-tuple-element.46), channel_id=1, source_target_pairs={{0,8},{1,9},{2,10},{3,11},{4,12},{5,13},{6,14},{7,15},{8,0},{9,1},... | collective-permute-start | bytes 196616 | tf_op jit(solution)/shard_map/ppermute | solution.py:223
  61.1 4.6 %collective-permute-start.7 = (bf16[6,2,2,32,128]{4,3,2,1,0:T(8,128)(2,1)S(1)}, bf16[6,2,2,32,128]{4,3,2,1,0:T(8,128)(2,1)S(1)}, u32[]{:S(2)}, u32[]{:S(2)}) collective-permute-start(bf16[6,2,2,32,128]{4,3,2,1,0:T(8,128)(2,1)S(1)} %slice_dynamic-update-slice_fusion), channel_id=1, source_target_pairs={{0,4},{1,5},{2,6},{3,7},{4,0},{5,1},{6,2},{7,3},{8,12},{9,13},{10,... | collective-permute-start | bytes 589832 | tf_op jit(solution)/shard_map/ppermute | solution.py:230
  64.4 1.3 %collective-permute-start.8 = (bf16[2,2,2,32,128]{4,3,2,1,0:T(8,128)(2,1)S(1)}, bf16[2,2,2,32,128]{4,3,2,1,0:T(8,128)(2,1)S(1)}, u32[]{:S(2)}, u32[]{:S(2)}) collective-permute-start(bf16[2,2,2,32,128]{4,3,2,1,0:T(8,128)(2,1)S(1)} %pad_maximum_fusion), channel_id=1, source_target_pairs={{0,4},{1,5},{2,6},{3,7},{4,0},{5,1},{6,2},{7,3},{8,12},{9,13},{10,... | collective-permute-start | bytes 196616 | tf_op jit(solution)/shard_map/ppermute | solution.py:230
  70.9 9.0 %collective-permute-start.9 = (f32[8,256]{1,0:T(8,128)S(1)}, f32[8,256]{1,0:T(8,128)S(1)}, u32[]{:S(2)}, u32[]{:S(2)}) collective-permute-start(f32[8,256]{1,0:T(8,128)S(1)} %get-tuple-element.54), channel_id=1, source_target_pairs={{0,124},{1,122},{2,126},{3,115},{4,125},{5,121},{6,127},{7,123},{8... | collective-permute-start | bytes 24584 | tf_op jit(solution)/shard_map/ppermute | solution.py:334
  73.1 7.0 %collective-permute-start.10 = (f32[8,256]{1,0:T(8,128)S(1)}, f32[8,256]{1,0:T(8,128)S(1)}, u32[]{:S(2)}, u32[]{:S(2)}) collective-permute-start(f32[8,256]{1,0:T(8,128)S(1)} %get-tuple-element.55), channel_id=1, source_target_pairs={{0,120},{1,121},{2,122},{3,123},{4,124},{5,125},{6,126},{7,127},{8... | collective-permute-start | bytes 24584 | tf_op jit(solution)/shard_map/ppermute | solution.py:334
  76.4 5.2 %collective-permute-start.11 = (f32[8,256]{1,0:T(8,128)S(1)}, f32[8,256]{1,0:T(8,128)S(1)}, u32[]{:S(2)}, u32[]{:S(2)}) collective-permute-start(f32[8,256]{1,0:T(8,128)S(1)} %get-tuple-element.56), channel_id=1, source_target_pairs={{0,16},{1,29},{2,25},{3,31},{4,24},{5,28},{6,26},{7,30},{8,20},{9,... | collective-permute-start | bytes 24584 | tf_op jit(solution)/shard_map/ppermute | solution.py:334
  76.4 5.2 %collective-permute-start.12 = (f32[8,256]{1,0:T(8,128)S(1)}, f32[8,256]{1,0:T(8,128)S(1)}, u32[]{:S(2)}, u32[]{:S(2)}) collective-permute-start(f32[8,256]{1,0:T(8,128)S(1)} %get-tuple-element.57), channel_id=1, source_target_pairs={{0,24},{1,25},{2,26},{3,27},{4,28},{5,29},{6,30},{7,31},{8,16},{9,... | collective-permute-start | bytes 24584 | tf_op jit(solution)/shard_map/ppermute | solution.py:334
  79.0 3.7 %collective-permute-start.13 = (f32[8,256]{1,0:T(8,128)S(1)}, f32[8,256]{1,0:T(8,128)S(1)}, u32[]{:S(2)}, u32[]{:S(2)}) collective-permute-start(f32[8,256]{1,0:T(8,128)S(1)} %get-tuple-element.58), channel_id=1, source_target_pairs={{0,8},{1,2},{2,1},{3,11},{4,5},{5,4},{6,7},{7,6},{8,0},{9,10},{10,... | collective-permute-start | bytes 24584 | tf_op jit(solution)/shard_map/ppermute | solution.py:334
  79.9 2.8 %collective-permute-start.14 = (f32[8,256]{1,0:T(8,128)S(1)}, f32[8,256]{1,0:T(8,128)S(1)}, u32[]{:S(2)}, u32[]{:S(2)}) collective-permute-start(f32[8,256]{1,0:T(8,128)S(1)} %get-tuple-element.59), channel_id=1, source_target_pairs={{0,4},{1,5},{2,6},{3,7},{4,0},{5,1},{6,2},{7,3},{8,12},{9,13},{10,... | collective-permute-start | bytes 24584 | tf_op jit(solution)/shard_map/ppermute | solution.py:334
  101.0 9.1 %collective-permute-start.15 = (bf16[16,8,128]{2,1,0:T(8,128)(2,1)S(1)}, bf16[16,8,128]{2,1,0:T(8,128)(2,1)S(1)}, u32[]{:S(2)}, u32[]{:S(2)}) collective-permute-start(bf16[16,8,128]{2,1,0:T(8,128)(2,1)S(1)} %slice.38), channel_id=1, source_target_pairs={{8,16},{9,17},{7,127},{6,126},{24,32},{25,33},{23,15},{22,14},{40,... | collective-permute-start | bytes 98312 | tf_op jit(solution)/shard_map/ppermute | solution.py:642
